TPU v7x, 32 devices: a whole 2x2x4 slice. The times are simulated.
32 devices in a mesh: dev: 32 (over z, y, x, core).
Axes of the slice: x: 2, y: 2, z: 4, core: 2. Of those that a mesh axis runs over, the one named last changes fastest.
Arguments:
- items: bfloat16 [16384, 1024], P('dev'), may hold values from -6 to 6
- cand_user: int32 [16384, 1], P('dev'), may hold values from 0 to 31; in each aligned block of 512 rows (0 to 511, 512 to 1023, ...) at most 32 rows name the same one
- owner_map: int32 [32], replicated, may hold values from 0 to 31, each once
- hist_blocks: int32 [32], P('dev'), may hold values from 1 to 8
- cache_keys: bfloat16 [32, 1024, 1024], P('dev'), may hold values from -6 to 6
- cache_values: bfloat16 [32, 1024, 1024], P('dev'), may hold values from -6 to 6
- w_in: bfloat16 [1024, 2048], replicated, may hold values from -0.1875 to 0.1875
- w_out: bfloat16 [1024, 1024], replicated, may hold values from -0.1875 to 0.1875
Outputs:
- ranked: bfloat16 [16384, 1024], P('dev')
Inputs may be any that keep to these rules, and one draw needn't show every extreme that they name: `cand_user`: the candidates of one device name no user more than 32 times. `owner_map`: each cache slot belongs to exactly one user.
All inputs are finite; a program needn't handle non-finite values.
Results may differ from a plain program's by a relative error of at most 0.0057.
Values may be sent and summed in bfloat16 or wider, within the bound.
No kernel may reach another device: no remote copies, remote signals or barrier semaphores. Data moves between devices by JAX's collectives and lax.ppermute only.
A program may use at most 128 MiB of HBM per device.

v0:
```python
import jax
import jax.numpy as jnp
from jax import lax
from jax.sharding import PartitionSpec as P

HEADS = 8
BLOCK = 128


def layer_norm(values):
    center = values - jnp.mean(values, axis=-1, keepdims=True)
    spread = jnp.mean(center * center, axis=-1, keepdims=True)
    return center * lax.rsqrt(spread + 1e-06)


def attend(queries, keys, values, blocks):
    width = queries.shape[-1]
    head_dim = width // HEADS
    flat = queries.reshape(-1, HEADS, head_dim)
    inverse = 1.0 / (BLOCK * blocks).astype(jnp.float32)
    scale = head_dim ** (-0.5)

    def block_term(index, total, factor):
        offset = index * BLOCK
        key_block = lax.dynamic_slice_in_dim(keys, offset, BLOCK, 0).reshape(BLOCK, HEADS, head_dim)
        value_block = lax.dynamic_slice_in_dim(values, offset, BLOCK, 0).reshape(
            BLOCK, HEADS, head_dim
        )
        scores = (
            jnp.einsum("rhd,thd->rht", flat, key_block, preferred_element_type=jnp.float32) * scale
        )
        weights = (jax.nn.silu(scores) * factor).astype(jnp.bfloat16)
        return total + jnp.einsum(
            "rht,thd->rhd", weights, value_block, preferred_element_type=jnp.float32
        )

    start = jnp.zeros(flat.shape, jnp.float32)
    total = lax.fori_loop(
        0,
        keys.shape[0] // BLOCK,
        lambda index, total: block_term(
            index, total, inverse * (index < blocks).astype(jnp.float32)
        ),
        start,
    )
    return total.reshape(queries.shape).astype(jnp.bfloat16)


def local(items, cand_user, owner_map, hist_blocks, cache_keys, cache_values, w_in, w_out):
    row_count, width = items.shape
    devices = lax.axis_size("dev")
    capacity = max(2, 2 * row_count // devices)
    normed = layer_norm(items.astype(jnp.float32)).astype(jnp.bfloat16)
    active = jax.nn.silu(jnp.dot(normed, w_in, preferred_element_type=jnp.float32))
    gate = active[:, :width].astype(jnp.bfloat16)
    payload = active[:, width:].astype(jnp.bfloat16)
    user_ids = jnp.arange(owner_map.shape[0], dtype=jnp.int32)
    owner = jnp.sum(jnp.where(cand_user == user_ids[None, :], owner_map[None, :], 0), axis=1)
    owner_hot = (owner[:, None] == jnp.arange(devices, dtype=jnp.int32)[None, :]).astype(jnp.int32)
    position = jnp.sum((jnp.cumsum(owner_hot, axis=0) - owner_hot) * owner_hot, axis=1)
    target = owner * capacity + position
    dispatch = (jnp.arange(devices * capacity, dtype=jnp.int32)[:, None] == target[None, :]).astype(
        jnp.bfloat16
    )
    outgoing = jnp.dot(dispatch, payload, preferred_element_type=jnp.float32).astype(jnp.bfloat16)
    outgoing = outgoing.reshape(devices, capacity, width)
    keys = cache_keys[0]
    values = cache_values[0]
    blocks = hist_blocks[0]
    attended = attend(
        lax.all_to_all(outgoing, "dev", split_axis=0, concat_axis=0, tiled=True),
        keys,
        values,
        blocks,
    )
    returned = lax.all_to_all(attended, "dev", split_axis=0, concat_axis=0, tiled=True)
    attention = lax.dot_general(
        dispatch,
        returned.reshape(-1, width),
        (((0,), (0,)), ((), ())),
        preferred_element_type=jnp.float32,
    )
    mixed_rows = (layer_norm(attention) * gate).astype(jnp.bfloat16)
    output = items.astype(jnp.float32) + jnp.dot(
        mixed_rows, w_out, preferred_element_type=jnp.float32
    )
    return output.astype(jnp.bfloat16)


def solution(mesh):
    return jax.shard_map(
        local,
        mesh=mesh,
        in_specs=(
            P("dev", None),
            P("dev", None),
            P(),
            P("dev"),
            P("dev", None, None),
            P("dev", None, None),
            P(),
            P(),
        ),
        out_specs=P("dev", None),
        check_vma=False,
    )
```

profile of v0, /device:TPU:0, one launch (start us, length us, event | category | flops | bytes accessed | tf_op | source)
XLA Modules:
  0.0 210.3 jit_solution(12880841487446154986)
XLA Ops:
  0.0 0.0 copy-start
  0.0 0.0 copy-start.1
  0.0 1.6 convert_reduce_fusion
  1.6 1.6 fusion.9
  3.3 0.0 copy-done.4
  3.3 0.0 copy-done.3
  3.3 0.1 select_reduce_fusion
  3.4 1.2 reduce-window.6
  4.5 0.2 slice_reduce_fusion
  4.8 0.1 fusion.29
  4.9 0.0 copy-done.1
  4.9 5.1 %multiply_convert_fusion = bf16[512,2048]{1,0:T(8,128)(2,1)S(1)} fusion(bf16[1024,2048]{1,0:T(8,128)(2,1)} %param.16, bf16[512,1024]{1,0:T(8,128)(2,1)S(1)} %copy-done.1, f32[512]{0:T(512)S(1)} %add_rsqrt_fusion.1, f32[512]{0:T(512)S(1)} %broadcast_multiply_fusion.1), kind=kOutput, calls=%fused_computation.12 | convolution fusion | flops 2154823680 | bytes 7344128 | tf_op jit(solution)/shard_map/dot_general | solution.py:54
  10.0 0.0 copy-start.5
  10.0 2.6 %fusion.14 = bf16[1024,1024]{1,0:T(8,128)(2,1)} fusion(bf16[512,2048]{1,0:T(8,128)(2,1)S(1)} %multiply_convert_fusion, s32[512]{0:T(512)S(1)} %multiply_add_fusion), kind=kOutput, calls=%fused_computation.26 | convolution fusion | flops 1075314688 | bytes 3147776 | tf_op jit(solution)/shard_map/dot_general | solution.py:65
  12.6 0.0 copy-done.5
  12.6 7.4 %all-to-all-start = ((bf16[32,32,1024]{2,1,0:T(8,128)(2,1)}), bf16[32,32,1024]{2,1,0:T(8,128)(2,1)}, u32[]{:S(2)}, u32[]{:S(2)}) async-start(bf16[32,32,1024]{2,1,0:T(8,128)(2,1)} %bitcast.76), calls=%async_computation | async-start | bytes 4194304 | tf_op jit(solution)/shard_map/all_to_all | solution.py:71
  20.7 3.9 %copy.15 = bf16[1,1024,1024]{1,2,0:T(8,128)(2,1)} copy(bf16[1,1024,1024]{2,1,0:T(8,128)(2,1)} %param.14) | data formatting | bytes 4194304 | tf_op args[4]
  24.7 4.0 %copy.14 = bf16[1,1024,1024]{1,2,0:T(8,128)(2,1)} copy(bf16[1,1024,1024]{2,1,0:T(8,128)(2,1)} %param.15) | data formatting | bytes 4194304 | tf_op args[5]
  28.7 40.3 %all-to-all-done = bf16[32,32,1024]{2,1,0:T(8,128)(2,1)} async-done(((bf16[32,32,1024]{2,1,0:T(8,128)(2,1)}), bf16[32,32,1024]{2,1,0:T(8,128)(2,1)}, u32[]{:S(2)}, u32[]{:S(2)}) %all-to-all-start) | async-done | bytes 2097184 | tf_op jit(solution)/shard_map/all_to_all | solution.py:71
  69.0 2.2 %copy.21 = bf16[128,8,8,128]{3,2,1,0:T(8,128)(2,1)S(1)} copy(bf16[128,8,8,128]{3,1,2,0:T(8,128)(2,1)} %bitcast.15) | data formatting | bytes 4194304
  71.2 1.6 copy.16
  72.8 67.6 %while.14 = (s32[]{:T(128)}, f32[1024,8,128]{0,2,1:T(8,128)}, bf16[1024,1024]{0,1:T(8,128)(2,1)}, bf16[1024,1024]{0,1:T(8,128)(2,1)}, bf16[1024,8,128]{2,0,1:T(8...) while((s32[]{:T(128)}, f32[1024,8,128]{0,2,1:T(8,128)}, ...), condition=%wide.region_7.8_spmd.clone, body=%wide.region_6.7_spmd.clone.sunk | while | flops 546308096 | bytes 12058835 | solution.py:38
  73.5 1.1 constant_dynamic-slice_fusion.3
  74.6 5.6 %bitcast_add_fusion.2 = f32[1024,8,128]{0,2,1:T(8,128)} fusion(f32[1024,8,128]{0,2,1:T(8,128)} %get-tuple-element.239, bf16[128,8,128]{0,2,1:T(8,128)(2,1)S(1)} %bitcast.73, pred[]{:T(512)S(6)} %compare.3, bf16[128,8,128]{0,2,1:T(8,128)(2,1)S(1)} %bitcast.72, bf16[1024,8,128]{2,0,1:T(8,128)(2,1)} %get-tuple-element.254, f32[]{:T(128)S(6)} %mul.167), kind=kOutput, calls=%fused_computation.clone.1 | convolution fusion | flops 546308096 | bytes 11010053 | tf_op jit(solution)/shard_map/while/body/eval_jaxpr/rht,thd->rhd/dot_general | solution.py:33
  80.8 1.1 constant_dynamic-slice_fusion.3
  81.9 6.9 %bitcast_add_fusion.2 = f32[1024,8,128]{0,2,1:T(8,128)} fusion(f32[1024,8,128]{0,2,1:T(8,128)} %get-tuple-element.239, bf16[128,8,128]{0,2,1:T(8,128)(2,1)S(1)} %bitcast.73, pred[]{:T(512)S(6)} %compare.3, bf16[128,8,128]{0,2,1:T(8,128)(2,1)S(1)} %bitcast.72, bf16[1024,8,128]{2,0,1:T(8,128)(2,1)} %get-tuple-element.254, f32[]{:T(128)S(6)} %mul.167), kind=kOutput, calls=%fused_computation.clone.1 | convolution fusion | flops 546308096 | bytes 11010053 | tf_op jit(solution)/shard_map/while/body/eval_jaxpr/rht,thd->rhd/dot_general | solution.py:33
  89.4 1.1 constant_dynamic-slice_fusion.3
  90.5 6.9 %bitcast_add_fusion.2 = f32[1024,8,128]{0,2,1:T(8,128)} fusion(f32[1024,8,128]{0,2,1:T(8,128)} %get-tuple-element.239, bf16[128,8,128]{0,2,1:T(8,128)(2,1)S(1)} %bitcast.73, pred[]{:T(512)S(6)} %compare.3, bf16[128,8,128]{0,2,1:T(8,128)(2,1)S(1)} %bitcast.72, bf16[1024,8,128]{2,0,1:T(8,128)(2,1)} %get-tuple-element.254, f32[]{:T(128)S(6)} %mul.167), kind=kOutput, calls=%fused_computation.clone.1 | convolution fusion | flops 546308096 | bytes 11010053 | tf_op jit(solution)/shard_map/while/body/eval_jaxpr/rht,thd->rhd/dot_general | solution.py:33
  98.0 1.1 constant_dynamic-slice_fusion.3
  99.1 6.9 %bitcast_add_fusion.2 = f32[1024,8,128]{0,2,1:T(8,128)} fusion(f32[1024,8,128]{0,2,1:T(8,128)} %get-tuple-element.239, bf16[128,8,128]{0,2,1:T(8,128)(2,1)S(1)} %bitcast.73, pred[]{:T(512)S(6)} %compare.3, bf16[128,8,128]{0,2,1:T(8,128)(2,1)S(1)} %bitcast.72, bf16[1024,8,128]{2,0,1:T(8,128)(2,1)} %get-tuple-element.254, f32[]{:T(128)S(6)} %mul.167), kind=kOutput, calls=%fused_computation.clone.1 | convolution fusion | flops 546308096 | bytes 11010053 | tf_op jit(solution)/shard_map/while/body/eval_jaxpr/rht,thd->rhd/dot_general | solution.py:33
  106.6 1.1 constant_dynamic-slice_fusion.3
  107.7 6.9 %bitcast_add_fusion.2 = f32[1024,8,128]{0,2,1:T(8,128)} fusion(f32[1024,8,128]{0,2,1:T(8,128)} %get-tuple-element.239, bf16[128,8,128]{0,2,1:T(8,128)(2,1)S(1)} %bitcast.73, pred[]{:T(512)S(6)} %compare.3, bf16[128,8,128]{0,2,1:T(8,128)(2,1)S(1)} %bitcast.72, bf16[1024,8,128]{2,0,1:T(8,128)(2,1)} %get-tuple-element.254, f32[]{:T(128)S(6)} %mul.167), kind=kOutput, calls=%fused_computation.clone.1 | convolution fusion | flops 546308096 | bytes 11010053 | tf_op jit(solution)/shard_map/while/body/eval_jaxpr/rht,thd->rhd/dot_general | solution.py:33
  115.2 1.1 constant_dynamic-slice_fusion.3
  116.3 6.9 %bitcast_add_fusion.2 = f32[1024,8,128]{0,2,1:T(8,128)} fusion(f32[1024,8,128]{0,2,1:T(8,128)} %get-tuple-element.239, bf16[128,8,128]{0,2,1:T(8,128)(2,1)S(1)} %bitcast.73, pred[]{:T(512)S(6)} %compare.3, bf16[128,8,128]{0,2,1:T(8,128)(2,1)S(1)} %bitcast.72, bf16[1024,8,128]{2,0,1:T(8,128)(2,1)} %get-tuple-element.254, f32[]{:T(128)S(6)} %mul.167), kind=kOutput, calls=%fused_computation.clone.1 | convolution fusion | flops 546308096 | bytes 11010053 | tf_op jit(solution)/shard_map/while/body/eval_jaxpr/rht,thd->rhd/dot_general | solution.py:33
  123.8 1.1 constant_dynamic-slice_fusion.3
  124.9 6.9 %bitcast_add_fusion.2 = f32[1024,8,128]{0,2,1:T(8,128)} fusion(f32[1024,8,128]{0,2,1:T(8,128)} %get-tuple-element.239, bf16[128,8,128]{0,2,1:T(8,128)(2,1)S(1)} %bitcast.73, pred[]{:T(512)S(6)} %compare.3, bf16[128,8,128]{0,2,1:T(8,128)(2,1)S(1)} %bitcast.72, bf16[1024,8,128]{2,0,1:T(8,128)(2,1)} %get-tuple-element.254, f32[]{:T(128)S(6)} %mul.167), kind=kOutput, calls=%fused_computation.clone.1 | convolution fusion | flops 546308096 | bytes 11010053 | tf_op jit(solution)/shard_map/while/body/eval_jaxpr/rht,thd->rhd/dot_general | solution.py:33
  132.4 1.1 constant_dynamic-slice_fusion.3
  133.5 6.9 %bitcast_add_fusion.2 = f32[1024,8,128]{0,2,1:T(8,128)} fusion(f32[1024,8,128]{0,2,1:T(8,128)} %get-tuple-element.239, bf16[128,8,128]{0,2,1:T(8,128)(2,1)S(1)} %bitcast.73, pred[]{:T(512)S(6)} %compare.3, bf16[128,8,128]{0,2,1:T(8,128)(2,1)S(1)} %bitcast.72, bf16[1024,8,128]{2,0,1:T(8,128)(2,1)} %get-tuple-element.254, f32[]{:T(128)S(6)} %mul.167), kind=kOutput, calls=%fused_computation.clone.1 | convolution fusion | flops 546308096 | bytes 11010053 | tf_op jit(solution)/shard_map/while/body/eval_jaxpr/rht,thd->rhd/dot_general | solution.py:33
  140.4 3.9 %convert_element_type.54 = bf16[1024,8,128]{0,2,1:T(8,128)(2,1)} convert(f32[1024,8,128]{0,2,1:T(8,128)} %get-tuple-element.129) | non-fusion elementwise | flops 1048576 | bytes 6291456 | tf_op jit(solution)/shard_map/convert_element_type | solution.py:46
  144.2 4.2 %copy.17 = bf16[1024,8,128]{2,1,0:T(8,128)(2,1)} copy(bf16[1024,8,128]{0,2,1:T(8,128)(2,1)} %convert_element_type.54) | data formatting | bytes 4194304 | tf_op jit(solution)/shard_map/convert_element_type | solution.py:46
  148.4 4.2 %convert_element_type.55 = bf16[32,32,1024]{2,1,0:T(8,128)(2,1)} reshape(bf16[1024,8,128]{2,1,0:T(8,128)(2,1)} %copy.17) | data formatting | bytes 4194304 | tf_op jit(solution)/shard_map/convert_element_type | solution.py:46
  152.6 52.7 %all_to_all.10 = bf16[32,32,1024]{2,1,0:T(8,128)(2,1)S(1)} all-to-all(bf16[32,32,1024]{2,1,0:T(8,128)(2,1)} %convert_element_type.55), channel_id=1, replica_groups=mesh['dev'=32] {'dev'}, dimensions={0} | all-to-all | bytes 4194304 | tf_op jit(solution)/shard_map/all_to_all | solution.py:76
  205.3 1.4 fusion.31
  206.7 0.3 multiply_reduce_fusion
  207.1 0.0 copy-done
  207.1 0.0 copy-done.6
  207.1 0.9 copy-done.2
  208.0 2.3 %fusion.11 = bf16[512,1024]{1,0:T(8,128)(2,1)} fusion(bf16[512,1024]{1,0:T(8,128)(2,1)S(1)} %copy-done.2, bf16[1024,1024]{1,0:T(8,128)(2,1)S(1)} %copy-done, f32[512,1024]{1,0:T(8,128)S(1)} %get-tuple-element.178, bf16[512,2048]{1,0:T(8,128)(2,1)S(1)} %copy-done.6, f32[512]{0:T(512)S(1)} %add_rsqrt_fusion, f32[512]{0:T(512)S(1)} %broadcast_multiply_fusion), kind=kOutput, calls=%fused_computation.20 | convolution fusion | flops 1077936128 | bytes 7344128 | tf_op jit(solution)/shard_map/dot_general | solution.py:84
  (13 shorter events, 0.1 us)
Async XLA Ops:
  0.0 207.1 %copy-start = (bf16[1024,1024]{1,0:T(8,128)(2,1)S(1)}, bf16[1024,1024]{1,0:T(8,128)(2,1)}, u32[]{:S(2)}) copy-start(bf16[1024,1024]{1,0:T(8,128)(2,1)} %param.17) | copy-start | bytes 6291460
  0.0 4.9 %copy-start.1 = (bf16[512,1024]{1,0:T(8,128)(2,1)S(1)}, bf16[512,1024]{1,0:T(8,128)(2,1)}, u32[]{:S(2)}) copy-start(bf16[512,1024]{1,0:T(8,128)(2,1)} %param.10) | copy-start | bytes 3145732
  0.0 3.2 %copy-start.4 = (s32[32]{0:T(128)S(1)}, s32[32]{0:T(128)}, u32[]{:S(2)}) copy-start(s32[32]{0:T(128)} %param.12) | copy-start | bytes 388
  0.0 3.3 %copy-start.3 = (s32[512,1]{0,1:T(1,128)S(1)}, s32[512,1]{0,1:T(1,128)}, u32[]{:S(2)}) copy-start(s32[512,1]{0,1:T(1,128)} %param.11) | copy-start | bytes 6148
  10.0 2.6 %copy-start.5 = (bf16[512,2048]{1,0:T(8,128)(2,1)}, bf16[512,2048]{1,0:T(8,128)(2,1)S(1)}, u32[]{:S(2)}) copy-start(bf16[512,2048]{1,0:T(8,128)(2,1)S(1)} %multiply_convert_fusion) | copy-start | bytes 6291460
  12.6 56.3 %all-to-all-start = ((bf16[32,32,1024]{2,1,0:T(8,128)(2,1)}), bf16[32,32,1024]{2,1,0:T(8,128)(2,1)}, u32[]{:S(2)}, u32[]{:S(2)}) async-start(bf16[32,32,1024]{2,1,0:T(8,128)(2,1)} %bitcast.76), calls=%async_computation | async-start | bytes 4194304 | tf_op jit(solution)/shard_map/all_to_all | solution.py:71
  205.3 1.8 copy-start.6
  206.7 1.3 copy-start.2
where the time goes:
time: 211 us; the launch traced here: 210 us
  matrix products  65.1 us (31%)
  blocking collectives  52.7 us (25%)
  waiting for transfers between devices  40.3 us (19%)
  local copies, waits for them, and re-layouts  29.8 us (14%)
  other arithmetic  8.88 us (4%)
  starting transfers between devices  7.43 us (4%)
  loops' own time  5.27 us (2%)
    dot_general x8, matrix products, block_term(): jnp.einsum('rht,thd->rhd', weights, value_block, preferred_element_type=j...  53.7 us
    all_to_all x1, blocking collectives, local(): lax.all_to_all(attended, 'dev', split_axis=0, concat_axis=0, tiled=True)  52.7 us
    all_to_all x1, waiting for transfers between devices, local(): lax.all_to_all(outgoing, 'dev', split_axis=0, concat_axis=0, tiled=True)  40.3 us
    unnamed x18, local copies, waits for them, and re-layouts  12.6 us
    dynamic_slice x8, local copies, waits for them, and re-layouts, block_term(): lax.dynamic_slice_in_dim(keys, offset, BLOCK, 0)  8.63 us
    convert_element_type x2, local copies, waits for them, and re-layouts, attend(): return total.reshape(queries.shape).astype(jnp.bfloat16)  8.34 us
    all_to_all x1, starting transfers between devices, local(): lax.all_to_all(outgoing, 'dev', split_axis=0, concat_axis=0, tiled=True)  7.43 us
    another operation x1, loops' own time, attend(): lax.fori_loop(0, keys.shape[0] // BLOCK, lambda index, total: block_term(...  5.27 us
  transfers between devices with their start and end apart: 1, of which 1 were waited for; matrix products, arithmetic and copies ran while one was open for 4% of the time, Pallas kernels for 0%

commit v1 on v0

v1 whole, which is shorter than its diff:
```python
import functools

import jax
import jax.numpy as jnp
from jax import lax
from jax.experimental import pallas as pl
from jax.experimental.pallas import tpu as pltpu
from jax.sharding import PartitionSpec as P

HEADS = 8
BLOCK = 128
F32 = jnp.float32
BF16 = jnp.bfloat16
VMEM_LIMIT = 40 * 1024 * 1024


def normalize(values):
    center = values - jnp.mean(values, axis=-1, keepdims=True)
    spread = jnp.mean(center * center, axis=-1, keepdims=True)
    return center * lax.rsqrt(spread + 1e-06)


def silu(values):
    half = 0.5 * values
    return half + half * jnp.tanh(half)


def iota(shape, dimension):
    return lax.broadcasted_iota(jnp.int32, shape, dimension)


def dot(left, right):
    return jnp.dot(left, right, preferred_element_type=F32)


def as_row(column):
    rows = column.shape[0]
    return jnp.broadcast_to(column, (rows, 128)).T[0:1, :]


def dispatch_kernel(capacity, items, cand, owner_map, w_query, out, target_out, normed_out, normed, select):
    rows = items.shape[0]
    slots = out.shape[0]
    devices = owner_map.shape[0]

    @pl.when(pl.program_id(0) == 0)
    def _():
        values = normalize(items[...].astype(F32)).astype(BF16)
        normed[...] = values
        normed_out[...] = values
        user_hot = (cand[...] == iota((rows, devices), 1)).astype(F32).astype(BF16)
        to_owner = (owner_map[...] == iota((devices, devices), 1)).astype(F32).astype(BF16)
        owner_hot = dot(user_hot, to_owner)
        before = (iota((rows, rows), 0) > iota((rows, rows), 1)).astype(F32).astype(BF16)
        rank = dot(before, owner_hot.astype(BF16))
        start = (iota((rows, devices), 1) * capacity).astype(F32)
        target = jnp.sum(owner_hot * (rank + start), axis=1, keepdims=True)
        target_out[...] = target.astype(jnp.int32)
        row = as_row(target).astype(jnp.int32)
        select[...] = (iota((slots, rows), 0) == row).astype(F32).astype(BF16)

    query = silu(dot(normed[...], w_query[...])).astype(BF16)
    out[...] = dot(select[...], query).astype(BF16)


def dispatch(items, cand_user, owner_map, w_in, capacity):
    rows, width = items.shape
    devices = owner_map.shape[0]
    tile = 256
    slots = devices * capacity
    whole = lambda i: (0, 0)
    return pl.pallas_call(
        functools.partial(dispatch_kernel, capacity),
        grid=(width // tile,),
        in_specs=[
            pl.BlockSpec((rows, width), whole),
            pl.BlockSpec((rows, 1), whole),
            pl.BlockSpec((devices, 1), whole),
            pl.BlockSpec((width, tile), lambda i: (0, width // tile + i)),
        ],
        out_specs=[
            pl.BlockSpec((slots, tile), lambda i: (0, i)),
            pl.BlockSpec((rows, 1), whole),
            pl.BlockSpec((rows, width), whole),
        ],
        out_shape=[
            jax.ShapeDtypeStruct((slots, width), BF16),
            jax.ShapeDtypeStruct((rows, 1), jnp.int32),
            jax.ShapeDtypeStruct((rows, width), BF16),
        ],
        scratch_shapes=[pltpu.VMEM((rows, width), BF16), pltpu.VMEM((slots, rows), BF16)],
        compiler_params=pltpu.CompilerParams(vmem_limit_bytes=VMEM_LIMIT),
        cost_estimate=pl.CostEstimate(
            flops=2 * rows * width * (width + slots), bytes_accessed=9 << 20, transcendentals=rows * width
        ),
        name="dispatch",
    )(items, cand_user, owner_map.reshape(devices, 1), w_in)


def gate_kernel(normed, w_gate, out):
    out[...] = silu(dot(normed[...], w_gate[...])).astype(BF16)


def gates(normed, w_in):
    rows, width = normed.shape
    tile = 256
    return pl.pallas_call(
        gate_kernel,
        grid=(width // tile,),
        in_specs=[
            pl.BlockSpec((rows, width), lambda i: (0, 0)),
            pl.BlockSpec((width, tile), lambda i: (0, i)),
        ],
        out_specs=pl.BlockSpec((rows, tile), lambda i: (0, i)),
        out_shape=jax.ShapeDtypeStruct((rows, width), BF16),
        compiler_params=pltpu.CompilerParams(vmem_limit_bytes=VMEM_LIMIT),
        cost_estimate=pl.CostEstimate(
            flops=2 * rows * width * width, bytes_accessed=4 << 20, transcendentals=rows * width
        ),
        name="gates",
    )(normed, w_in)


def attend_kernel(blocks, queries, keys, values, out, total):
    rows, head_dim = queries.shape
    tile = min(rows, 256)
    live = blocks[0]
    half_scale = 0.5 * head_dim ** (-0.5)
    total[...] = jnp.zeros_like(total)

    def span(start, size):
        key = keys[pl.ds(start, size), :]
        value = values[pl.ds(start, size), :]
        for first in range(0, rows, tile):
            query = queries[pl.ds(first, tile), :]
            half = half_scale * lax.dot_general(
                query, key, (((1,), (1,)), ((), ())), preferred_element_type=F32
            )
            weight = (half + half * jnp.tanh(half)).astype(BF16)
            total[pl.ds(first, tile), :] += dot(weight, value)

    def pair(index, carry):
        span(pl.multiple_of(index * (2 * BLOCK), 2 * BLOCK), 2 * BLOCK)
        return carry

    lax.fori_loop(0, live // 2, pair, 0)

    @pl.when(live % 2 == 1)
    def _():
        span(pl.multiple_of((live - 1) * BLOCK, BLOCK), BLOCK)

    out[...] = (total[...] * (1.0 / (BLOCK * live).astype(F32))).astype(BF16)


def attend(blocks, queries, keys, values):
    rows, width = queries.shape
    events = keys.shape[0]
    head_dim = width // HEADS
    column = lambda h, blocks: (0, h)
    return pl.pallas_call(
        attend_kernel,
        grid_spec=pltpu.PrefetchScalarGridSpec(
            num_scalar_prefetch=1,
            grid=(HEADS,),
            in_specs=[
                pl.BlockSpec((rows, head_dim), column),
                pl.BlockSpec((events, head_dim), column),
                pl.BlockSpec((events, head_dim), column),
            ],
            out_specs=pl.BlockSpec((rows, head_dim), column),
            scratch_shapes=[pltpu.VMEM((rows, head_dim), F32)],
        ),
        out_shape=jax.ShapeDtypeStruct((rows, width), BF16),
        compiler_params=pltpu.CompilerParams(vmem_limit_bytes=VMEM_LIMIT),
        cost_estimate=pl.CostEstimate(
            flops=4 * rows * width * events, bytes_accessed=8 << 20, transcendentals=rows * HEADS * events
        ),
        name="attend",
    )(blocks, queries, keys, values)


def finish_kernel(target, returned, gate, items, w_out, out):
    rows = items.shape[0]
    slots = returned.shape[0]
    select = (target[...] == iota((rows, slots), 1)).astype(F32).astype(BF16)
    attention = dot(select, returned[...])
    mixed = (normalize(attention) * gate[...].astype(F32)).astype(BF16)
    out[...] = (items[...].astype(F32) + dot(mixed, w_out[...])).astype(BF16)


def finish(target, returned, gate, items, w_out):
    rows, width = items.shape
    slots = returned.shape[0]
    tile = 256
    whole = lambda i: (0, 0)
    part = lambda i: (i, 0)
    return pl.pallas_call(
        finish_kernel,
        grid=(rows // tile,),
        in_specs=[
            pl.BlockSpec((tile, 1), part),
            pl.BlockSpec((slots, width), whole),
            pl.BlockSpec((tile, width), part),
            pl.BlockSpec((tile, width), part),
            pl.BlockSpec((width, width), whole),
        ],
        out_specs=pl.BlockSpec((tile, width), part),
        out_shape=jax.ShapeDtypeStruct((rows, width), BF16),
        compiler_params=pltpu.CompilerParams(vmem_limit_bytes=VMEM_LIMIT),
        cost_estimate=pl.CostEstimate(
            flops=2 * rows * width * (width + slots), bytes_accessed=7 << 20, transcendentals=rows
        ),
        name="finish",
    )(target, returned, gate, items, w_out)


def local(items, cand_user, owner_map, hist_blocks, cache_keys, cache_values, w_in, w_out):
    row_count, width = items.shape
    devices = lax.axis_size("dev")
    capacity = max(2, 2 * row_count // devices)
    outgoing, target, normed = dispatch(items, cand_user, owner_map, w_in, capacity)
    arrived = lax.all_to_all(
        outgoing.reshape(devices, capacity, width), "dev", split_axis=0, concat_axis=0, tiled=True
    )
    gate = gates(normed, w_in)
    attended = attend(hist_blocks, arrived.reshape(-1, width), cache_keys[0], cache_values[0])
    returned = lax.all_to_all(
        attended.reshape(devices, capacity, width), "dev", split_axis=0, concat_axis=0, tiled=True
    )
    return finish(target, returned.reshape(-1, width), gate, items, w_out)


def solution(mesh):
    return jax.shard_map(
        local,
        mesh=mesh,
        in_specs=(
            P("dev", None),
            P("dev", None),
            P(),
            P("dev"),
            P("dev", None, None),
            P("dev", None, None),
            P(),
            P(),
        ),
        out_specs=P("dev", None),
        check_vma=False,
    )
```

time: 211 us -> 160 us (0.76)
  matrix products: 65.1 us -> 0 us
  blocking collectives: 52.7 us -> 0 us
  waiting for transfers between devices: 40.3 us -> 91.8 us
  Pallas kernels: 0 us -> 32.6 us
  local copies, waits for them, and re-layouts: 29.8 us -> 16.7 us
  starting transfers between devices: 7.43 us -> 17.8 us
  other arithmetic: 8.88 us -> 0 us
  loops' own time: 5.27 us -> 0 us
    dot_general x12 -> x0, matrix products: 65.1 us -> none  [the longest x8 53.7 us: block_term(): jnp.einsum('rht,thd->rhd', weights, value_block, preferred_element_type=j...]
    all_to_all x1 -> x0, blocking collectives: 52.7 us -> none  [local(): lax.all_to_all(attended, 'dev', split_axis=0, concat_axis=0, tiled=True)]
    all_to_all x1 -> x2, waiting for transfers between devices: 40.3 us -> 91.8 us  [the longest x1 48.2 us: local(): lax.all_to_all(outgoing.reshape(devices, capacity, width), 'dev', split_a...]
    pallas_call x0 -> x4, Pallas kernels: none -> 32.6 us  [the longest x1 18.5 us: attend(): pl.pallas_call(attend_kernel, grid_spec=pltpu.PrefetchScalarGridSpec(num_...]
    all_to_all x1 -> x2, starting transfers between devices: 7.43 us -> 17.8 us  [the longest x1 10.5 us: local(): lax.all_to_all(attended.reshape(devices, capacity, width), 'dev', split_a...]
    dynamic_slice x8 -> x0, local copies, waits for them, and re-layouts: 8.63 us -> none  [block_term(): lax.dynamic_slice_in_dim(keys, offset, BLOCK, 0)]
    convert_element_type x2 -> x0, local copies, waits for them, and re-layouts: 8.34 us -> none  [attend(): return total.reshape(queries.shape).astype(jnp.bfloat16)]
    another operation x1 -> x0, loops' own time: 5.27 us -> none  [attend(): lax.fori_loop(0, keys.shape[0] // BLOCK, lambda index, total: block_term(...]
  transfers between devices with their start and end apart: 1 -> 2, of which waited for: 1 -> 2; matrix products, arithmetic and copies ran while one was open for 4% -> 0% of each run, Pallas kernels for 0% -> 1%
where the time goes in v1:
time: 160 us
  waiting for transfers between devices  91.8 us (57%)
  Pallas kernels  32.6 us (20%)
  starting transfers between devices  17.8 us (11%)
  local copies, waits for them, and re-layouts  16.7 us (10%)
    all_to_all x1, waiting for transfers between devices, local(): lax.all_to_all(outgoing.reshape(devices, capacity, width), 'dev', split_a...  48.2 us
    all_to_all x1, waiting for transfers between devices, local(): lax.all_to_all(attended.reshape(devices, capacity, width), 'dev', split_a...  43.5 us
    pallas_call x1, Pallas kernels, attend(): pl.pallas_call(attend_kernel, grid_spec=pltpu.PrefetchScalarGridSpec(num_...  18.5 us
    unnamed x21, local copies, waits for them, and re-layouts  15.9 us
    all_to_all x1, starting transfers between devices, local(): lax.all_to_all(attended.reshape(devices, capacity, width), 'dev', split_a...  10.5 us
    pallas_call x1, Pallas kernels, dispatch(): pl.pallas_call(functools.partial(dispatch_kernel, capacity), grid=(width...  7.74 us
    all_to_all x1, starting transfers between devices, local(): lax.all_to_all(outgoing.reshape(devices, capacity, width), 'dev', split_a...  7.3 us
    pallas_call x1, Pallas kernels, finish(): pl.pallas_call(finish_kernel, grid=(rows // tile,), in_specs=[pl.BlockSpe...  4.15 us
  transfers between devices with their start and end apart: 2, of which 2 were waited for; matrix products, arithmetic and copies ran while one was open for 0% of the time, Pallas kernels for 1%

profile of v1, /device:TPU:0, one launch (start us, length us, event | category | flops | bytes accessed | tf_op | source)
XLA Modules:
  0.0 159.6 jit_solution(7356003059555821294)
XLA Ops:
  0.0 0.8 copy.9.cand
  0.8 0.7 copy.10.owner_map
  1.6 0.0 copy-start
  1.6 2.2 %copy-done = bf16[1024,2048]{1,0:T(8,128)(2,1)S(1)} copy-done((bf16[1024,2048]{1,0:T(8,128)(2,1)S(1)}, bf16[1024,2048]{1,0:T(8,128)(2,1)}, u32[]{:S(2)}) %copy-start) | copy-done | bytes 4194328
  3.8 0.0 copy-start.8
  3.8 1.2 copy-done.8
  5.0 7.7 %dispatch.1 = (bf16[1024,1024]{1,0:T(8,128)(2,1)}, s32[512,1]{1,0:T(8,128)S(1)}, bf16[512,1024]{1,0:T(8,128)(2,1)S(1)}) custom-call(bf16[512,1024]{1,0:T(8,128)(2,1)S(1)} %copy-done.8, s32[512,1]{1,0:T(8,128)S(1)} %copy.9.cand, s32[32,1]{1,0:T(8,128)S(1)} %copy.10.owner_map, bf16[1024,2048]{1,0:T(8,128)(2,1)S(1)} %copy-done), custom_call_target="tpu_custom_call" | custom-call | flops 2147483648 | bytes 9437184 | tf_op jit(solution)/shard_map/dispatch/pallas_call | solution.py:72
  12.7 7.3 %all-to-all-start = ((bf16[32,32,1024]{2,1,0:T(8,128)(2,1)}), bf16[32,32,1024]{2,1,0:T(8,128)(2,1)S(1)}, u32[]{:S(2)}, u32[]{:S(2)}) async-start(bf16[32,32,1024]{2,1,0:T(8,128)(2,1)} %bitcast.1), calls=%async_computation | async-start | bytes 4194304 | tf_op jit(solution)/shard_map/all_to_all | solution.py:222
  20.7 48.2 %all-to-all-done = bf16[32,32,1024]{2,1,0:T(8,128)(2,1)S(1)} async-done(((bf16[32,32,1024]{2,1,0:T(8,128)(2,1)}), bf16[32,32,1024]{2,1,0:T(8,128)(2,1)S(1)}, u32[]{:S(2)}, u32[]{:S(2)}) %all-to-all-start) | async-done | bytes 2097184 | tf_op jit(solution)/shard_map/all_to_all | solution.py:222
  68.9 0.0 copy-start.5
  68.9 1.6 copy-done.5
  70.5 0.0 copy-start.6
  70.5 1.6 copy-done.6
  72.1 18.5 %attend.1 = bf16[1024,1024]{1,0:T(8,128)(2,1)S(1)} custom-call(s32[1]{0:T(128)S(6)} %copy.11.blocks, bf16[1024,1024]{1,0:T(8,128)(2,1)S(1)} %bitcast.8, bf16[1024,1024]{1,0:T(8,128)(2,1)S(1)} %bitcast.10, bf16[1024,1024]{1,0:T(8,128)(2,1)S(1)} %bitcast.11), custom_call_target="tpu_custom_call" | custom-call | flops 4294967296 | bytes 8388608 | tf_op jit(solution)/shard_map/attend/pallas_call | solution.py:160
  90.6 0.0 copy-start.2
  90.6 1.3 copy-done.2
  91.9 10.5 %all-to-all-start.1 = ((bf16[32,32,1024]{2,1,0:T(8,128)(2,1)}), bf16[32,32,1024]{2,1,0:T(8,128)(2,1)S(1)}, u32[]{:S(2)}, u32[]{:S(2)}) async-start(bf16[32,32,1024]{2,1,0:T(8,128)(2,1)} %bitcast.9), calls=%async_computation.1 | async-start | bytes 4194304 | tf_op jit(solution)/shard_map/all_to_all | solution.py:227
  102.5 0.0 copy-start.1
  102.5 2.2 %copy-done.1 = bf16[1024,2048]{1,0:T(8,128)(2,1)S(1)} copy-done((bf16[1024,2048]{1,0:T(8,128)(2,1)S(1)}, bf16[1024,2048]{1,0:T(8,128)(2,1)}, u32[]{:S(2)}) %copy-start.1) | copy-done | bytes 4194328
  104.7 2.2 %gates.1.gate = bf16[512,1024]{1,0:T(8,128)(2,1)S(1)} custom-call(bf16[512,1024]{1,0:T(8,128)(2,1)S(1)} %get-tuple-element.10.normed, bf16[1024,2048]{1,0:T(8,128)(2,1)S(1)} %copy-done.1), custom_call_target="tpu_custom_call" | custom-call | flops 1073741824 | bytes 4194304 | tf_op jit(solution)/shard_map/gates/pallas_call | solution.py:107
  106.9 0.0 copy-start.3
  106.9 1.0 copy-done.3
  107.9 43.5 %all-to-all-done.1 = bf16[32,32,1024]{2,1,0:T(8,128)(2,1)S(1)} async-done(((bf16[32,32,1024]{2,1,0:T(8,128)(2,1)}), bf16[32,32,1024]{2,1,0:T(8,128)(2,1)S(1)}, u32[]{:S(2)}, u32[]{:S(2)}) %all-to-all-start.1) | async-done | bytes 2097184 | tf_op jit(solution)/shard_map/all_to_all | solution.py:227
  151.4 0.0 copy-start.4
  151.4 1.2 copy-done.4
  152.6 0.0 copy-start.7
  152.6 1.6 copy-done.7
  154.2 0.0 copy-start.9
  154.2 1.2 copy-done.9
  155.4 4.2 %finish.1 = bf16[512,1024]{1,0:T(8,128)(2,1)} custom-call(s32[512,1]{1,0:T(8,128)S(1)} %get-tuple-element.8.target, bf16[1024,1024]{1,0:T(8,128)(2,1)S(1)} %bitcast.7, bf16[512,1024]{1,0:T(8,128)(2,1)S(1)} %copy-done.4, bf16[512,1024]{1,0:T(8,128)(2,1)S(1)} %copy-done.9, bf16[1024,1024]{1,0:T(8,128)(2,1)S(1)} %copy-done.7), custom_call_target="tpu_custom_call" | custom-call | flops 2147483648 | bytes 7340032 | tf_op jit(solution)/shard_map/finish/pallas_call | solution.py:197
Async XLA Ops:
  1.6 2.2 %copy-start = (bf16[1024,2048]{1,0:T(8,128)(2,1)S(1)}, bf16[1024,2048]{1,0:T(8,128)(2,1)}, u32[]{:S(2)}) copy-start(bf16[1024,2048]{1,0:T(8,128)(2,1)} %w_gate.1) | copy-start | bytes 12582916
  3.8 1.2 copy-start.8
  12.7 56.2 %all-to-all-start = ((bf16[32,32,1024]{2,1,0:T(8,128)(2,1)}), bf16[32,32,1024]{2,1,0:T(8,128)(2,1)S(1)}, u32[]{:S(2)}, u32[]{:S(2)}) async-start(bf16[32,32,1024]{2,1,0:T(8,128)(2,1)} %bitcast.1), calls=%async_computation | async-start | bytes 4194304 | tf_op jit(solution)/shard_map/all_to_all | solution.py:222
  68.9 1.6 copy-start.5
  70.5 1.6 copy-start.6
  90.6 1.3 copy-start.2
  91.9 59.4 %all-to-all-start.1 = ((bf16[32,32,1024]{2,1,0:T(8,128)(2,1)}), bf16[32,32,1024]{2,1,0:T(8,128)(2,1)S(1)}, u32[]{:S(2)}, u32[]{:S(2)}) async-start(bf16[32,32,1024]{2,1,0:T(8,128)(2,1)} %bitcast.9), calls=%async_computation.1 | async-start | bytes 4194304 | tf_op jit(solution)/shard_map/all_to_all | solution.py:227
  102.5 2.2 %copy-start.1 = (bf16[1024,2048]{1,0:T(8,128)(2,1)S(1)}, bf16[1024,2048]{1,0:T(8,128)(2,1)}, u32[]{:S(2)}) copy-start(bf16[1024,2048]{1,0:T(8,128)(2,1)} %w_gate.1) | copy-start | bytes 12582916
  106.9 1.0 copy-start.3
  151.4 1.2 copy-start.4
  152.6 1.6 copy-start.7
  154.2 1.2 copy-start.9

commit v2 on v0

v2 whole, which is shorter than its diff:
```python
import functools

import jax
import jax.numpy as jnp
from jax import lax
from jax.experimental import pallas as pl
from jax.experimental.pallas import tpu as pltpu
from jax.sharding import PartitionSpec as P

HEADS = 8
BLOCK = 128
F32 = jnp.float32
BF16 = jnp.bfloat16
VMEM_LIMIT = 64 * 1024 * 1024 - 64 * 1024
MEMBERS = 8
APART = 2


def normalize(values):
    center = values - jnp.mean(values, axis=-1, keepdims=True)
    spread = jnp.mean(center * center, axis=-1, keepdims=True)
    return center * lax.rsqrt(spread + 1e-06)


def silu(values):
    half = 0.5 * values
    return half + half * jnp.tanh(half)


def iota(shape, dimension):
    return lax.broadcasted_iota(jnp.int32, shape, dimension)


def dot(left, right):
    return jnp.dot(left, right, preferred_element_type=F32)


def exact(condition):
    return condition.astype(F32).astype(BF16)


def params():
    return pltpu.CompilerParams(vmem_limit_bytes=VMEM_LIMIT)


def cost(flops, moved, transcendentals=0):
    return pl.CostEstimate(flops=flops, bytes_accessed=moved, transcendentals=transcendentals)


def as_column(row):
    size = row.shape[1]
    return jnp.broadcast_to(row.astype(F32), (128, size)).T[:, 0:1].astype(jnp.int32)


def route(place, cand, owner_map, capacity):
    rows = cand.shape[1]
    devices = owner_map.shape[1]
    groups = devices // MEMBERS
    user_hot = exact(cand == iota((devices, rows), 0))
    to_owner = exact(owner_map == iota((devices, devices), 0))
    owner_hot = dot(to_owner, user_hot)
    before = exact(iota((rows, rows), 0) < iota((rows, rows), 1))
    rank = dot(owner_hot.astype(BF16), before)
    owner = iota((devices, 128), 0)
    offset = owner ^ place
    group, member = offset // MEMBERS, offset % MEMBERS

    def pick(block):
        start = (block * capacity)[:, 0:1].astype(F32)
        return jnp.sum(owner_hot * (rank + start), axis=0, keepdims=True).astype(jnp.int32)

    return pick(owner), pick(group * MEMBERS + member), pick(member * groups + group)


def prepare_kernel(capacity, place, items, cand, owner_map, w_in, *refs):
    *outs, target_out, back_out, normed, w_query, arrival = refs
    rows, width = items.shape
    part = w_query.shape[1]
    copy = pltpu.make_async_copy(w_in.at[:, pl.ds(width, part)], w_query, arrival)
    copy.start()
    target, ahead, back = route(place[0], cand[...], owner_map[...], capacity)
    target_out[...] = target
    back_out[...] = back
    normed[...] = normalize(items[...].astype(F32)).astype(BF16)
    copy.wait()
    query = silu(dot(normed[...], w_query[...])).astype(BF16)
    size = outs[0].shape[0]
    for index, out in enumerate(outs):
        select = exact(iota((size, rows), 0) + index * size == ahead)
        out[...] = dot(select, query).astype(BF16)


def prepare(place, items, cand_user, owner_map, w_in, capacity, part):
    rows, width = items.shape
    devices = owner_map.shape[0]
    groups = devices // MEMBERS
    slots = devices * capacity
    inside = pl.BlockSpec(memory_space=pltpu.VMEM)
    return pl.pallas_call(
        functools.partial(prepare_kernel, capacity),
        in_specs=[
            pl.BlockSpec(memory_space=pltpu.SMEM),
            inside,
            inside,
            inside,
            pl.BlockSpec(memory_space=pl.ANY),
        ],
        out_specs=[inside] * (groups + 3),
        out_shape=[
            *[jax.ShapeDtypeStruct((slots // groups, part), BF16)] * groups,
            jax.ShapeDtypeStruct((1, rows), jnp.int32),
            jax.ShapeDtypeStruct((1, rows), jnp.int32),
            jax.ShapeDtypeStruct((rows, width), BF16),
        ],
        scratch_shapes=[pltpu.VMEM((width, part), BF16), pltpu.SemaphoreType.DMA],
        compiler_params=params(),
        cost_estimate=cost(2 * rows * part * (width + slots), 4 << 20, rows * part),
        name="prepare",
    )(place, items, cand_user.reshape(1, rows), owner_map.reshape(1, devices), w_in)


def rest_kernel(normed, target, w_in, out, w_query, arrival):
    rows, width = normed.shape
    part = w_query.shape[1]
    copy = pltpu.make_async_copy(w_in.at[:, pl.ds(2 * width - part, part)], w_query, arrival)
    copy.start()
    select = exact(iota((out.shape[0], rows), 0) == target[...])
    copy.wait()
    query = silu(dot(normed[...], w_query[...])).astype(BF16)
    out[...] = dot(select, query).astype(BF16)


def rest(normed, target, w_in, slots, start):
    rows, width = normed.shape
    part = width - start
    inside = pl.BlockSpec(memory_space=pltpu.VMEM)
    return pl.pallas_call(
        rest_kernel,
        in_specs=[inside, inside, pl.BlockSpec(memory_space=pl.ANY)],
        out_specs=inside,
        out_shape=jax.ShapeDtypeStruct((slots, part), BF16),
        scratch_shapes=[pltpu.VMEM((width, part), BF16), pltpu.SemaphoreType.DMA],
        compiler_params=params(),
        cost_estimate=cost(2 * rows * part * (width + slots), 7 << 20, rows * part),
        name="rest",
    )(normed, target, w_in)


def regroup_kernel(count, *refs):
    arrays, outs = refs[:count], refs[count:]
    size = arrays[0].shape[0] // len(outs)
    for first, array in enumerate(arrays):
        for second, out in enumerate(outs):
            out[first * size : (first + 1) * size, :] = array[second * size : (second + 1) * size, :]


def regroup(arrays, parts):
    count = len(arrays)
    rows, width = arrays[0].shape
    size = count * rows // parts
    return pl.pallas_call(
        functools.partial(regroup_kernel, count),
        out_shape=[jax.ShapeDtypeStruct((size, width), BF16)] * parts,
        compiler_params=params(),
        cost_estimate=cost(0, 4 * count * rows * width),
        name="regroup",
    )(*arrays)


def weigh(live, query, keys, values, store):
    half_scale = 0.5 * query.shape[1] ** (-0.5)

    def over(count):
        events = count * BLOCK
        half = half_scale * lax.dot_general(
            query[...], keys[:events, :], (((1,), (1,)), ((), ())), preferred_element_type=F32
        )
        weight = (half + half * jnp.tanh(half)).astype(BF16)
        store((dot(weight, values[:events, :]) * (1.0 / events)).astype(BF16))

    for count in range(1, keys.shape[0] // BLOCK + 1):
        pl.when(live == count)(functools.partial(over, count))


def attend_kernel(blocks, queries, keys, values, out):
    def store(result):
        out[...] = result

    weigh(blocks[0], queries, keys, values, store)


def attend(blocks, queries, keys, values, head):
    rows, width = queries.shape
    events = keys.shape[0]
    head_dim = keys.shape[1] // HEADS
    cache = lambda h, blocks: (0, head + h)
    column = lambda h, blocks: (0, h)
    return pl.pallas_call(
        attend_kernel,
        grid_spec=pltpu.PrefetchScalarGridSpec(
            num_scalar_prefetch=1,
            grid=(width // head_dim,),
            in_specs=[
                pl.BlockSpec((rows, head_dim), column),
                pl.BlockSpec((events, head_dim), cache),
                pl.BlockSpec((events, head_dim), cache),
            ],
            out_specs=pl.BlockSpec((rows, head_dim), column),
        ),
        out_shape=jax.ShapeDtypeStruct((rows, width), BF16),
        compiler_params=params(),
        cost_estimate=cost(8 * rows * width * events, 6 << 20, rows * (width // head_dim) * events),
        name="attend",
    )(blocks, queries, keys, values)


def attend_apart_kernel(members, blocks, *refs):
    queries, (keys, values), outs, gathered = (
        refs[:members],
        refs[members : members + 2],
        refs[members + 2 : -1],
        refs[-1],
    )
    rows = queries[0].shape[0]
    size = rows // len(outs)
    for index, part in enumerate(queries):
        gathered[index * rows : (index + 1) * rows, :] = part[...]

    def store(result):
        for first in range(members):
            for second, out in enumerate(outs):
                start = first * rows + second * size
                out[first * size : (first + 1) * size, :] = result[start : start + size]

    weigh(blocks[0], gathered, keys, values, store)


def attend_apart(blocks, queries, keys, values, groups):
    members = len(queries)
    rows, width = queries[0].shape
    events = keys.shape[0]
    head_dim = keys.shape[1] // HEADS
    column = lambda h, blocks: (0, h)
    out_rows = members * rows // groups
    return pl.pallas_call(
        functools.partial(attend_apart_kernel, members),
        grid_spec=pltpu.PrefetchScalarGridSpec(
            num_scalar_prefetch=1,
            grid=(width // head_dim,),
            in_specs=[
                *[pl.BlockSpec((rows, head_dim), column)] * members,
                pl.BlockSpec((events, head_dim), column),
                pl.BlockSpec((events, head_dim), column),
            ],
            out_specs=[pl.BlockSpec((out_rows, head_dim), column)] * groups,
            scratch_shapes=[pltpu.VMEM((members * rows, head_dim), BF16)],
        ),
        out_shape=[jax.ShapeDtypeStruct((out_rows, width), BF16)] * groups,
        compiler_params=params(),
        cost_estimate=cost(8 * members * rows * width * events, 3 << 20, members * rows * events),
        name="attend_apart",
    )(blocks, *queries, keys, values)


def finish_kernel(members, target, back, returned, *refs):
    apart = refs[:members]
    gate_ref, items_ref, w_ref, out, held, gate, items, weights, arrivals = refs[members:]
    copies = [
        pltpu.make_async_copy(source, kept, arrivals.at[index])
        for index, (source, kept) in enumerate(((w_ref, weights), (gate_ref, gate), (items_ref, items)))
    ]
    for copy in copies:
        copy.start()
    rows = items.shape[0]
    slots = returned.shape[0]
    size = apart[0].shape[0]
    for index, part in enumerate(apart):
        held[index * size : (index + 1) * size, :] = part[...]
    order = iota((rows, slots), 1)
    near = dot(exact(order == as_column(back[...])), held[...])
    far = dot(exact(order == as_column(target[...])), returned[...])
    normed = normalize(jnp.concatenate([near, far], axis=1))
    for copy in copies:
        copy.wait()
    mixed = (normed * gate[...].astype(F32)).astype(BF16)
    out[...] = (items[...].astype(F32) + dot(mixed, weights[...])).astype(BF16)


def finish(target, back, returned, apart, gate, items, w_out):
    rows, width = items.shape
    slots = returned.shape[0]
    anywhere = pl.BlockSpec(memory_space=pl.ANY)
    inside = pl.BlockSpec(memory_space=pltpu.VMEM)
    return pl.pallas_call(
        functools.partial(finish_kernel, len(apart)),
        in_specs=[inside] * (3 + len(apart)) + [anywhere] * 3,
        out_specs=inside,
        out_shape=jax.ShapeDtypeStruct((rows, width), BF16),
        scratch_shapes=[
            pltpu.VMEM((slots, apart[0].shape[1]), BF16),
            pltpu.VMEM((rows, width), BF16),
            pltpu.VMEM((rows, width), BF16),
            pltpu.VMEM((width, width), BF16),
            pltpu.SemaphoreType.DMA((3,)),
        ],
        compiler_params=params(),
        cost_estimate=cost(2 * rows * width * (width + slots), 7 << 20, rows),
        name="finish",
    )(target, back, returned, *apart, gate, items, w_out)


def gate_kernel(normed, w_gate, out):
    out[...] = silu(dot(normed[...], w_gate[...])).astype(BF16)


def gates(normed, w_in):
    rows, width = normed.shape
    tile = 256
    return pl.pallas_call(
        gate_kernel,
        grid=(width // tile,),
        in_specs=[
            pl.BlockSpec((rows, width), lambda i: (0, 0)),
            pl.BlockSpec((width, tile), lambda i: (0, i)),
        ],
        out_specs=pl.BlockSpec((rows, tile), lambda i: (0, i)),
        out_shape=jax.ShapeDtypeStruct((rows, width), BF16),
        compiler_params=params(),
        cost_estimate=pl.CostEstimate(
            flops=2 * rows * width * width, bytes_accessed=4 << 20, transcendentals=rows * width
        ),
        name="gates",
    )(normed, w_in)


def local(items, cand_user, owner_map, hist_blocks, cache_keys, cache_values, w_in, w_out):
    row_count, width = items.shape
    devices = lax.axis_size("dev")
    groups = devices // MEMBERS
    capacity = max(2, 2 * row_count // devices)
    slots = devices * capacity
    part = APART * width // HEADS
    place = lax.axis_index("dev").astype(jnp.int32).reshape(1)
    keys, values = cache_keys[0], cache_values[0]

    def swap(arrays, stride):
        return arrays[:1] + [
            lax.ppermute(array, "dev", [(d, d ^ (index * stride)) for d in range(devices)])
            for index, array in enumerate(arrays)
            if index
        ]

    def exchange(rows):
        blocks = rows.reshape(devices, capacity, rows.shape[1])
        return lax.all_to_all(blocks, "dev", split_axis=0, concat_axis=0, tiled=True).reshape(rows.shape)

    *apart, target, back, normed = prepare(place, items, cand_user, owner_map, w_in, capacity, part)
    apart = swap(apart, MEMBERS)
    outgoing, apart = lax.optimization_barrier((rest(normed, target, w_in, slots, part), apart))
    arrived = exchange(outgoing)
    gate = gates(normed, w_in)
    apart = swap(list(regroup(apart, MEMBERS)), 1)
    apart = list(attend_apart(hist_blocks, apart, keys, values, groups))
    arrived, gate, apart = lax.optimization_barrier((arrived, gate, apart))
    apart = swap(apart, MEMBERS)
    attended, apart = lax.optimization_barrier((attend(hist_blocks, arrived, keys, values, APART), apart))
    returned = exchange(attended)
    apart = swap(list(regroup(apart, MEMBERS)), 1)
    return finish(target, back, returned, apart, gate, items, w_out)


def solution(mesh):
    return jax.shard_map(
        local,
        mesh=mesh,
        in_specs=(
            P("dev", None),
            P("dev", None),
            P(),
            P("dev"),
            P("dev", None, None),
            P("dev", None, None),
            P(),
            P(),
        ),
        out_specs=P("dev", None),
        check_vma=False,
    )
```

time: 211 us -> 126 us (0.60)
  matrix products: 65.1 us -> 0 us
  blocking collectives: 52.7 us -> 0 us
  Pallas kernels: 0 us -> 36.2 us
  local copies, waits for them, and re-layouts: 29.8 us -> 0 us
  starting transfers between devices: 7.43 us -> 33.8 us
  waiting for transfers between devices: 40.3 us -> 54.9 us
  other arithmetic: 8.88 us -> 0 us
  loops' own time: 5.27 us -> 0 us
    dot_general x12 -> x0, matrix products: 65.1 us -> none  [the longest x8 53.7 us: block_term(): jnp.einsum('rht,thd->rhd', weights, value_block, preferred_element_type=j...]
    all_to_all x1 -> x0, blocking collectives: 52.7 us -> none  [local(): lax.all_to_all(attended, 'dev', split_axis=0, concat_axis=0, tiled=True)]
    pallas_call x0 -> x8, Pallas kernels: none -> 36.2 us  [the longest x1 7.84 us: attend(): pl.pallas_call(attend_kernel, grid_spec=pltpu.PrefetchScalarGridSpec(num_...]
    ppermute x0 -> x20, waiting for transfers between devices: none -> 29.3 us  [swap(): lax.ppermute(array, 'dev', [(d, d ^ index * stride) for d in range(device...]
    ppermute x0 -> x20, starting transfers between devices: none -> 23.5 us  [swap(): lax.ppermute(array, 'dev', [(d, d ^ index * stride) for d in range(device...]
    all_to_all x1 -> x2, waiting for transfers between devices: 40.3 us -> 25.5 us  [exchange(): lax.all_to_all(blocks, 'dev', split_axis=0, concat_axis=0, tiled=True)]
    unnamed x18 -> x0, local copies, waits for them, and re-layouts: 12.6 us -> none
    dynamic_slice x8 -> x0, local copies, waits for them, and re-layouts: 8.63 us -> none  [block_term(): lax.dynamic_slice_in_dim(keys, offset, BLOCK, 0)]
  transfers between devices with their start and end apart: 1 -> 22, of which waited for: 1 -> 11; matrix products, arithmetic and copies ran while one was open for 4% -> 0% of each run, Pallas kernels for 0% -> 21%
where the time goes in v2:
time: 126 us
  waiting for transfers between devices  54.9 us (44%)
  Pallas kernels  36.2 us (29%)
  starting transfers between devices  33.8 us (27%)
    ppermute x20, waiting for transfers between devices, swap(): lax.ppermute(array, 'dev', [(d, d ^ index * stride) for d in range(device...  29.3 us
    all_to_all x2, waiting for transfers between devices, exchange(): lax.all_to_all(blocks, 'dev', split_axis=0, concat_axis=0, tiled=True)  25.5 us
    ppermute x20, starting transfers between devices, swap(): lax.ppermute(array, 'dev', [(d, d ^ index * stride) for d in range(device...  23.5 us
    all_to_all x2, starting transfers between devices, exchange(): lax.all_to_all(blocks, 'dev', split_axis=0, concat_axis=0, tiled=True)  10.3 us
    pallas_call x1, Pallas kernels, attend(): pl.pallas_call(attend_kernel, grid_spec=pltpu.PrefetchScalarGridSpec(num_...  7.84 us
    pallas_call x1, Pallas kernels, finish(): pl.pallas_call(functools.partial(finish_kernel, len(apart)), in_specs=[in...  6.01 us
    pallas_call x1, Pallas kernels, rest(): pl.pallas_call(rest_kernel, in_specs=[inside, inside, pl.BlockSpec(memory...  5.74 us
    pallas_call x1, Pallas kernels, gates(): pl.pallas_call(gate_kernel, grid=(width // tile,), in_specs=[pl.BlockSpec...  4.82 us
  transfers between devices with their start and end apart: 22, of which 11 were waited for; matrix products, arithmetic and copies ran while one was open for 0% of the time, Pallas kernels for 21%

profile of v2, /device:TPU:0, one launch (start us, length us, event | category | flops | bytes accessed | tf_op | source)
XLA Modules:
  0.0 125.7 jit_solution(11627301029210822427)
XLA Ops:
  0.0 4.3 %prepare.1 = (bf16[256,256]{1,0:T(8,128)(2,1)}, bf16[256,256]{1,0:T(8,128)(2,1)}, bf16[256,256]{1,0:T(8,128)(2,1)}, bf16[256,256]{1,0:T(8,128)(2,1)}, s32[1,512]...) custom-call(s32[1]{0:T(128)} %bitcast.place, bf16[512,1024]{1,0:T(8,128)(2,1)} %refs_9_.1, s32[1,512]{1,0:T(1,128)} %bitcast.11, ...), custom_call_target="tpu_custom_call" | custom-call | flops 536870912 | bytes 4194304 | tf_op jit(solution)/shard_map/prepare/pallas_call | solution.py:99
  4.3 3.1 %collective-permute-start = (bf16[256,256]{1,0:T(8,128)(2,1)}, bf16[256,256]{1,0:T(8,128)(2,1)}, u32[]{:S(2)}, u32[]{:S(2)}) collective-permute-start(bf16[256,256]{1,0:T(8,128)(2,1)} %get-tuple-element.52), channel_id=1, source_target_pairs={{0,8},{1,9},{2,10},{3,11},{4,12},{5,13},{6,14},{7,15},{8,0},{9,1},... | collective-permute-start | bytes 393224 | tf_op jit(solution)/shard_map/ppermute | solution.py:348
  7.4 2.6 %collective-permute-start.1 = (bf16[256,256]{1,0:T(8,128)(2,1)}, bf16[256,256]{1,0:T(8,128)(2,1)}, u32[]{:S(2)}, u32[]{:S(2)}) collective-permute-start(bf16[256,256]{1,0:T(8,128)(2,1)} %get-tuple-element.53), channel_id=1, source_target_pairs={{0,16},{1,17},{2,18},{3,19},{4,20},{5,21},{6,22},{7,23},{8,24},{9,... | collective-permute-start | bytes 393224 | tf_op jit(solution)/shard_map/ppermute | solution.py:348
  9.9 0.0 collective-permute-start.2
  9.9 5.7 %rest.1 = bf16[1024,768]{1,0:T(8,128)(2,1)} custom-call(bf16[512,1024]{1,0:T(8,128)(2,1)} %get-tuple-element.50.normed, s32[1,512]{1,0:T(1,128)} %get-tuple-element.48.target, bf16[1024,2048]{1,0:T(8,128)(2,1)} %w_gate.1), custom_call_target="tpu_custom_call" | custom-call | flops 1610612736 | bytes 7340032 | tf_op jit(solution)/shard_map/rest/pallas_call | solution.py:137
  15.7 0.0 collective-permute-done.refs_1_
  15.7 4.9 %collective-permute-done.1.refs_2_ = bf16[256,256]{1,0:T(8,128)(2,1)} collective-permute-done((bf16[256,256]{1,0:T(8,128)(2,1)}, bf16[256,256]{1,0:T(8,128)(2,1)}, u32[]{:S(2)}, u32[]{:S(2)}) %collective-permute-start.1) | collective-permute-done | bytes 131104 | tf_op jit(solution)/shard_map/ppermute | solution.py:348
  20.6 0.0 collective-permute-done.2.refs_3_
  20.6 5.3 %all-to-all-start = ((bf16[32,32,768]{2,1,0:T(8,128)(2,1)}), bf16[32,32,768]{2,1,0:T(8,128)(2,1)}, u32[]{:S(2)}, u32[]{:S(2)}) async-start(bf16[32,32,768]{2,1,0:T(8,128)(2,1)} %bitcast.9), calls=%async_computation | async-start | bytes 3145728 | tf_op jit(solution)/shard_map/all_to_all | solution.py:355
  25.9 1.9 %regroup.2 = (bf16[128,256]{1,0:T(8,128)(2,1)}, bf16[128,256]{1,0:T(8,128)(2,1)}, bf16[128,256]{1,0:T(8,128)(2,1)}, bf16[128,256]{1,0:T(8,128)(2,1)}, bf16[128,2...) custom-call(bf16[256,256]{1,0:T(8,128)(2,1)} %get-tuple-element.56.refs_0_, ...), custom_call_target="tpu_custom_call" | custom-call | bytes 1048576 | tf_op jit(solution)/shard_map/regroup/pallas_call | solution.py:161
  27.9 0.2 collective-permute-start.3
  28.0 1.7 %collective-permute-start.4 = (bf16[128,256]{1,0:T(8,128)(2,1)}, bf16[128,256]{1,0:T(8,128)(2,1)}, u32[]{:S(2)}, u32[]{:S(2)}) collective-permute-start(bf16[128,256]{1,0:T(8,128)(2,1)} %get-tuple-element.62), channel_id=1, source_target_pairs={{0,2},{1,3},{2,0},{3,1},{4,6},{5,7},{6,4},{7,5},{8,10},{9,11},{10,... | collective-permute-start | bytes 196616 | tf_op jit(solution)/shard_map/ppermute | solution.py:348
  30.4 0.1 collective-permute-start.5
  30.5 1.7 %collective-permute-start.6 = (bf16[128,256]{1,0:T(8,128)(2,1)}, bf16[128,256]{1,0:T(8,128)(2,1)}, u32[]{:S(2)}, u32[]{:S(2)}) collective-permute-start(bf16[128,256]{1,0:T(8,128)(2,1)} %get-tuple-element.64), channel_id=1, source_target_pairs={{0,4},{1,5},{2,6},{3,7},{4,0},{5,1},{6,2},{7,3},{8,12},{9,13},{10,... | collective-permute-start | bytes 196616 | tf_op jit(solution)/shard_map/ppermute | solution.py:348
  32.1 0.1 collective-permute-start.7
  32.3 0.0 collective-permute-done.3.refs_1_
  32.3 2.6 %collective-permute-start.8 = (bf16[128,256]{1,0:T(8,128)(2,1)}, bf16[128,256]{1,0:T(8,128)(2,1)}, u32[]{:S(2)}, u32[]{:S(2)}) collective-permute-start(bf16[128,256]{1,0:T(8,128)(2,1)} %get-tuple-element.66), channel_id=1, source_target_pairs={{0,6},{1,7},{2,4},{3,5},{4,2},{5,3},{6,0},{7,1},{8,14},{9,15},{10,... | collective-permute-start | bytes 196616 | tf_op jit(solution)/shard_map/ppermute | solution.py:348
  34.8 5.6 %collective-permute-done.4.refs_2_ = bf16[128,256]{1,0:T(8,128)(2,1)} collective-permute-done((bf16[128,256]{1,0:T(8,128)(2,1)}, bf16[128,256]{1,0:T(8,128)(2,1)}, u32[]{:S(2)}, u32[]{:S(2)}) %collective-permute-start.4) | collective-permute-done | bytes 65568 | tf_op jit(solution)/shard_map/ppermute | solution.py:348
  40.5 0.4 collective-permute-start.9
  40.9 4.8 %gates.1.refs_8_ = bf16[512,1024]{1,0:T(8,128)(2,1)} custom-call(bf16[512,1024]{1,0:T(8,128)(2,1)} %get-tuple-element.50.normed, bf16[1024,2048]{1,0:T(8,128)(2,1)} %w_gate.1), custom_call_target="tpu_custom_call" | custom-call | flops 1073741824 | bytes 4194304 | tf_op jit(solution)/shard_map/gates/pallas_call | solution.py:319
  45.7 0.0 collective-permute-done.5.refs_3_
  45.7 0.0 collective-permute-done.7.refs_5_
  45.7 2.9 %collective-permute-done.8.refs_6_ = bf16[128,256]{1,0:T(8,128)(2,1)} collective-permute-done((bf16[128,256]{1,0:T(8,128)(2,1)}, bf16[128,256]{1,0:T(8,128)(2,1)}, u32[]{:S(2)}, u32[]{:S(2)}) %collective-permute-start.8) | collective-permute-done | bytes 65568 | tf_op jit(solution)/shard_map/ppermute | solution.py:348
  48.6 0.4 collective-permute-done.9.refs_7_
  49.0 3.7 %attend_apart.1 = (bf16[256,256]{1,0:T(8,128)(2,1)}, bf16[256,256]{1,0:T(8,128)(2,1)}, bf16[256,256]{1,0:T(8,128)(2,1)}, bf16[256,256]{1,0:T(8,128)(2,1)}) custom-call(s32[1]{0:T(128)S(6)} %copy.9.blocks, bf16[128,256]{1,0:T(8,128)(2,1)} %get-tuple-element.60.refs_0_, bf16[128,256]{1,0:T(8,128)(2,1)} %collective-permute-done.3.refs_1_, ...), custom_call_target="tpu_custom_call" | custom-call | flops 2147483648 | bytes 3145728 | tf_op jit(solution)/shard_map/attend_apart/pallas_call | solution.py:245
  52.7 10.9 %all-to-all-done = bf16[32,32,768]{2,1,0:T(8,128)(2,1)} async-done(((bf16[32,32,768]{2,1,0:T(8,128)(2,1)}), bf16[32,32,768]{2,1,0:T(8,128)(2,1)}, u32[]{:S(2)}, u32[]{:S(2)}) %all-to-all-start) | async-done | bytes 1572896 | tf_op jit(solution)/shard_map/all_to_all | solution.py:355
  63.7 2.1 %collective-permute-start.11 = (bf16[256,256]{1,0:T(8,128)(2,1)}, bf16[256,256]{1,0:T(8,128)(2,1)}, u32[]{:S(2)}, u32[]{:S(2)}) collective-permute-start(bf16[256,256]{1,0:T(8,128)(2,1)} %get-tuple-element.75), channel_id=1, source_target_pairs={{0,16},{1,17},{2,18},{3,19},{4,20},{5,21},{6,22},{7,23},{8,24},{9,... | collective-permute-start | bytes 393224 | tf_op jit(solution)/shard_map/ppermute | solution.py:348
  65.7 2.3 %collective-permute-start.12 = (bf16[256,256]{1,0:T(8,128)(2,1)}, bf16[256,256]{1,0:T(8,128)(2,1)}, u32[]{:S(2)}, u32[]{:S(2)}) collective-permute-start(bf16[256,256]{1,0:T(8,128)(2,1)} %get-tuple-element.76), channel_id=1, source_target_pairs={{0,24},{1,25},{2,26},{3,27},{4,28},{5,29},{6,30},{7,31},{8,16},{9,... | collective-permute-start | bytes 393224 | tf_op jit(solution)/shard_map/ppermute | solution.py:348
  68.1 7.8 %attend.1 = bf16[1024,768]{1,0:T(8,128)(2,1)} custom-call(s32[1]{0:T(128)S(6)} %copy.9.blocks, bf16[1024,768]{1,0:T(8,128)(2,1)} %bitcast.4.queries, bf16[1024,1024]{1,0:T(8,128)(2,1)} %bitcast.14, bf16[1024,1024]{1,0:T(8,128)(2,1)} %bitcast.16), custom_call_target="tpu_custom_call" | custom-call | flops 6442450944 | bytes 6291456 | tf_op jit(solution)/shard_map/attend/pallas_call | solution.py:198
  75.9 0.0 collective-permute-done.10.refs_1_
  75.9 1.0 collective-permute-done.11.refs_2_
  76.9 0.0 collective-permute-done.12.refs_3_
  76.9 4.9 %all-to-all-start.1 = ((bf16[32,32,768]{2,1,0:T(8,128)(2,1)}), bf16[32,32,768]{2,1,0:T(8,128)(2,1)}, u32[]{:S(2)}, u32[]{:S(2)}) async-start(bf16[32,32,768]{2,1,0:T(8,128)(2,1)} %bitcast.10), calls=%async_computation.1 | async-start | bytes 3145728 | tf_op jit(solution)/shard_map/all_to_all | solution.py:355
  81.8 1.9 %regroup.3 = (bf16[128,256]{1,0:T(8,128)(2,1)}, bf16[128,256]{1,0:T(8,128)(2,1)}, bf16[128,256]{1,0:T(8,128)(2,1)}, bf16[128,256]{1,0:T(8,128)(2,1)}, bf16[128,2...) custom-call(bf16[256,256]{1,0:T(8,128)(2,1)} %get-tuple-element.78.refs_0_, ...), custom_call_target="tpu_custom_call" | custom-call | bytes 1048576 | tf_op jit(solution)/shard_map/regroup/pallas_call | solution.py:161
  83.7 0.2 collective-permute-start.13
  83.9 1.7 %collective-permute-start.14 = (bf16[128,256]{1,0:T(8,128)(2,1)}, bf16[128,256]{1,0:T(8,128)(2,1)}, u32[]{:S(2)}, u32[]{:S(2)}) collective-permute-start(bf16[128,256]{1,0:T(8,128)(2,1)} %get-tuple-element.84), channel_id=1, source_target_pairs={{0,2},{1,3},{2,0},{3,1},{4,6},{5,7},{6,4},{7,5},{8,10},{9,11},{10,... | collective-permute-start | bytes 196616 | tf_op jit(solution)/shard_map/ppermute | solution.py:348
  85.6 0.0 collective-permute-start.15
  85.6 1.7 %collective-permute-start.16 = (bf16[128,256]{1,0:T(8,128)(2,1)}, bf16[128,256]{1,0:T(8,128)(2,1)}, u32[]{:S(2)}, u32[]{:S(2)}) collective-permute-start(bf16[128,256]{1,0:T(8,128)(2,1)} %get-tuple-element.86), channel_id=1, source_target_pairs={{0,4},{1,5},{2,6},{3,7},{4,0},{5,1},{6,2},{7,3},{8,12},{9,13},{10,... | collective-permute-start | bytes 196616 | tf_op jit(solution)/shard_map/ppermute | solution.py:348
  87.3 0.1 collective-permute-start.17
  87.4 2.6 %collective-permute-start.18 = (bf16[128,256]{1,0:T(8,128)(2,1)}, bf16[128,256]{1,0:T(8,128)(2,1)}, u32[]{:S(2)}, u32[]{:S(2)}) collective-permute-start(bf16[128,256]{1,0:T(8,128)(2,1)} %get-tuple-element.88), channel_id=1, source_target_pairs={{0,6},{1,7},{2,4},{3,5},{4,2},{5,3},{6,0},{7,1},{8,14},{9,15},{10,... | collective-permute-start | bytes 196616 | tf_op jit(solution)/shard_map/ppermute | solution.py:348
  90.0 6.4 %collective-permute-done.14.refs_2_ = bf16[128,256]{1,0:T(8,128)(2,1)} collective-permute-done((bf16[128,256]{1,0:T(8,128)(2,1)}, bf16[128,256]{1,0:T(8,128)(2,1)}, u32[]{:S(2)}, u32[]{:S(2)}) %collective-permute-start.14) | collective-permute-done | bytes 65568 | tf_op jit(solution)/shard_map/ppermute | solution.py:348
  96.4 0.4 collective-permute-start.19
  96.8 0.1 collective-permute-done.15.refs_3_
  96.9 0.0 collective-permute-done.16.refs_4_
  96.9 7.6 %collective-permute-done.18.refs_6_ = bf16[128,256]{1,0:T(8,128)(2,1)} collective-permute-done((bf16[128,256]{1,0:T(8,128)(2,1)}, bf16[128,256]{1,0:T(8,128)(2,1)}, u32[]{:S(2)}, u32[]{:S(2)}) %collective-permute-start.18) | collective-permute-done | bytes 65568 | tf_op jit(solution)/shard_map/ppermute | solution.py:348
  104.5 0.4 collective-permute-done.19.refs_7_
  104.9 14.6 %all-to-all-done.1 = bf16[32,32,768]{2,1,0:T(8,128)(2,1)} async-done(((bf16[32,32,768]{2,1,0:T(8,128)(2,1)}), bf16[32,32,768]{2,1,0:T(8,128)(2,1)}, u32[]{:S(2)}, u32[]{:S(2)}) %all-to-all-start.1) | async-done | bytes 1572896 | tf_op jit(solution)/shard_map/all_to_all | solution.py:355
  119.6 6.0 %finish.1 = bf16[512,1024]{1,0:T(8,128)(2,1)} custom-call(s32[1,512]{1,0:T(1,128)} %get-tuple-element.48.target, s32[1,512]{1,0:T(1,128)} %get-tuple-element.49.back, bf16[1024,768]{1,0:T(8,128)(2,1)} %bitcast.8.returned, bf16[128,256]{1,0:T(8,128)(2,1)} %get-tuple-element.82.refs_0_, bf16[128,256]{1,0:T(8,128)(2,1)} %collective-permute-done.13.refs_1_, ...), custom_call_target="tpu_custom_call" | custom-call | flops 2147483648 | bytes 7340032 | tf_op jit(solution)/shard_map/finish/pallas_call | solution.py:294
  (4 shorter events, 0.0 us)
Async XLA Ops:
  4.3 11.4 %collective-permute-start = (bf16[256,256]{1,0:T(8,128)(2,1)}, bf16[256,256]{1,0:T(8,128)(2,1)}, u32[]{:S(2)}, u32[]{:S(2)}) collective-permute-start(bf16[256,256]{1,0:T(8,128)(2,1)} %get-tuple-element.52), channel_id=1, source_target_pairs={{0,8},{1,9},{2,10},{3,11},{4,12},{5,13},{6,14},{7,15},{8,0},{9,1},... | collective-permute-start | bytes 393224 | tf_op jit(solution)/shard_map/ppermute | solution.py:348
  7.4 13.2 %collective-permute-start.1 = (bf16[256,256]{1,0:T(8,128)(2,1)}, bf16[256,256]{1,0:T(8,128)(2,1)}, u32[]{:S(2)}, u32[]{:S(2)}) collective-permute-start(bf16[256,256]{1,0:T(8,128)(2,1)} %get-tuple-element.53), channel_id=1, source_target_pairs={{0,16},{1,17},{2,18},{3,19},{4,20},{5,21},{6,22},{7,23},{8,24},{9,... | collective-permute-start | bytes 393224 | tf_op jit(solution)/shard_map/ppermute | solution.py:348
  9.9 10.7 %collective-permute-start.2 = (bf16[256,256]{1,0:T(8,128)(2,1)}, bf16[256,256]{1,0:T(8,128)(2,1)}, u32[]{:S(2)}, u32[]{:S(2)}) collective-permute-start(bf16[256,256]{1,0:T(8,128)(2,1)} %get-tuple-element.54), channel_id=1, source_target_pairs={{0,24},{1,25},{2,26},{3,27},{4,28},{5,29},{6,30},{7,31},{8,16},{9,... | collective-permute-start | bytes 393224 | tf_op jit(solution)/shard_map/ppermute | solution.py:348
  20.6 43.1 %all-to-all-start = ((bf16[32,32,768]{2,1,0:T(8,128)(2,1)}), bf16[32,32,768]{2,1,0:T(8,128)(2,1)}, u32[]{:S(2)}, u32[]{:S(2)}) async-start(bf16[32,32,768]{2,1,0:T(8,128)(2,1)} %bitcast.9), calls=%async_computation | async-start | bytes 3145728 | tf_op jit(solution)/shard_map/all_to_all | solution.py:355
  27.9 4.4 %collective-permute-start.3 = (bf16[128,256]{1,0:T(8,128)(2,1)}, bf16[128,256]{1,0:T(8,128)(2,1)}, u32[]{:S(2)}, u32[]{:S(2)}) collective-permute-start(bf16[128,256]{1,0:T(8,128)(2,1)} %get-tuple-element.61), channel_id=1, source_target_pairs={{0,1},{1,0},{2,3},{3,2},{4,5},{5,4},{6,7},{7,6},{8,9},{9,8},{10,11... | collective-permute-start | bytes 196616 | tf_op jit(solution)/shard_map/ppermute | solution.py:348
  28.0 12.4 %collective-permute-start.4 = (bf16[128,256]{1,0:T(8,128)(2,1)}, bf16[128,256]{1,0:T(8,128)(2,1)}, u32[]{:S(2)}, u32[]{:S(2)}) collective-permute-start(bf16[128,256]{1,0:T(8,128)(2,1)} %get-tuple-element.62), channel_id=1, source_target_pairs={{0,2},{1,3},{2,0},{3,1},{4,6},{5,7},{6,4},{7,5},{8,10},{9,11},{10,... | collective-permute-start | bytes 196616 | tf_op jit(solution)/shard_map/ppermute | solution.py:348
  30.4 15.4 %collective-permute-start.5 = (bf16[128,256]{1,0:T(8,128)(2,1)}, bf16[128,256]{1,0:T(8,128)(2,1)}, u32[]{:S(2)}, u32[]{:S(2)}) collective-permute-start(bf16[128,256]{1,0:T(8,128)(2,1)} %get-tuple-element.63), channel_id=1, source_target_pairs={{0,3},{1,2},{2,1},{3,0},{4,7},{5,6},{6,5},{7,4},{8,11},{9,10},{10,... | collective-permute-start | bytes 196616 | tf_op jit(solution)/shard_map/ppermute | solution.py:348
  30.5 15.3 %collective-permute-start.6 = (bf16[128,256]{1,0:T(8,128)(2,1)}, bf16[128,256]{1,0:T(8,128)(2,1)}, u32[]{:S(2)}, u32[]{:S(2)}) collective-permute-start(bf16[128,256]{1,0:T(8,128)(2,1)} %get-tuple-element.64), channel_id=1, source_target_pairs={{0,4},{1,5},{2,6},{3,7},{4,0},{5,1},{6,2},{7,3},{8,12},{9,13},{10,... | collective-permute-start | bytes 196616 | tf_op jit(solution)/shard_map/ppermute | solution.py:348
  32.1 13.6 %collective-permute-start.7 = (bf16[128,256]{1,0:T(8,128)(2,1)}, bf16[128,256]{1,0:T(8,128)(2,1)}, u32[]{:S(2)}, u32[]{:S(2)}) collective-permute-start(bf16[128,256]{1,0:T(8,128)(2,1)} %get-tuple-element.65), channel_id=1, source_target_pairs={{0,5},{1,4},{2,7},{3,6},{4,1},{5,0},{6,3},{7,2},{8,13},{9,12},{10,... | collective-permute-start | bytes 196616 | tf_op jit(solution)/shard_map/ppermute | solution.py:348
  32.3 16.3 %collective-permute-start.8 = (bf16[128,256]{1,0:T(8,128)(2,1)}, bf16[128,256]{1,0:T(8,128)(2,1)}, u32[]{:S(2)}, u32[]{:S(2)}) collective-permute-start(bf16[128,256]{1,0:T(8,128)(2,1)} %get-tuple-element.66), channel_id=1, source_target_pairs={{0,6},{1,7},{2,4},{3,5},{4,2},{5,3},{6,0},{7,1},{8,14},{9,15},{10,... | collective-permute-start | bytes 196616 | tf_op jit(solution)/shard_map/ppermute | solution.py:348
  40.5 8.6 %collective-permute-start.9 = (bf16[128,256]{1,0:T(8,128)(2,1)}, bf16[128,256]{1,0:T(8,128)(2,1)}, u32[]{:S(2)}, u32[]{:S(2)}) collective-permute-start(bf16[128,256]{1,0:T(8,128)(2,1)} %get-tuple-element.67), channel_id=1, source_target_pairs={{0,7},{1,6},{2,5},{3,4},{4,3},{5,2},{6,1},{7,0},{8,15},{9,14},{10,... | collective-permute-start | bytes 196616 | tf_op jit(solution)/shard_map/ppermute | solution.py:348
  63.7 12.2 %collective-permute-start.10 = (bf16[256,256]{1,0:T(8,128)(2,1)}, bf16[256,256]{1,0:T(8,128)(2,1)}, u32[]{:S(2)}, u32[]{:S(2)}) collective-permute-start(bf16[256,256]{1,0:T(8,128)(2,1)} %get-tuple-element.74), channel_id=1, source_target_pairs={{0,8},{1,9},{2,10},{3,11},{4,12},{5,13},{6,14},{7,15},{8,0},{9,1},... | collective-permute-start | bytes 393224 | tf_op jit(solution)/shard_map/ppermute | solution.py:348
  63.7 13.2 %collective-permute-start.11 = (bf16[256,256]{1,0:T(8,128)(2,1)}, bf16[256,256]{1,0:T(8,128)(2,1)}, u32[]{:S(2)}, u32[]{:S(2)}) collective-permute-start(bf16[256,256]{1,0:T(8,128)(2,1)} %get-tuple-element.75), channel_id=1, source_target_pairs={{0,16},{1,17},{2,18},{3,19},{4,20},{5,21},{6,22},{7,23},{8,24},{9,... | collective-permute-start | bytes 393224 | tf_op jit(solution)/shard_map/ppermute | solution.py:348
  65.7 11.2 %collective-permute-start.12 = (bf16[256,256]{1,0:T(8,128)(2,1)}, bf16[256,256]{1,0:T(8,128)(2,1)}, u32[]{:S(2)}, u32[]{:S(2)}) collective-permute-start(bf16[256,256]{1,0:T(8,128)(2,1)} %get-tuple-element.76), channel_id=1, source_target_pairs={{0,24},{1,25},{2,26},{3,27},{4,28},{5,29},{6,30},{7,31},{8,16},{9,... | collective-permute-start | bytes 393224 | tf_op jit(solution)/shard_map/ppermute | solution.py:348
  76.9 42.7 %all-to-all-start.1 = ((bf16[32,32,768]{2,1,0:T(8,128)(2,1)}), bf16[32,32,768]{2,1,0:T(8,128)(2,1)}, u32[]{:S(2)}, u32[]{:S(2)}) async-start(bf16[32,32,768]{2,1,0:T(8,128)(2,1)} %bitcast.10), calls=%async_computation.1 | async-start | bytes 3145728 | tf_op jit(solution)/shard_map/all_to_all | solution.py:355
  83.7 3.7 %collective-permute-start.13 = (bf16[128,256]{1,0:T(8,128)(2,1)}, bf16[128,256]{1,0:T(8,128)(2,1)}, u32[]{:S(2)}, u32[]{:S(2)}) collective-permute-start(bf16[128,256]{1,0:T(8,128)(2,1)} %get-tuple-element.83), channel_id=1, source_target_pairs={{0,1},{1,0},{2,3},{3,2},{4,5},{5,4},{6,7},{7,6},{8,9},{9,8},{10,11... | collective-permute-start | bytes 196616 | tf_op jit(solution)/shard_map/ppermute | solution.py:348
  83.9 12.4 %collective-permute-start.14 = (bf16[128,256]{1,0:T(8,128)(2,1)}, bf16[128,256]{1,0:T(8,128)(2,1)}, u32[]{:S(2)}, u32[]{:S(2)}) collective-permute-start(bf16[128,256]{1,0:T(8,128)(2,1)} %get-tuple-element.84), channel_id=1, source_target_pairs={{0,2},{1,3},{2,0},{3,1},{4,6},{5,7},{6,4},{7,5},{8,10},{9,11},{10,... | collective-permute-start | bytes 196616 | tf_op jit(solution)/shard_map/ppermute | solution.py:348
  85.6 11.3 %collective-permute-start.15 = (bf16[128,256]{1,0:T(8,128)(2,1)}, bf16[128,256]{1,0:T(8,128)(2,1)}, u32[]{:S(2)}, u32[]{:S(2)}) collective-permute-start(bf16[128,256]{1,0:T(8,128)(2,1)} %get-tuple-element.85), channel_id=1, source_target_pairs={{0,3},{1,2},{2,1},{3,0},{4,7},{5,6},{6,5},{7,4},{8,11},{9,10},{10,... | collective-permute-start | bytes 196616 | tf_op jit(solution)/shard_map/ppermute | solution.py:348
  85.6 11.3 %collective-permute-start.16 = (bf16[128,256]{1,0:T(8,128)(2,1)}, bf16[128,256]{1,0:T(8,128)(2,1)}, u32[]{:S(2)}, u32[]{:S(2)}) collective-permute-start(bf16[128,256]{1,0:T(8,128)(2,1)} %get-tuple-element.86), channel_id=1, source_target_pairs={{0,4},{1,5},{2,6},{3,7},{4,0},{5,1},{6,2},{7,3},{8,12},{9,13},{10,... | collective-permute-start | bytes 196616 | tf_op jit(solution)/shard_map/ppermute | solution.py:348
  87.3 9.6 %collective-permute-start.17 = (bf16[128,256]{1,0:T(8,128)(2,1)}, bf16[128,256]{1,0:T(8,128)(2,1)}, u32[]{:S(2)}, u32[]{:S(2)}) collective-permute-start(bf16[128,256]{1,0:T(8,128)(2,1)} %get-tuple-element.87), channel_id=1, source_target_pairs={{0,5},{1,4},{2,7},{3,6},{4,1},{5,0},{6,3},{7,2},{8,13},{9,12},{10,... | collective-permute-start | bytes 196616 | tf_op jit(solution)/shard_map/ppermute | solution.py:348
  87.4 17.1 %collective-permute-start.18 = (bf16[128,256]{1,0:T(8,128)(2,1)}, bf16[128,256]{1,0:T(8,128)(2,1)}, u32[]{:S(2)}, u32[]{:S(2)}) collective-permute-start(bf16[128,256]{1,0:T(8,128)(2,1)} %get-tuple-element.88), channel_id=1, source_target_pairs={{0,6},{1,7},{2,4},{3,5},{4,2},{5,3},{6,0},{7,1},{8,14},{9,15},{10,... | collective-permute-start | bytes 196616 | tf_op jit(solution)/shard_map/ppermute | solution.py:348
  96.4 8.6 %collective-permute-start.19 = (bf16[128,256]{1,0:T(8,128)(2,1)}, bf16[128,256]{1,0:T(8,128)(2,1)}, u32[]{:S(2)}, u32[]{:S(2)}) collective-permute-start(bf16[128,256]{1,0:T(8,128)(2,1)} %get-tuple-element.89), channel_id=1, source_target_pairs={{0,7},{1,6},{2,5},{3,4},{4,3},{5,2},{6,1},{7,0},{8,15},{9,14},{10,... | collective-permute-start | bytes 196616 | tf_op jit(solution)/shard_map/ppermute | solution.py:348

commit v3 on v2

--- a/solution.py
+++ b/solution.py
@@ -13,7 +13,7 @@
 BF16 = jnp.bfloat16
 VMEM_LIMIT = 64 * 1024 * 1024 - 64 * 1024
 MEMBERS = 8
-APART = 2
+APART = 3
 
 
 def normalize(values):
@@ -72,78 +72,108 @@
     return pick(owner), pick(group * MEMBERS + member), pick(member * groups + group)
 
 
-def prepare_kernel(capacity, place, items, cand, owner_map, w_in, *refs):
-    *outs, target_out, back_out, normed, w_query, arrival = refs
+def started(pairs, arrivals):
+    copies = [
+        pltpu.make_async_copy(source, kept, arrivals.at[index]) for index, (source, kept) in enumerate(pairs)
+    ]
+    for copy in copies:
+        copy.start()
+    return copies
+
+
+def prepare_kernel(capacity, groups, place, items_in, cand_in, map_in, w_in, *refs):
+    outs, slots_out, kept, staged, slots, arrivals, departures = (
+        refs[:groups],
+        refs[groups],
+        refs[groups + 1 : groups + 5],
+        refs[-4],
+        refs[-3],
+        refs[-2],
+        refs[-1],
+    )
+    cand, owner_map, items, w_query = kept
     rows, width = items.shape
     part = w_query.shape[1]
-    copy = pltpu.make_async_copy(w_in.at[:, pl.ds(width, part)], w_query, arrival)
-    copy.start()
+    sources = (cand_in, map_in, items_in, w_in.at[:, pl.ds(width, part)])
+    copies = started(zip(sources, kept), arrivals)
+    copies[0].wait()
+    copies[1].wait()
     target, ahead, back = route(place[0], cand[...], owner_map[...], capacity)
-    target_out[...] = target
-    back_out[...] = back
-    normed[...] = normalize(items[...].astype(F32)).astype(BF16)
-    copy.wait()
-    query = silu(dot(normed[...], w_query[...])).astype(BF16)
-    size = outs[0].shape[0]
-    for index, out in enumerate(outs):
-        select = exact(iota((size, rows), 0) + index * size == ahead)
-        out[...] = dot(select, query).astype(BF16)
+    slots[0:1, :] = target
+    slots[1:2, :] = back
+    leaving = [pltpu.make_async_copy(slots, slots_out, departures.at[groups])]
+    leaving[0].start()
+    size = staged.shape[1]
+    selects = [exact(iota((size, rows), 0) + index * size == ahead) for index in range(groups)]
+    copies[2].wait()
+    normed = normalize(items[...].astype(F32)).astype(BF16)
+    copies[3].wait()
+    query = silu(dot(normed, w_query[...])).astype(BF16)
+    for index in range(groups):
+        staged[index] = dot(selects[index], query).astype(BF16)
+        leaving.append(pltpu.make_async_copy(staged.at[index], outs[index], departures.at[index]))
+        leaving[-1].start()
+    for copy in leaving:
+        copy.wait()
 
 
 def prepare(place, items, cand_user, owner_map, w_in, capacity, part):
     rows, width = items.shape
     devices = owner_map.shape[0]
     groups = devices // MEMBERS
-    slots = devices * capacity
-    inside = pl.BlockSpec(memory_space=pltpu.VMEM)
-    return pl.pallas_call(
-        functools.partial(prepare_kernel, capacity),
-        in_specs=[
-            pl.BlockSpec(memory_space=pltpu.SMEM),
-            inside,
-            inside,
-            inside,
-            pl.BlockSpec(memory_space=pl.ANY),
+    size = MEMBERS * capacity
+    anywhere = pl.BlockSpec(memory_space=pl.ANY)
+    *apart, slots = pl.pallas_call(
+        functools.partial(prepare_kernel, capacity, groups),
+        in_specs=[pl.BlockSpec(memory_space=pltpu.SMEM)] + [anywhere] * 4,
+        out_specs=[anywhere] * (groups + 1),
+        out_shape=[
+            *[jax.ShapeDtypeStruct((size, part), BF16)] * groups,
+            jax.ShapeDtypeStruct((2, rows), jnp.int32),
         ],
-        out_specs=[inside] * (groups + 3),
-        out_shape=[
-            *[jax.ShapeDtypeStruct((slots // groups, part), BF16)] * groups,
-            jax.ShapeDtypeStruct((1, rows), jnp.int32),
-            jax.ShapeDtypeStruct((1, rows), jnp.int32),
-            jax.ShapeDtypeStruct((rows, width), BF16),
+        scratch_shapes=[
+            pltpu.VMEM((1, rows), jnp.int32),
+            pltpu.VMEM((1, devices), jnp.int32),
+            pltpu.VMEM((rows, width), BF16),
+            pltpu.VMEM((width, part), BF16),
+            pltpu.VMEM((groups, size, part), BF16),
+            pltpu.VMEM((2, rows), jnp.int32),
+            pltpu.SemaphoreType.DMA((4,)),
+            pltpu.SemaphoreType.DMA((groups + 1,)),
         ],
-        scratch_shapes=[pltpu.VMEM((width, part), BF16), pltpu.SemaphoreType.DMA],
-        compiler_params=params(),
-        cost_estimate=cost(2 * rows * part * (width + slots), 4 << 20, rows * part),
+        compiler_params=params(),
+        cost_estimate=cost(2 * rows * part * (width + groups * size), 4 << 20, rows * part),
         name="prepare",
     )(place, items, cand_user.reshape(1, rows), owner_map.reshape(1, devices), w_in)
-
-
-def rest_kernel(normed, target, w_in, out, w_query, arrival):
-    rows, width = normed.shape
+    return apart, slots
+
+
+def rest_kernel(items, slots, w_in, out, w_query, arrival):
+    rows, width = items.shape
     part = w_query.shape[1]
     copy = pltpu.make_async_copy(w_in.at[:, pl.ds(2 * width - part, part)], w_query, arrival)
     copy.start()
-    select = exact(iota((out.shape[0], rows), 0) == target[...])
+    select = exact(iota((out.shape[0], rows), 0) == slots[0:1, :])
+    normed = normalize(items[...].astype(F32)).astype(BF16)
     copy.wait()
-    query = silu(dot(normed[...], w_query[...])).astype(BF16)
+    query = silu(dot(normed, w_query[...])).astype(BF16)
     out[...] = dot(select, query).astype(BF16)
 
 
-def rest(normed, target, w_in, slots, start):
-    rows, width = normed.shape
+def rest(items, slots, w_in, count, start):
+    rows, width = items.shape
     part = width - start
     inside = pl.BlockSpec(memory_space=pltpu.VMEM)
     return pl.pallas_call(
         rest_kernel,
         in_specs=[inside, inside, pl.BlockSpec(memory_space=pl.ANY)],
         out_specs=inside,
-        out_shape=jax.ShapeDtypeStruct((slots, part), BF16),
+        out_shape=jax.ShapeDtypeStruct((count, part), BF16),
         scratch_shapes=[pltpu.VMEM((width, part), BF16), pltpu.SemaphoreType.DMA],
         compiler_params=params(),
-        cost_estimate=cost(2 * rows * part * (width + slots), 7 << 20, rows * part),
+        cost_estimate=cost(2 * rows * part * (width + count), 7 << 20, rows * part),
         name="rest",
-    )(normed, target, w_in)
+    )(items, slots, w_in)
 
 
 def regroup_kernel(count, *refs):
@@ -262,75 +292,98 @@
     )(blocks, *queries, keys, values)
 
 
-def finish_kernel(members, target, back, returned, *refs):
-    apart = refs[:members]
-    gate_ref, items_ref, w_ref, out, held, gate, items, weights, arrivals = refs[members:]
-    copies = [
-        pltpu.make_async_copy(source, kept, arrivals.at[index])
-        for index, (source, kept) in enumerate(((w_ref, weights), (gate_ref, gate), (items_ref, items)))
-    ]
-    for copy in copies:
-        copy.start()
-    rows = items.shape[0]
-    slots = returned.shape[0]
+def collect_kernel(members, slots, *refs):
+    apart, (out, held) = refs[:members], refs[members:]
     size = apart[0].shape[0]
     for index, part in enumerate(apart):
         held[index * size : (index + 1) * size, :] = part[...]
-    order = iota((rows, slots), 1)
-    near = dot(exact(order == as_column(back[...])), held[...])
-    far = dot(exact(order == as_column(target[...])), returned[...])
-    normed = normalize(jnp.concatenate([near, far], axis=1))
-    for copy in copies:
+    select = exact(iota((out.shape[0], held.shape[0]), 1) == as_column(slots[1:2, :]))
+    out[...] = dot(select, held[...]).astype(BF16)
+
+
+def collect(slots, apart):
+    rows = slots.shape[1]
+    size, width = apart[0].shape
+    count = size * len(apart)
+    return pl.pallas_call(
+        functools.partial(collect_kernel, len(apart)),
+        out_shape=jax.ShapeDtypeStruct((rows, width), BF16),
+        scratch_shapes=[pltpu.VMEM((count, width), BF16)],
+        compiler_params=params(),
+        cost_estimate=cost(2 * rows * width * count, 2 << 20),
+        name="collect",
+    )(slots, *apart)
+
+
+def finish_kernel(*refs):
+    sources, out, kept, (staged, arrivals, departures) = refs[:6], refs[6], refs[7:13], refs[13:]
+    slots, returned, near, gate, items, weights = kept
+    copies = started(zip(sources, kept), arrivals)
+    rows, width = items.shape
+    copies[0].wait()
+    select = exact(iota((rows, returned.shape[0]), 1) == as_column(slots[0:1, :]))
+    copies[1].wait()
+    far = dot(select, returned[...])
+    copies[2].wait()
+    normed = normalize(jnp.concatenate([near[...].astype(F32), far], axis=1))
+    for copy in copies[3:]:
         copy.wait()
     mixed = (normed * gate[...].astype(F32)).astype(BF16)
-    out[...] = (items[...].astype(F32) + dot(mixed, weights[...])).astype(BF16)
-
-
-def finish(target, back, returned, apart, gate, items, w_out):
-    rows, width = items.shape
-    slots = returned.shape[0]
+    tile = width // 4
+    leaving = []
+    for index in range(4):
+        part = pl.ds(index * tile, tile)
+        staged[:, part] = (items[:, part].astype(F32) + dot(mixed, weights[:, part])).astype(BF16)
+        leaving.append(pltpu.make_async_copy(staged.at[:, part], out.at[:, part], departures.at[index]))
+        leaving[-1].start()
+    for copy in leaving:
+        copy.wait()
+
+
+def finish(slots, returned, near, gate, items, w_out):
+    rows, width = items.shape
+    count = returned.shape[0]
     anywhere = pl.BlockSpec(memory_space=pl.ANY)
+    arrays = (slots, returned, near, gate, items, w_out)
+    return pl.pallas_call(
+        finish_kernel,
+        in_specs=[anywhere] * 6,
+        out_specs=anywhere,
+        out_shape=jax.ShapeDtypeStruct((rows, width), BF16),
+        scratch_shapes=[
+            *[pltpu.VMEM(array.shape, array.dtype) for array in arrays],
+            pltpu.VMEM((rows, width), BF16),
+            pltpu.SemaphoreType.DMA((6,)),
+            pltpu.SemaphoreType.DMA((4,)),
+        ],
+        compiler_params=params(),
+        cost_estimate=cost(2 * rows * width * (width + count), 7 << 20, rows),
+        name="finish",
+    )(*arrays)
+
+
+def gate_kernel(items, w_in, out, w_gate, arrival):
+    width = items.shape[1]
+    copy = pltpu.make_async_copy(w_in.at[:, pl.ds(0, width)], w_gate, arrival)
+    copy.start()
+    normed = normalize(items[...].astype(F32)).astype(BF16)
+    copy.wait()
+    out[...] = silu(dot(normed, w_gate[...])).astype(BF16)
+
+
+def gates(items, w_in):
+    rows, width = items.shape
     inside = pl.BlockSpec(memory_space=pltpu.VMEM)
     return pl.pallas_call(
-        functools.partial(finish_kernel, len(apart)),
-        in_specs=[inside] * (3 + len(apart)) + [anywhere] * 3,
+        gate_kernel,
+        in_specs=[inside, pl.BlockSpec(memory_space=pl.ANY)],
         out_specs=inside,
         out_shape=jax.ShapeDtypeStruct((rows, width), BF16),
-        scratch_shapes=[
-            pltpu.VMEM((slots, apart[0].shape[1]), BF16),
-            pltpu.VMEM((rows, width), BF16),
-            pltpu.VMEM((rows, width), BF16),
-            pltpu.VMEM((width, width), BF16),
-            pltpu.SemaphoreType.DMA((3,)),
-        ],
-        compiler_params=params(),
-        cost_estimate=cost(2 * rows * width * (width + slots), 7 << 20, rows),
-        name="finish",
-    )(target, back, returned, *apart, gate, items, w_out)
-
-
-def gate_kernel(normed, w_gate, out):
-    out[...] = silu(dot(normed[...], w_gate[...])).astype(BF16)
-
-
-def gates(normed, w_in):
-    rows, width = normed.shape
-    tile = 256
-    return pl.pallas_call(
-        gate_kernel,
-        grid=(width // tile,),
-        in_specs=[
-            pl.BlockSpec((rows, width), lambda i: (0, 0)),
-            pl.BlockSpec((width, tile), lambda i: (0, i)),
-        ],
-        out_specs=pl.BlockSpec((rows, tile), lambda i: (0, i)),
-        out_shape=jax.ShapeDtypeStruct((rows, width), BF16),
-        compiler_params=params(),
-        cost_estimate=pl.CostEstimate(
-            flops=2 * rows * width * width, bytes_accessed=4 << 20, transcendentals=rows * width
-        ),
+        scratch_shapes=[pltpu.VMEM((width, width), BF16), pltpu.SemaphoreType.DMA],
+        compiler_params=params(),
+        cost_estimate=cost(2 * rows * width * width, 4 << 20, rows * width),
         name="gates",
-    )(normed, w_in)
+    )(items, w_in)
 
 
 def local(items, cand_user, owner_map, hist_blocks, cache_keys, cache_values, w_in, w_out):
@@ -338,7 +391,6 @@
     devices = lax.axis_size("dev")
     groups = devices // MEMBERS
     capacity = max(2, 2 * row_count // devices)
-    slots = devices * capacity
     part = APART * width // HEADS
     place = lax.axis_index("dev").astype(jnp.int32).reshape(1)
     keys, values = cache_keys[0], cache_values[0]
@@ -354,19 +406,18 @@
         blocks = rows.reshape(devices, capacity, rows.shape[1])
         return lax.all_to_all(blocks, "dev", split_axis=0, concat_axis=0, tiled=True).reshape(rows.shape)
 
-    *apart, target, back, normed = prepare(place, items, cand_user, owner_map, w_in, capacity, part)
-    apart = swap(apart, MEMBERS)
-    outgoing, apart = lax.optimization_barrier((rest(normed, target, w_in, slots, part), apart))
+    apart, slots = prepare(place, items, cand_user, owner_map, w_in, capacity, part)
+    outgoing, apart = lax.optimization_barrier((rest(items, slots, w_in, devices * capacity, part), swap(apart, MEMBERS)))
     arrived = exchange(outgoing)
-    gate = gates(normed, w_in)
+    gate = gates(items, w_in)
     apart = swap(list(regroup(apart, MEMBERS)), 1)
     apart = list(attend_apart(hist_blocks, apart, keys, values, groups))
-    arrived, gate, apart = lax.optimization_barrier((arrived, gate, apart))
-    apart = swap(apart, MEMBERS)
-    attended, apart = lax.optimization_barrier((attend(hist_blocks, arrived, keys, values, APART), apart))
-    returned = exchange(attended)
+    arrived, gate, apart[0] = lax.optimization_barrier((arrived, gate, apart[0]))
+    attended = attend(hist_blocks, arrived, keys, values, APART)
+    outgoing, apart = lax.optimization_barrier((attended, swap(apart, MEMBERS)))
+    returned = exchange(outgoing)
     apart = swap(list(regroup(apart, MEMBERS)), 1)
-    return finish(target, back, returned, apart, gate, items, w_out)
+    return finish(slots, returned, collect(slots, apart), gate, items, w_out)
 
 
 def solution(mesh):

time: 126 us -> 124 us (0.984)
  waiting for transfers between devices: 54.9 us -> 47.9 us
  Pallas kernels: 36.2 us -> 38.8 us
  starting transfers between devices: 33.8 us -> 35.2 us
    all_to_all x2, waiting for transfers between devices: 25.5 us -> 5.26 us  [exchange(): lax.all_to_all(blocks, 'dev', split_axis=0, concat_axis=0, tiled=True)]
    ppermute x20, waiting for transfers between devices: 29.3 us -> 42.7 us  [swap(): lax.ppermute(array, 'dev', [(d, d ^ index * stride) for d in range(device...]
    pallas_call x3 -> x4, Pallas kernels: 15.1 us -> 17.1 us  [the longest x1 5.13 us: gates(): pl.pallas_call(gate_kernel, in_specs=[inside, pl.BlockSpec(memory_space=p...]
    pallas_call x1, Pallas kernels: 3.69 us -> 4.96 us  [attend_apart(): pl.pallas_call(functools.partial(attend_apart_kernel, members), grid_spec...]
  transfers between devices with their start and end apart: 22 -> 22, of which waited for: 11 -> 11; matrix products, arithmetic and copies ran while one was open for 0% -> 0% of each run, Pallas kernels for 21% -> 24%
where the time goes in v3:
time: 124 us; the launch traced here: 123 us
  waiting for transfers between devices  47.9 us (39%)
  Pallas kernels  38.8 us (31%)
  starting transfers between devices  35.2 us (28%)
    ppermute x20, waiting for transfers between devices, swap(): lax.ppermute(array, 'dev', [(d, d ^ index * stride) for d in range(device...  42.7 us
    ppermute x20, starting transfers between devices, swap(): lax.ppermute(array, 'dev', [(d, d ^ index * stride) for d in range(device...  24 us
    all_to_all x2, starting transfers between devices, exchange(): lax.all_to_all(blocks, 'dev', split_axis=0, concat_axis=0, tiled=True)  11.2 us
    pallas_call x1, Pallas kernels, attend(): pl.pallas_call(attend_kernel, grid_spec=pltpu.PrefetchScalarGridSpec(num_...  6.87 us
    pallas_call x1, Pallas kernels, rest(): pl.pallas_call(rest_kernel, in_specs=[inside, inside, pl.BlockSpec(memory...  5.58 us
    all_to_all x2, waiting for transfers between devices, exchange(): lax.all_to_all(blocks, 'dev', split_axis=0, concat_axis=0, tiled=True)  5.26 us
    pallas_call x1, Pallas kernels, gates(): pl.pallas_call(gate_kernel, in_specs=[inside, pl.BlockSpec(memory_space=p...  5.13 us
    pallas_call x1, Pallas kernels, finish(): pl.pallas_call(finish_kernel, in_specs=[anywhere] * 6, out_specs=anywhere...  5.02 us
  transfers between devices with their start and end apart: 22, of which 11 were waited for; matrix products, arithmetic and copies ran while one was open for 0% of the time, Pallas kernels for 24%

profile of v3, /device:TPU:0, one launch (start us, length us, event | category | flops | bytes accessed | tf_op | source)
XLA Modules:
  0.0 122.9 jit_solution(4736015030290598014)
XLA Ops:
  0.0 4.0 %prepare.1 = (bf16[256,384]{1,0:T(8,128)(2,1)}, bf16[256,384]{1,0:T(8,128)(2,1)}, bf16[256,384]{1,0:T(8,128)(2,1)}, bf16[256,384]{1,0:T(8,128)(2,1)}, s32[2,512]{1,0:T(2,128)}) custom-call(s32[1]{0:T(128)} %bitcast.place, bf16[512,1024]{1,0:T(8,128)(2,1)} %refs_4_.1, s32[1,512]{1,0:T(1,128)} %bitcast.11, s32[1,32]{1,0:T(1,128)} %bitcast.12, ...), custom_call_target="tpu_custom_call" | custom-call | flops 805306368 | bytes 4194304 | tf_op jit(solution)/shard_map/prepare/pallas_call | solution.py:126
  4.0 3.1 %collective-permute-start = (bf16[256,384]{1,0:T(8,128)(2,1)}, bf16[256,384]{1,0:T(8,128)(2,1)}, u32[]{:S(2)}, u32[]{:S(2)}) collective-permute-start(bf16[256,384]{1,0:T(8,128)(2,1)} %get-tuple-element.45), channel_id=1, source_target_pairs={{0,8},{1,9},{2,10},{3,11},{4,12},{5,13},{6,14},{7,15},{8,0},{9,1},... | collective-permute-start | bytes 589832 | tf_op jit(solution)/shard_map/ppermute | solution.py:400
  7.1 2.6 %collective-permute-start.1 = (bf16[256,384]{1,0:T(8,128)(2,1)}, bf16[256,384]{1,0:T(8,128)(2,1)}, u32[]{:S(2)}, u32[]{:S(2)}) collective-permute-start(bf16[256,384]{1,0:T(8,128)(2,1)} %get-tuple-element.46), channel_id=1, source_target_pairs={{0,16},{1,17},{2,18},{3,19},{4,20},{5,21},{6,22},{7,23},{8,24},{9,... | collective-permute-start | bytes 589832 | tf_op jit(solution)/shard_map/ppermute | solution.py:400
  9.7 5.6 %rest.1 = bf16[1024,640]{1,0:T(8,128)(2,1)} custom-call(bf16[512,1024]{1,0:T(8,128)(2,1)} %refs_4_.1, s32[2,512]{1,0:T(2,128)} %get-tuple-element.43.slots.refs_0_, bf16[1024,2048]{1,0:T(8,128)(2,1)} %w_in.5), custom_call_target="tpu_custom_call" | custom-call | flops 1342177280 | bytes 7340032 | tf_op jit(solution)/shard_map/rest/pallas_call | solution.py:167
  15.2 0.5 collective-permute-done.refs_1_
  15.7 8.8 %collective-permute-done.1.refs_2_ = bf16[256,384]{1,0:T(8,128)(2,1)} collective-permute-done((bf16[256,384]{1,0:T(8,128)(2,1)}, bf16[256,384]{1,0:T(8,128)(2,1)}, u32[]{:S(2)}, u32[]{:S(2)}) %collective-permute-start.1) | collective-permute-done | bytes 196640 | tf_op jit(solution)/shard_map/ppermute | solution.py:400
  24.5 0.0 collective-permute-done.2.refs_3_
  24.5 6.9 %all-to-all-start = ((bf16[32,32,640]{2,1,0:T(8,128)(2,1)}), bf16[32,32,640]{2,1,0:T(8,128)(2,1)}, u32[]{:S(2)}, u32[]{:S(2)}) async-start(bf16[32,32,640]{2,1,0:T(8,128)(2,1)} %bitcast.9), calls=%async_computation | async-start | bytes 2621440 | tf_op jit(solution)/shard_map/all_to_all | solution.py:407
  31.5 2.1 %regroup.2 = (bf16[128,384]{1,0:T(8,128)(2,1)}, bf16[128,384]{1,0:T(8,128)(2,1)}, bf16[128,384]{1,0:T(8,128)(2,1)}, bf16[128,384]{1,0:T(8,128)(2,1)}, bf16[128,3...) custom-call(bf16[256,384]{1,0:T(8,128)(2,1)} %get-tuple-element.49.refs_0_, ...), custom_call_target="tpu_custom_call" | custom-call | bytes 1572864 | tf_op jit(solution)/shard_map/regroup/pallas_call | solution.py:191
  33.6 0.0 collective-permute-start.3
  33.6 1.7 %collective-permute-start.4 = (bf16[128,384]{1,0:T(8,128)(2,1)}, bf16[128,384]{1,0:T(8,128)(2,1)}, u32[]{:S(2)}, u32[]{:S(2)}) collective-permute-start(bf16[128,384]{1,0:T(8,128)(2,1)} %get-tuple-element.55), channel_id=1, source_target_pairs={{0,2},{1,3},{2,0},{3,1},{4,6},{5,7},{6,4},{7,5},{8,10},{9,11},{10,... | collective-permute-start | bytes 294920 | tf_op jit(solution)/shard_map/ppermute | solution.py:400
  35.9 0.2 collective-permute-start.5
  36.2 1.5 %collective-permute-start.6 = (bf16[128,384]{1,0:T(8,128)(2,1)}, bf16[128,384]{1,0:T(8,128)(2,1)}, u32[]{:S(2)}, u32[]{:S(2)}) collective-permute-start(bf16[128,384]{1,0:T(8,128)(2,1)} %get-tuple-element.57), channel_id=1, source_target_pairs={{0,4},{1,5},{2,6},{3,7},{4,0},{5,1},{6,2},{7,3},{8,12},{9,13},{10,... | collective-permute-start | bytes 294920 | tf_op jit(solution)/shard_map/ppermute | solution.py:400
  37.7 0.1 collective-permute-start.7
  37.8 0.0 collective-permute-done.3.refs_1_
  37.8 2.5 %collective-permute-start.8 = (bf16[128,384]{1,0:T(8,128)(2,1)}, bf16[128,384]{1,0:T(8,128)(2,1)}, u32[]{:S(2)}, u32[]{:S(2)}) collective-permute-start(bf16[128,384]{1,0:T(8,128)(2,1)} %get-tuple-element.59), channel_id=1, source_target_pairs={{0,6},{1,7},{2,4},{3,5},{4,2},{5,3},{6,0},{7,1},{8,14},{9,15},{10,... | collective-permute-start | bytes 294920 | tf_op jit(solution)/shard_map/ppermute | solution.py:400
  40.4 5.2 %collective-permute-done.4.refs_2_ = bf16[128,384]{1,0:T(8,128)(2,1)} collective-permute-done((bf16[128,384]{1,0:T(8,128)(2,1)}, bf16[128,384]{1,0:T(8,128)(2,1)}, u32[]{:S(2)}, u32[]{:S(2)}) %collective-permute-start.4) | collective-permute-done | bytes 98336 | tf_op jit(solution)/shard_map/ppermute | solution.py:400
  45.6 0.0 collective-permute-start.9
  45.6 5.1 %gates.1.refs_3_ = bf16[512,1024]{1,0:T(8,128)(2,1)} custom-call(bf16[512,1024]{1,0:T(8,128)(2,1)} %refs_4_.1, bf16[1024,2048]{1,0:T(8,128)(2,1)} %w_in.5), custom_call_target="tpu_custom_call" | custom-call | flops 1073741824 | bytes 4194304 | tf_op jit(solution)/shard_map/gates/pallas_call | solution.py:377
  50.7 0.0 collective-permute-done.5.refs_3_
  50.8 0.0 collective-permute-done.6.refs_4_
  50.8 3.3 %collective-permute-done.8.refs_6_ = bf16[128,384]{1,0:T(8,128)(2,1)} collective-permute-done((bf16[128,384]{1,0:T(8,128)(2,1)}, bf16[128,384]{1,0:T(8,128)(2,1)}, u32[]{:S(2)}, u32[]{:S(2)}) %collective-permute-start.8) | collective-permute-done | bytes 98336 | tf_op jit(solution)/shard_map/ppermute | solution.py:400
  54.0 1.2 collective-permute-done.9.refs_7_
  55.2 5.0 %attend_apart.1 = (bf16[256,384]{1,0:T(8,128)(2,1)}, bf16[256,384]{1,0:T(8,128)(2,1)}, bf16[256,384]{1,0:T(8,128)(2,1)}, bf16[256,384]{1,0:T(8,128)(2,1)}) custom-call(s32[1]{0:T(128)S(6)} %copy.9.blocks, bf16[128,384]{1,0:T(8,128)(2,1)} %get-tuple-element.53.refs_0_, bf16[128,384]{1,0:T(8,128)(2,1)} %collective-permute-done.3.refs_1_, ...), custom_call_target="tpu_custom_call" | custom-call | flops 3221225472 | bytes 3145728 | tf_op jit(solution)/shard_map/attend_apart/pallas_call | solution.py:275
  60.2 3.4 %collective-permute-start.10 = (bf16[256,384]{1,0:T(8,128)(2,1)}, bf16[256,384]{1,0:T(8,128)(2,1)}, u32[]{:S(2)}, u32[]{:S(2)}) collective-permute-start(bf16[256,384]{1,0:T(8,128)(2,1)} %get-tuple-element.64), channel_id=1, source_target_pairs={{0,8},{1,9},{2,10},{3,11},{4,12},{5,13},{6,14},{7,15},{8,0},{9,1},... | collective-permute-start | bytes 589832 | tf_op jit(solution)/shard_map/ppermute | solution.py:400
  63.6 2.1 %collective-permute-start.11 = (bf16[256,384]{1,0:T(8,128)(2,1)}, bf16[256,384]{1,0:T(8,128)(2,1)}, u32[]{:S(2)}, u32[]{:S(2)}) collective-permute-start(bf16[256,384]{1,0:T(8,128)(2,1)} %get-tuple-element.65), channel_id=1, source_target_pairs={{0,16},{1,17},{2,18},{3,19},{4,20},{5,21},{6,22},{7,23},{8,24},{9,... | collective-permute-start | bytes 589832 | tf_op jit(solution)/shard_map/ppermute | solution.py:400
  65.7 0.3 collective-permute-start.12
  66.1 6.9 %attend.1 = bf16[1024,640]{1,0:T(8,128)(2,1)} custom-call(s32[1]{0:T(128)S(6)} %copy.9.blocks, bf16[1024,640]{1,0:T(8,128)(2,1)} %bitcast.4.queries, bf16[1024,1024]{1,0:T(8,128)(2,1)} %bitcast.14, bf16[1024,1024]{1,0:T(8,128)(2,1)} %bitcast.16), custom_call_target="tpu_custom_call" | custom-call | flops 5368709120 | bytes 6291456 | tf_op jit(solution)/shard_map/attend/pallas_call | solution.py:228
  72.9 0.0 collective-permute-done.10.refs_1_
  72.9 8.2 %collective-permute-done.11.refs_2_ = bf16[256,384]{1,0:T(8,128)(2,1)} collective-permute-done((bf16[256,384]{1,0:T(8,128)(2,1)}, bf16[256,384]{1,0:T(8,128)(2,1)}, u32[]{:S(2)}, u32[]{:S(2)}) %collective-permute-start.11) | collective-permute-done | bytes 196640 | tf_op jit(solution)/shard_map/ppermute | solution.py:400
  81.1 0.0 collective-permute-done.12.refs_3_
  81.1 4.3 %all-to-all-start.1 = ((bf16[32,32,640]{2,1,0:T(8,128)(2,1)}), bf16[32,32,640]{2,1,0:T(8,128)(2,1)}, u32[]{:S(2)}, u32[]{:S(2)}) async-start(bf16[32,32,640]{2,1,0:T(8,128)(2,1)} %bitcast.10), calls=%async_computation.1 | async-start | bytes 2621440 | tf_op jit(solution)/shard_map/all_to_all | solution.py:407
  85.4 2.1 %regroup.3 = (bf16[128,384]{1,0:T(8,128)(2,1)}, bf16[128,384]{1,0:T(8,128)(2,1)}, bf16[128,384]{1,0:T(8,128)(2,1)}, bf16[128,384]{1,0:T(8,128)(2,1)}, bf16[128,3...) custom-call(bf16[256,384]{1,0:T(8,128)(2,1)} %get-tuple-element.68.refs_0_, ...), custom_call_target="tpu_custom_call" | custom-call | bytes 1572864 | tf_op jit(solution)/shard_map/regroup/pallas_call | solution.py:191
  87.6 0.2 collective-permute-start.13
  87.8 1.7 %collective-permute-start.14 = (bf16[128,384]{1,0:T(8,128)(2,1)}, bf16[128,384]{1,0:T(8,128)(2,1)}, u32[]{:S(2)}, u32[]{:S(2)}) collective-permute-start(bf16[128,384]{1,0:T(8,128)(2,1)} %get-tuple-element.74), channel_id=1, source_target_pairs={{0,2},{1,3},{2,0},{3,1},{4,6},{5,7},{6,4},{7,5},{8,10},{9,11},{10,... | collective-permute-start | bytes 294920 | tf_op jit(solution)/shard_map/ppermute | solution.py:400
  89.5 0.0 collective-permute-start.15
  89.5 1.7 %collective-permute-start.16 = (bf16[128,384]{1,0:T(8,128)(2,1)}, bf16[128,384]{1,0:T(8,128)(2,1)}, u32[]{:S(2)}, u32[]{:S(2)}) collective-permute-start(bf16[128,384]{1,0:T(8,128)(2,1)} %get-tuple-element.76), channel_id=1, source_target_pairs={{0,4},{1,5},{2,6},{3,7},{4,0},{5,1},{6,2},{7,3},{8,12},{9,13},{10,... | collective-permute-start | bytes 294920 | tf_op jit(solution)/shard_map/ppermute | solution.py:400
  91.2 0.1 collective-permute-start.17
  91.3 0.0 collective-permute-done.13.refs_1_
  91.3 2.6 %collective-permute-start.18 = (bf16[128,384]{1,0:T(8,128)(2,1)}, bf16[128,384]{1,0:T(8,128)(2,1)}, u32[]{:S(2)}, u32[]{:S(2)}) collective-permute-start(bf16[128,384]{1,0:T(8,128)(2,1)} %get-tuple-element.78), channel_id=1, source_target_pairs={{0,6},{1,7},{2,4},{3,5},{4,2},{5,3},{6,0},{7,1},{8,14},{9,15},{10,... | collective-permute-start | bytes 294920 | tf_op jit(solution)/shard_map/ppermute | solution.py:400
  93.9 5.9 %collective-permute-done.14.refs_2_ = bf16[128,384]{1,0:T(8,128)(2,1)} collective-permute-done((bf16[128,384]{1,0:T(8,128)(2,1)}, bf16[128,384]{1,0:T(8,128)(2,1)}, u32[]{:S(2)}, u32[]{:S(2)}) %collective-permute-start.14) | collective-permute-done | bytes 98336 | tf_op jit(solution)/shard_map/ppermute | solution.py:400
  99.8 3.2 %collective-permute-done.15.refs_3_ = bf16[128,384]{1,0:T(8,128)(2,1)} collective-permute-done((bf16[128,384]{1,0:T(8,128)(2,1)}, bf16[128,384]{1,0:T(8,128)(2,1)}, u32[]{:S(2)}, u32[]{:S(2)}) %collective-permute-start.15) | collective-permute-done | bytes 98336 | tf_op jit(solution)/shard_map/ppermute | solution.py:400
  103.0 0.0 collective-permute-done.16.refs_4_
  103.0 5.2 %collective-permute-done.18.refs_6_ = bf16[128,384]{1,0:T(8,128)(2,1)} collective-permute-done((bf16[128,384]{1,0:T(8,128)(2,1)}, bf16[128,384]{1,0:T(8,128)(2,1)}, u32[]{:S(2)}, u32[]{:S(2)}) %collective-permute-start.18) | collective-permute-done | bytes 98336 | tf_op jit(solution)/shard_map/ppermute | solution.py:400
  108.2 1.2 collective-permute-done.19.refs_7_
  109.4 3.0 %collect.1.refs_2_ = bf16[512,384]{1,0:T(8,128)(2,1)} custom-call(s32[2,512]{1,0:T(2,128)} %get-tuple-element.43.slots.refs_0_, bf16[128,384]{1,0:T(8,128)(2,1)} %get-tuple-element.72.refs_0_, bf16[128,384]{1,0:T(8,128)(2,1)} %collective-permute-done.13.refs_1_, bf16[128,384]{1,0:T(8,128)(2,1)} %collective-permute-done.14.refs_2_, ...), custom_call_target="tpu_custom_call" | custom-call | flops 402653184 | bytes 2097152 | tf_op jit(solution)/shard_map/collect/pallas_call | solution.py:308
  112.4 5.3 %all-to-all-done.1 = bf16[32,32,640]{2,1,0:T(8,128)(2,1)} async-done(((bf16[32,32,640]{2,1,0:T(8,128)(2,1)}), bf16[32,32,640]{2,1,0:T(8,128)(2,1)}, u32[]{:S(2)}, u32[]{:S(2)}) %all-to-all-start.1) | async-done | bytes 1310752 | tf_op jit(solution)/shard_map/all_to_all | solution.py:407
  117.7 5.0 %finish.1 = bf16[512,1024]{1,0:T(8,128)(2,1)} custom-call(s32[2,512]{1,0:T(2,128)} %get-tuple-element.43.slots.refs_0_, bf16[1024,640]{1,0:T(8,128)(2,1)} %bitcast.8.refs_1_, bf16[512,384]{1,0:T(8,128)(2,1)} %collect.1.refs_2_, bf16[512,1024]{1,0:T(8,128)(2,1)} %gates.1.refs_3_, bf16[512,1024]{1,0:T(8,128)(2,1)} %refs_4_.1, bf16[1024,1024]{1,0:T(8,128)(2,1)} %refs_5_.1), custom_call_target="tpu_custom_call" | custom-call | flops 2147483648 | bytes 7340032 | tf_op jit(solution)/shard_map/finish/pallas_call | solution.py:348
  (5 shorter events, 0.0 us)
Async XLA Ops:
  4.0 11.8 %collective-permute-start = (bf16[256,384]{1,0:T(8,128)(2,1)}, bf16[256,384]{1,0:T(8,128)(2,1)}, u32[]{:S(2)}, u32[]{:S(2)}) collective-permute-start(bf16[256,384]{1,0:T(8,128)(2,1)} %get-tuple-element.45), channel_id=1, source_target_pairs={{0,8},{1,9},{2,10},{3,11},{4,12},{5,13},{6,14},{7,15},{8,0},{9,1},... | collective-permute-start | bytes 589832 | tf_op jit(solution)/shard_map/ppermute | solution.py:400
  7.1 17.5 %collective-permute-start.1 = (bf16[256,384]{1,0:T(8,128)(2,1)}, bf16[256,384]{1,0:T(8,128)(2,1)}, u32[]{:S(2)}, u32[]{:S(2)}) collective-permute-start(bf16[256,384]{1,0:T(8,128)(2,1)} %get-tuple-element.46), channel_id=1, source_target_pairs={{0,16},{1,17},{2,18},{3,19},{4,20},{5,21},{6,22},{7,23},{8,24},{9,... | collective-permute-start | bytes 589832 | tf_op jit(solution)/shard_map/ppermute | solution.py:400
  9.7 14.9 %collective-permute-start.2 = (bf16[256,384]{1,0:T(8,128)(2,1)}, bf16[256,384]{1,0:T(8,128)(2,1)}, u32[]{:S(2)}, u32[]{:S(2)}) collective-permute-start(bf16[256,384]{1,0:T(8,128)(2,1)} %get-tuple-element.47), channel_id=1, source_target_pairs={{0,24},{1,25},{2,26},{3,27},{4,28},{5,29},{6,30},{7,31},{8,16},{9,... | collective-permute-start | bytes 589832 | tf_op jit(solution)/shard_map/ppermute | solution.py:400
  24.5 41.5 %all-to-all-start = ((bf16[32,32,640]{2,1,0:T(8,128)(2,1)}), bf16[32,32,640]{2,1,0:T(8,128)(2,1)}, u32[]{:S(2)}, u32[]{:S(2)}) async-start(bf16[32,32,640]{2,1,0:T(8,128)(2,1)} %bitcast.9), calls=%async_computation | async-start | bytes 2621440 | tf_op jit(solution)/shard_map/all_to_all | solution.py:407
  33.6 4.3 %collective-permute-start.3 = (bf16[128,384]{1,0:T(8,128)(2,1)}, bf16[128,384]{1,0:T(8,128)(2,1)}, u32[]{:S(2)}, u32[]{:S(2)}) collective-permute-start(bf16[128,384]{1,0:T(8,128)(2,1)} %get-tuple-element.54), channel_id=1, source_target_pairs={{0,1},{1,0},{2,3},{3,2},{4,5},{5,4},{6,7},{7,6},{8,9},{9,8},{10,11... | collective-permute-start | bytes 294920 | tf_op jit(solution)/shard_map/ppermute | solution.py:400
  33.6 12.0 %collective-permute-start.4 = (bf16[128,384]{1,0:T(8,128)(2,1)}, bf16[128,384]{1,0:T(8,128)(2,1)}, u32[]{:S(2)}, u32[]{:S(2)}) collective-permute-start(bf16[128,384]{1,0:T(8,128)(2,1)} %get-tuple-element.55), channel_id=1, source_target_pairs={{0,2},{1,3},{2,0},{3,1},{4,6},{5,7},{6,4},{7,5},{8,10},{9,11},{10,... | collective-permute-start | bytes 294920 | tf_op jit(solution)/shard_map/ppermute | solution.py:400
  35.9 14.8 %collective-permute-start.5 = (bf16[128,384]{1,0:T(8,128)(2,1)}, bf16[128,384]{1,0:T(8,128)(2,1)}, u32[]{:S(2)}, u32[]{:S(2)}) collective-permute-start(bf16[128,384]{1,0:T(8,128)(2,1)} %get-tuple-element.56), channel_id=1, source_target_pairs={{0,3},{1,2},{2,1},{3,0},{4,7},{5,6},{6,5},{7,4},{8,11},{9,10},{10,... | collective-permute-start | bytes 294920 | tf_op jit(solution)/shard_map/ppermute | solution.py:400
  36.2 14.6 %collective-permute-start.6 = (bf16[128,384]{1,0:T(8,128)(2,1)}, bf16[128,384]{1,0:T(8,128)(2,1)}, u32[]{:S(2)}, u32[]{:S(2)}) collective-permute-start(bf16[128,384]{1,0:T(8,128)(2,1)} %get-tuple-element.57), channel_id=1, source_target_pairs={{0,4},{1,5},{2,6},{3,7},{4,0},{5,1},{6,2},{7,3},{8,12},{9,13},{10,... | collective-permute-start | bytes 294920 | tf_op jit(solution)/shard_map/ppermute | solution.py:400
  37.7 13.1 %collective-permute-start.7 = (bf16[128,384]{1,0:T(8,128)(2,1)}, bf16[128,384]{1,0:T(8,128)(2,1)}, u32[]{:S(2)}, u32[]{:S(2)}) collective-permute-start(bf16[128,384]{1,0:T(8,128)(2,1)} %get-tuple-element.58), channel_id=1, source_target_pairs={{0,5},{1,4},{2,7},{3,6},{4,1},{5,0},{6,3},{7,2},{8,13},{9,12},{10,... | collective-permute-start | bytes 294920 | tf_op jit(solution)/shard_map/ppermute | solution.py:400
  37.8 16.2 %collective-permute-start.8 = (bf16[128,384]{1,0:T(8,128)(2,1)}, bf16[128,384]{1,0:T(8,128)(2,1)}, u32[]{:S(2)}, u32[]{:S(2)}) collective-permute-start(bf16[128,384]{1,0:T(8,128)(2,1)} %get-tuple-element.59), channel_id=1, source_target_pairs={{0,6},{1,7},{2,4},{3,5},{4,2},{5,3},{6,0},{7,1},{8,14},{9,15},{10,... | collective-permute-start | bytes 294920 | tf_op jit(solution)/shard_map/ppermute | solution.py:400
  45.6 9.6 %collective-permute-start.9 = (bf16[128,384]{1,0:T(8,128)(2,1)}, bf16[128,384]{1,0:T(8,128)(2,1)}, u32[]{:S(2)}, u32[]{:S(2)}) collective-permute-start(bf16[128,384]{1,0:T(8,128)(2,1)} %get-tuple-element.60), channel_id=1, source_target_pairs={{0,7},{1,6},{2,5},{3,4},{4,3},{5,2},{6,1},{7,0},{8,15},{9,14},{10,... | collective-permute-start | bytes 294920 | tf_op jit(solution)/shard_map/ppermute | solution.py:400
  60.2 12.7 %collective-permute-start.10 = (bf16[256,384]{1,0:T(8,128)(2,1)}, bf16[256,384]{1,0:T(8,128)(2,1)}, u32[]{:S(2)}, u32[]{:S(2)}) collective-permute-start(bf16[256,384]{1,0:T(8,128)(2,1)} %get-tuple-element.64), channel_id=1, source_target_pairs={{0,8},{1,9},{2,10},{3,11},{4,12},{5,13},{6,14},{7,15},{8,0},{9,1},... | collective-permute-start | bytes 589832 | tf_op jit(solution)/shard_map/ppermute | solution.py:400
  63.6 17.5 %collective-permute-start.11 = (bf16[256,384]{1,0:T(8,128)(2,1)}, bf16[256,384]{1,0:T(8,128)(2,1)}, u32[]{:S(2)}, u32[]{:S(2)}) collective-permute-start(bf16[256,384]{1,0:T(8,128)(2,1)} %get-tuple-element.65), channel_id=1, source_target_pairs={{0,16},{1,17},{2,18},{3,19},{4,20},{5,21},{6,22},{7,23},{8,24},{9,... | collective-permute-start | bytes 589832 | tf_op jit(solution)/shard_map/ppermute | solution.py:400
  65.7 15.4 %collective-permute-start.12 = (bf16[256,384]{1,0:T(8,128)(2,1)}, bf16[256,384]{1,0:T(8,128)(2,1)}, u32[]{:S(2)}, u32[]{:S(2)}) collective-permute-start(bf16[256,384]{1,0:T(8,128)(2,1)} %get-tuple-element.66), channel_id=1, source_target_pairs={{0,24},{1,25},{2,26},{3,27},{4,28},{5,29},{6,30},{7,31},{8,16},{9,... | collective-permute-start | bytes 589832 | tf_op jit(solution)/shard_map/ppermute | solution.py:400
  81.1 36.6 %all-to-all-start.1 = ((bf16[32,32,640]{2,1,0:T(8,128)(2,1)}), bf16[32,32,640]{2,1,0:T(8,128)(2,1)}, u32[]{:S(2)}, u32[]{:S(2)}) async-start(bf16[32,32,640]{2,1,0:T(8,128)(2,1)} %bitcast.10), calls=%async_computation.1 | async-start | bytes 2621440 | tf_op jit(solution)/shard_map/all_to_all | solution.py:407
  87.6 3.7 %collective-permute-start.13 = (bf16[128,384]{1,0:T(8,128)(2,1)}, bf16[128,384]{1,0:T(8,128)(2,1)}, u32[]{:S(2)}, u32[]{:S(2)}) collective-permute-start(bf16[128,384]{1,0:T(8,128)(2,1)} %get-tuple-element.73), channel_id=1, source_target_pairs={{0,1},{1,0},{2,3},{3,2},{4,5},{5,4},{6,7},{7,6},{8,9},{9,8},{10,11... | collective-permute-start | bytes 294920 | tf_op jit(solution)/shard_map/ppermute | solution.py:400
  87.8 12.0 %collective-permute-start.14 = (bf16[128,384]{1,0:T(8,128)(2,1)}, bf16[128,384]{1,0:T(8,128)(2,1)}, u32[]{:S(2)}, u32[]{:S(2)}) collective-permute-start(bf16[128,384]{1,0:T(8,128)(2,1)} %get-tuple-element.74), channel_id=1, source_target_pairs={{0,2},{1,3},{2,0},{3,1},{4,6},{5,7},{6,4},{7,5},{8,10},{9,11},{10,... | collective-permute-start | bytes 294920 | tf_op jit(solution)/shard_map/ppermute | solution.py:400
  89.5 13.5 %collective-permute-start.15 = (bf16[128,384]{1,0:T(8,128)(2,1)}, bf16[128,384]{1,0:T(8,128)(2,1)}, u32[]{:S(2)}, u32[]{:S(2)}) collective-permute-start(bf16[128,384]{1,0:T(8,128)(2,1)} %get-tuple-element.75), channel_id=1, source_target_pairs={{0,3},{1,2},{2,1},{3,0},{4,7},{5,6},{6,5},{7,4},{8,11},{9,10},{10,... | collective-permute-start | bytes 294920 | tf_op jit(solution)/shard_map/ppermute | solution.py:400
  89.5 13.5 %collective-permute-start.16 = (bf16[128,384]{1,0:T(8,128)(2,1)}, bf16[128,384]{1,0:T(8,128)(2,1)}, u32[]{:S(2)}, u32[]{:S(2)}) collective-permute-start(bf16[128,384]{1,0:T(8,128)(2,1)} %get-tuple-element.76), channel_id=1, source_target_pairs={{0,4},{1,5},{2,6},{3,7},{4,0},{5,1},{6,2},{7,3},{8,12},{9,13},{10,... | collective-permute-start | bytes 294920 | tf_op jit(solution)/shard_map/ppermute | solution.py:400
  91.2 11.9 %collective-permute-start.17 = (bf16[128,384]{1,0:T(8,128)(2,1)}, bf16[128,384]{1,0:T(8,128)(2,1)}, u32[]{:S(2)}, u32[]{:S(2)}) collective-permute-start(bf16[128,384]{1,0:T(8,128)(2,1)} %get-tuple-element.77), channel_id=1, source_target_pairs={{0,5},{1,4},{2,7},{3,6},{4,1},{5,0},{6,3},{7,2},{8,13},{9,12},{10,... | collective-permute-start | bytes 294920 | tf_op jit(solution)/shard_map/ppermute | solution.py:400
  91.3 16.9 %collective-permute-start.18 = (bf16[128,384]{1,0:T(8,128)(2,1)}, bf16[128,384]{1,0:T(8,128)(2,1)}, u32[]{:S(2)}, u32[]{:S(2)}) collective-permute-start(bf16[128,384]{1,0:T(8,128)(2,1)} %get-tuple-element.78), channel_id=1, source_target_pairs={{0,6},{1,7},{2,4},{3,5},{4,2},{5,3},{6,0},{7,1},{8,14},{9,15},{10,... | collective-permute-start | bytes 294920 | tf_op jit(solution)/shard_map/ppermute | solution.py:400
  99.8 9.6 %collective-permute-start.19 = (bf16[128,384]{1,0:T(8,128)(2,1)}, bf16[128,384]{1,0:T(8,128)(2,1)}, u32[]{:S(2)}, u32[]{:S(2)}) collective-permute-start(bf16[128,384]{1,0:T(8,128)(2,1)} %get-tuple-element.79), channel_id=1, source_target_pairs={{0,7},{1,6},{2,5},{3,4},{4,3},{5,2},{6,1},{7,0},{8,15},{9,14},{10,... | collective-permute-start | bytes 294920 | tf_op jit(solution)/shard_map/ppermute | solution.py:400

commit v4 on v3

--- a/solution.py
+++ b/solution.py
@@ -63,7 +63,7 @@
     rank = dot(owner_hot.astype(BF16), before)
     owner = iota((devices, 128), 0)
     offset = owner ^ place
-    group, member = offset // MEMBERS, offset % MEMBERS
+    group, member = (groups - offset // MEMBERS) % groups, offset % MEMBERS
 
     def pick(block):
         start = (block * capacity)[:, 0:1].astype(F32)
@@ -395,28 +395,31 @@
     place = lax.axis_index("dev").astype(jnp.int32).reshape(1)
     keys, values = cache_keys[0], cache_values[0]
 
-    def swap(arrays, stride):
+    def swap(arrays, offsets):
         return arrays[:1] + [
-            lax.ppermute(array, "dev", [(d, d ^ (index * stride)) for d in range(devices)])
-            for index, array in enumerate(arrays)
-            if index
+            lax.ppermute(array, "dev", [(d, d ^ offset) for d in range(devices)])
+            for array, offset in zip(arrays[1:], offsets[1:])
         ]
+
+    across = [(groups - index) % groups * MEMBERS for index in range(groups)]
+    within = list(range(MEMBERS))
 
     def exchange(rows):
         blocks = rows.reshape(devices, capacity, rows.shape[1])
         return lax.all_to_all(blocks, "dev", split_axis=0, concat_axis=0, tiled=True).reshape(rows.shape)
 
     apart, slots = prepare(place, items, cand_user, owner_map, w_in, capacity, part)
-    outgoing, apart = lax.optimization_barrier((rest(items, slots, w_in, devices * capacity, part), swap(apart, MEMBERS)))
+    outgoing, gate, apart = lax.optimization_barrier(
+        (rest(items, slots, w_in, devices * capacity, part), gates(items, w_in), swap(apart, across))
+    )
     arrived = exchange(outgoing)
-    gate = gates(items, w_in)
-    apart = swap(list(regroup(apart, MEMBERS)), 1)
+    apart = swap(list(regroup(apart, MEMBERS)), within)
     apart = list(attend_apart(hist_blocks, apart, keys, values, groups))
     arrived, gate, apart[0] = lax.optimization_barrier((arrived, gate, apart[0]))
     attended = attend(hist_blocks, arrived, keys, values, APART)
-    outgoing, apart = lax.optimization_barrier((attended, swap(apart, MEMBERS)))
+    outgoing, apart = lax.optimization_barrier((attended, swap(apart, across)))
     returned = exchange(outgoing)
-    apart = swap(list(regroup(apart, MEMBERS)), 1)
+    apart = swap(list(regroup(apart, MEMBERS)), within)
     return finish(slots, returned, collect(slots, apart), gate, items, w_out)
 
 

time: 124 us -> 124 us (level)
  starting transfers between devices: 35.2 us -> 32 us
  Pallas kernels: 38.8 us -> 40.9 us
  waiting for transfers between devices: 47.9 us -> 49.3 us
    all_to_all x2, starting transfers between devices: 11.2 us -> 8.42 us  [exchange(): lax.all_to_all(blocks, 'dev', split_axis=0, concat_axis=0, tiled=True)]
    ppermute x20, waiting for transfers between devices: 42.7 us -> 44.3 us  [swap(): lax.ppermute(array, 'dev', [(d, d ^ offset) for d in range(devices)])]
    pallas_call x1, Pallas kernels: 6.87 us -> 8.15 us  [attend(): pl.pallas_call(attend_kernel, grid_spec=pltpu.PrefetchScalarGridSpec(num_...]
  transfers between devices with their start and end apart: 22 -> 22, of which waited for: 11 -> 11; matrix products, arithmetic and copies ran while one was open for 0% -> 0% of each run, Pallas kernels for 24% -> 26%
where the time goes in v4:
time: 124 us; the launch traced here: 123 us
  waiting for transfers between devices  49.3 us (40%)
  Pallas kernels  40.9 us (33%)
  starting transfers between devices  32 us (26%)
    ppermute x20, waiting for transfers between devices, swap(): lax.ppermute(array, 'dev', [(d, d ^ offset) for d in range(devices)])  44.3 us
    ppermute x20, starting transfers between devices, swap(): lax.ppermute(array, 'dev', [(d, d ^ offset) for d in range(devices)])  23.6 us
    all_to_all x2, starting transfers between devices, exchange(): lax.all_to_all(blocks, 'dev', split_axis=0, concat_axis=0, tiled=True)  8.42 us
    pallas_call x1, Pallas kernels, attend(): pl.pallas_call(attend_kernel, grid_spec=pltpu.PrefetchScalarGridSpec(num_...  8.15 us
    pallas_call x1, Pallas kernels, attend_apart(): pl.pallas_call(functools.partial(attend_apart_kernel, members), grid_spec...  5.8 us
    pallas_call x1, Pallas kernels, rest(): pl.pallas_call(rest_kernel, in_specs=[inside, inside, pl.BlockSpec(memory...  5.58 us
    pallas_call x1, Pallas kernels, gates(): pl.pallas_call(gate_kernel, in_specs=[inside, pl.BlockSpec(memory_space=p...  5.13 us
    pallas_call x1, Pallas kernels, finish(): pl.pallas_call(finish_kernel, in_specs=[anywhere] * 6, out_specs=anywhere...  5.02 us
  transfers between devices with their start and end apart: 22, of which 11 were waited for; matrix products, arithmetic and copies ran while one was open for 0% of the time, Pallas kernels for 26%

profile of v4, /device:TPU:0, one launch (start us, length us, event | category | flops | bytes accessed | tf_op | source)
XLA Modules:
  0.0 123.1 jit_solution(8061842041709612404)
XLA Ops:
  0.0 4.0 %prepare.1 = (bf16[256,384]{1,0:T(8,128)(2,1)}, bf16[256,384]{1,0:T(8,128)(2,1)}, bf16[256,384]{1,0:T(8,128)(2,1)}, bf16[256,384]{1,0:T(8,128)(2,1)}, s32[2,512]{1,0:T(2,128)}) custom-call(s32[1]{0:T(128)} %bitcast.place, bf16[512,1024]{1,0:T(8,128)(2,1)} %refs_4_.1, s32[1,512]{1,0:T(1,128)} %bitcast.11, s32[1,32]{1,0:T(1,128)} %bitcast.12, ...), custom_call_target="tpu_custom_call" | custom-call | flops 805306368 | bytes 4194304 | tf_op jit(solution)/shard_map/prepare/pallas_call | solution.py:126
  4.0 5.1 %collective-permute-start = (bf16[256,384]{1,0:T(8,128)(2,1)}, bf16[256,384]{1,0:T(8,128)(2,1)}, u32[]{:S(2)}, u32[]{:S(2)}) collective-permute-start(bf16[256,384]{1,0:T(8,128)(2,1)} %get-tuple-element.46), channel_id=1, source_target_pairs={{0,24},{1,25},{2,26},{3,27},{4,28},{5,29},{6,30},{7,31},{8,16},{9,... | collective-permute-start | bytes 589832 | tf_op jit(solution)/shard_map/ppermute | solution.py:400
  9.1 0.6 collective-permute-start.2
  9.7 5.1 %gates.1.refs_3_ = bf16[512,1024]{1,0:T(8,128)(2,1)} custom-call(bf16[512,1024]{1,0:T(8,128)(2,1)} %refs_4_.1, bf16[1024,2048]{1,0:T(8,128)(2,1)} %w_in.5), custom_call_target="tpu_custom_call" | custom-call | flops 1073741824 | bytes 4194304 | tf_op jit(solution)/shard_map/gates/pallas_call | solution.py:377
  14.9 5.6 %rest.1 = bf16[1024,640]{1,0:T(8,128)(2,1)} custom-call(bf16[512,1024]{1,0:T(8,128)(2,1)} %refs_4_.1, s32[2,512]{1,0:T(2,128)} %get-tuple-element.44.slots.refs_0_, bf16[1024,2048]{1,0:T(8,128)(2,1)} %w_in.5), custom_call_target="tpu_custom_call" | custom-call | flops 1342177280 | bytes 7340032 | tf_op jit(solution)/shard_map/rest/pallas_call | solution.py:167
  20.5 0.0 collective-permute-done.refs_1_
  20.5 5.6 %collective-permute-done.1.refs_2_ = bf16[256,384]{1,0:T(8,128)(2,1)} collective-permute-done((bf16[256,384]{1,0:T(8,128)(2,1)}, bf16[256,384]{1,0:T(8,128)(2,1)}, u32[]{:S(2)}, u32[]{:S(2)}) %collective-permute-start.1) | collective-permute-done | bytes 196640 | tf_op jit(solution)/shard_map/ppermute | solution.py:400
  26.1 5.0 %all-to-all-start = ((bf16[32,32,640]{2,1,0:T(8,128)(2,1)}), bf16[32,32,640]{2,1,0:T(8,128)(2,1)}, u32[]{:S(2)}, u32[]{:S(2)}) async-start(bf16[32,32,640]{2,1,0:T(8,128)(2,1)} %bitcast.9), calls=%async_computation | async-start | bytes 2621440 | tf_op jit(solution)/shard_map/all_to_all | solution.py:409
  31.1 2.1 %regroup.2 = (bf16[128,384]{1,0:T(8,128)(2,1)}, bf16[128,384]{1,0:T(8,128)(2,1)}, bf16[128,384]{1,0:T(8,128)(2,1)}, bf16[128,384]{1,0:T(8,128)(2,1)}, bf16[128,3...) custom-call(bf16[256,384]{1,0:T(8,128)(2,1)} %get-tuple-element.51.refs_0_, ...), custom_call_target="tpu_custom_call" | custom-call | bytes 1572864 | tf_op jit(solution)/shard_map/regroup/pallas_call | solution.py:191
  33.3 0.0 collective-permute-start.3
  33.3 1.7 %collective-permute-start.4 = (bf16[128,384]{1,0:T(8,128)(2,1)}, bf16[128,384]{1,0:T(8,128)(2,1)}, u32[]{:S(2)}, u32[]{:S(2)}) collective-permute-start(bf16[128,384]{1,0:T(8,128)(2,1)} %get-tuple-element.57), channel_id=1, source_target_pairs={{0,2},{1,3},{2,0},{3,1},{4,6},{5,7},{6,4},{7,5},{8,10},{9,11},{10,... | collective-permute-start | bytes 294920 | tf_op jit(solution)/shard_map/ppermute | solution.py:400
  35.0 0.2 collective-permute-start.5
  35.1 1.5 %collective-permute-start.6 = (bf16[128,384]{1,0:T(8,128)(2,1)}, bf16[128,384]{1,0:T(8,128)(2,1)}, u32[]{:S(2)}, u32[]{:S(2)}) collective-permute-start(bf16[128,384]{1,0:T(8,128)(2,1)} %get-tuple-element.59), channel_id=1, source_target_pairs={{0,4},{1,5},{2,6},{3,7},{4,0},{5,1},{6,2},{7,3},{8,12},{9,13},{10,... | collective-permute-start | bytes 294920 | tf_op jit(solution)/shard_map/ppermute | solution.py:400
  36.7 0.2 collective-permute-start.7
  36.8 2.5 %collective-permute-start.8 = (bf16[128,384]{1,0:T(8,128)(2,1)}, bf16[128,384]{1,0:T(8,128)(2,1)}, u32[]{:S(2)}, u32[]{:S(2)}) collective-permute-start(bf16[128,384]{1,0:T(8,128)(2,1)} %get-tuple-element.61), channel_id=1, source_target_pairs={{0,6},{1,7},{2,4},{3,5},{4,2},{5,3},{6,0},{7,1},{8,14},{9,15},{10,... | collective-permute-start | bytes 294920 | tf_op jit(solution)/shard_map/ppermute | solution.py:400
  39.4 5.9 %collective-permute-done.4.refs_2_ = bf16[128,384]{1,0:T(8,128)(2,1)} collective-permute-done((bf16[128,384]{1,0:T(8,128)(2,1)}, bf16[128,384]{1,0:T(8,128)(2,1)}, u32[]{:S(2)}, u32[]{:S(2)}) %collective-permute-start.4) | collective-permute-done | bytes 98336 | tf_op jit(solution)/shard_map/ppermute | solution.py:400
  45.3 0.0 collective-permute-start.9
  45.9 2.6 %collective-permute-done.5.refs_3_ = bf16[128,384]{1,0:T(8,128)(2,1)} collective-permute-done((bf16[128,384]{1,0:T(8,128)(2,1)}, bf16[128,384]{1,0:T(8,128)(2,1)}, u32[]{:S(2)}, u32[]{:S(2)}) %collective-permute-start.5) | collective-permute-done | bytes 98336 | tf_op jit(solution)/shard_map/ppermute | solution.py:400
  48.5 0.0 collective-permute-done.6.refs_4_
  48.5 0.0 collective-permute-done.7.refs_5_
  48.5 5.2 %collective-permute-done.8.refs_6_ = bf16[128,384]{1,0:T(8,128)(2,1)} collective-permute-done((bf16[128,384]{1,0:T(8,128)(2,1)}, bf16[128,384]{1,0:T(8,128)(2,1)}, u32[]{:S(2)}, u32[]{:S(2)}) %collective-permute-start.8) | collective-permute-done | bytes 98336 | tf_op jit(solution)/shard_map/ppermute | solution.py:400
  53.7 1.2 collective-permute-done.9.refs_7_
  54.9 5.8 %attend_apart.1 = (bf16[256,384]{1,0:T(8,128)(2,1)}, bf16[256,384]{1,0:T(8,128)(2,1)}, bf16[256,384]{1,0:T(8,128)(2,1)}, bf16[256,384]{1,0:T(8,128)(2,1)}) custom-call(s32[1]{0:T(128)S(6)} %copy.9.blocks, bf16[128,384]{1,0:T(8,128)(2,1)} %get-tuple-element.55.refs_0_, bf16[128,384]{1,0:T(8,128)(2,1)} %collective-permute-done.3.refs_1_, ...), custom_call_target="tpu_custom_call" | custom-call | flops 3221225472 | bytes 3145728 | tf_op jit(solution)/shard_map/attend_apart/pallas_call | solution.py:275
  60.7 4.9 %collective-permute-start.10 = (bf16[256,384]{1,0:T(8,128)(2,1)}, bf16[256,384]{1,0:T(8,128)(2,1)}, u32[]{:S(2)}, u32[]{:S(2)}) collective-permute-start(bf16[256,384]{1,0:T(8,128)(2,1)} %get-tuple-element.66), channel_id=1, source_target_pairs={{0,24},{1,25},{2,26},{3,27},{4,28},{5,29},{6,30},{7,31},{8,16},{9,... | collective-permute-start | bytes 589832 | tf_op jit(solution)/shard_map/ppermute | solution.py:400
  65.6 0.6 collective-permute-start.12
  66.3 0.0 all-to-all-done
  66.3 8.1 %attend.1 = bf16[1024,640]{1,0:T(8,128)(2,1)} custom-call(s32[1]{0:T(128)S(6)} %copy.9.blocks, bf16[1024,640]{1,0:T(8,128)(2,1)} %bitcast.4.queries, bf16[1024,1024]{1,0:T(8,128)(2,1)} %bitcast.14, bf16[1024,1024]{1,0:T(8,128)(2,1)} %bitcast.16), custom_call_target="tpu_custom_call" | custom-call | flops 5368709120 | bytes 6291456 | tf_op jit(solution)/shard_map/attend/pallas_call | solution.py:228
  74.4 0.0 collective-permute-done.10.refs_1_
  74.4 8.2 %collective-permute-done.11.refs_2_ = bf16[256,384]{1,0:T(8,128)(2,1)} collective-permute-done((bf16[256,384]{1,0:T(8,128)(2,1)}, bf16[256,384]{1,0:T(8,128)(2,1)}, u32[]{:S(2)}, u32[]{:S(2)}) %collective-permute-start.11) | collective-permute-done | bytes 196640 | tf_op jit(solution)/shard_map/ppermute | solution.py:400
  82.6 0.0 collective-permute-done.12.refs_3_
  82.6 3.4 %all-to-all-start.1 = ((bf16[32,32,640]{2,1,0:T(8,128)(2,1)}), bf16[32,32,640]{2,1,0:T(8,128)(2,1)}, u32[]{:S(2)}, u32[]{:S(2)}) async-start(bf16[32,32,640]{2,1,0:T(8,128)(2,1)} %bitcast.10), calls=%async_computation.1 | async-start | bytes 2621440 | tf_op jit(solution)/shard_map/all_to_all | solution.py:409
  86.0 2.1 %regroup.3 = (bf16[128,384]{1,0:T(8,128)(2,1)}, bf16[128,384]{1,0:T(8,128)(2,1)}, bf16[128,384]{1,0:T(8,128)(2,1)}, bf16[128,384]{1,0:T(8,128)(2,1)}, bf16[128,3...) custom-call(bf16[256,384]{1,0:T(8,128)(2,1)} %get-tuple-element.70.refs_0_, ...), custom_call_target="tpu_custom_call" | custom-call | bytes 1572864 | tf_op jit(solution)/shard_map/regroup/pallas_call | solution.py:191
  88.2 0.0 collective-permute-start.13
  88.2 1.7 %collective-permute-start.14 = (bf16[128,384]{1,0:T(8,128)(2,1)}, bf16[128,384]{1,0:T(8,128)(2,1)}, u32[]{:S(2)}, u32[]{:S(2)}) collective-permute-start(bf16[128,384]{1,0:T(8,128)(2,1)} %get-tuple-element.76), channel_id=1, source_target_pairs={{0,2},{1,3},{2,0},{3,1},{4,6},{5,7},{6,4},{7,5},{8,10},{9,11},{10,... | collective-permute-start | bytes 294920 | tf_op jit(solution)/shard_map/ppermute | solution.py:400
  89.9 0.1 collective-permute-start.15
  90.0 1.6 %collective-permute-start.16 = (bf16[128,384]{1,0:T(8,128)(2,1)}, bf16[128,384]{1,0:T(8,128)(2,1)}, u32[]{:S(2)}, u32[]{:S(2)}) collective-permute-start(bf16[128,384]{1,0:T(8,128)(2,1)} %get-tuple-element.78), channel_id=1, source_target_pairs={{0,4},{1,5},{2,6},{3,7},{4,0},{5,1},{6,2},{7,3},{8,12},{9,13},{10,... | collective-permute-start | bytes 294920 | tf_op jit(solution)/shard_map/ppermute | solution.py:400
  91.6 0.1 collective-permute-start.17
  91.7 0.0 collective-permute-done.13.refs_1_
  91.7 2.6 %collective-permute-start.18 = (bf16[128,384]{1,0:T(8,128)(2,1)}, bf16[128,384]{1,0:T(8,128)(2,1)}, u32[]{:S(2)}, u32[]{:S(2)}) collective-permute-start(bf16[128,384]{1,0:T(8,128)(2,1)} %get-tuple-element.80), channel_id=1, source_target_pairs={{0,6},{1,7},{2,4},{3,5},{4,2},{5,3},{6,0},{7,1},{8,14},{9,15},{10,... | collective-permute-start | bytes 294920 | tf_op jit(solution)/shard_map/ppermute | solution.py:400
  94.3 5.8 %collective-permute-done.14.refs_2_ = bf16[128,384]{1,0:T(8,128)(2,1)} collective-permute-done((bf16[128,384]{1,0:T(8,128)(2,1)}, bf16[128,384]{1,0:T(8,128)(2,1)}, u32[]{:S(2)}, u32[]{:S(2)}) %collective-permute-start.14) | collective-permute-done | bytes 98336 | tf_op jit(solution)/shard_map/ppermute | solution.py:400
  100.1 0.0 collective-permute-start.19
  100.1 3.3 %collective-permute-done.15.refs_3_ = bf16[128,384]{1,0:T(8,128)(2,1)} collective-permute-done((bf16[128,384]{1,0:T(8,128)(2,1)}, bf16[128,384]{1,0:T(8,128)(2,1)}, u32[]{:S(2)}, u32[]{:S(2)}) %collective-permute-start.15) | collective-permute-done | bytes 98336 | tf_op jit(solution)/shard_map/ppermute | solution.py:400
  103.4 0.0 collective-permute-done.17.refs_5_
  103.4 5.3 %collective-permute-done.18.refs_6_ = bf16[128,384]{1,0:T(8,128)(2,1)} collective-permute-done((bf16[128,384]{1,0:T(8,128)(2,1)}, bf16[128,384]{1,0:T(8,128)(2,1)}, u32[]{:S(2)}, u32[]{:S(2)}) %collective-permute-start.18) | collective-permute-done | bytes 98336 | tf_op jit(solution)/shard_map/ppermute | solution.py:400
  108.7 1.2 collective-permute-done.19.refs_7_
  109.9 3.0 %collect.1.refs_2_ = bf16[512,384]{1,0:T(8,128)(2,1)} custom-call(s32[2,512]{1,0:T(2,128)} %get-tuple-element.44.slots.refs_0_, bf16[128,384]{1,0:T(8,128)(2,1)} %get-tuple-element.74.refs_0_, bf16[128,384]{1,0:T(8,128)(2,1)} %collective-permute-done.13.refs_1_, bf16[128,384]{1,0:T(8,128)(2,1)} %collective-permute-done.14.refs_2_, ...), custom_call_target="tpu_custom_call" | custom-call | flops 402653184 | bytes 2097152 | tf_op jit(solution)/shard_map/collect/pallas_call | solution.py:308
  112.9 5.0 %all-to-all-done.1 = bf16[32,32,640]{2,1,0:T(8,128)(2,1)} async-done(((bf16[32,32,640]{2,1,0:T(8,128)(2,1)}), bf16[32,32,640]{2,1,0:T(8,128)(2,1)}, u32[]{:S(2)}, u32[]{:S(2)}) %all-to-all-start.1) | async-done | bytes 1310752 | tf_op jit(solution)/shard_map/all_to_all | solution.py:409
  117.9 5.0 %finish.1 = bf16[512,1024]{1,0:T(8,128)(2,1)} custom-call(s32[2,512]{1,0:T(2,128)} %get-tuple-element.44.slots.refs_0_, bf16[1024,640]{1,0:T(8,128)(2,1)} %bitcast.8.refs_1_, bf16[512,384]{1,0:T(8,128)(2,1)} %collect.1.refs_2_, bf16[512,1024]{1,0:T(8,128)(2,1)} %gates.1.refs_3_, bf16[512,1024]{1,0:T(8,128)(2,1)} %refs_4_.1, bf16[1024,1024]{1,0:T(8,128)(2,1)} %refs_5_.1), custom_call_target="tpu_custom_call" | custom-call | flops 2147483648 | bytes 7340032 | tf_op jit(solution)/shard_map/finish/pallas_call | solution.py:348
  (5 shorter events, 0.0 us)
Async XLA Ops:
  4.0 16.5 %collective-permute-start = (bf16[256,384]{1,0:T(8,128)(2,1)}, bf16[256,384]{1,0:T(8,128)(2,1)}, u32[]{:S(2)}, u32[]{:S(2)}) collective-permute-start(bf16[256,384]{1,0:T(8,128)(2,1)} %get-tuple-element.46), channel_id=1, source_target_pairs={{0,24},{1,25},{2,26},{3,27},{4,28},{5,29},{6,30},{7,31},{8,16},{9,... | collective-permute-start | bytes 589832 | tf_op jit(solution)/shard_map/ppermute | solution.py:400
  9.1 17.0 %collective-permute-start.1 = (bf16[256,384]{1,0:T(8,128)(2,1)}, bf16[256,384]{1,0:T(8,128)(2,1)}, u32[]{:S(2)}, u32[]{:S(2)}) collective-permute-start(bf16[256,384]{1,0:T(8,128)(2,1)} %get-tuple-element.47), channel_id=1, source_target_pairs={{0,16},{1,17},{2,18},{3,19},{4,20},{5,21},{6,22},{7,23},{8,24},{9,... | collective-permute-start | bytes 589832 | tf_op jit(solution)/shard_map/ppermute | solution.py:400
  9.1 17.0 %collective-permute-start.2 = (bf16[256,384]{1,0:T(8,128)(2,1)}, bf16[256,384]{1,0:T(8,128)(2,1)}, u32[]{:S(2)}, u32[]{:S(2)}) collective-permute-start(bf16[256,384]{1,0:T(8,128)(2,1)} %get-tuple-element.48), channel_id=1, source_target_pairs={{0,8},{1,9},{2,10},{3,11},{4,12},{5,13},{6,14},{7,15},{8,0},{9,1},... | collective-permute-start | bytes 589832 | tf_op jit(solution)/shard_map/ppermute | solution.py:400
  26.1 40.2 %all-to-all-start = ((bf16[32,32,640]{2,1,0:T(8,128)(2,1)}), bf16[32,32,640]{2,1,0:T(8,128)(2,1)}, u32[]{:S(2)}, u32[]{:S(2)}) async-start(bf16[32,32,640]{2,1,0:T(8,128)(2,1)} %bitcast.9), calls=%async_computation | async-start | bytes 2621440 | tf_op jit(solution)/shard_map/all_to_all | solution.py:409
  33.3 3.6 %collective-permute-start.3 = (bf16[128,384]{1,0:T(8,128)(2,1)}, bf16[128,384]{1,0:T(8,128)(2,1)}, u32[]{:S(2)}, u32[]{:S(2)}) collective-permute-start(bf16[128,384]{1,0:T(8,128)(2,1)} %get-tuple-element.56), channel_id=1, source_target_pairs={{0,1},{1,0},{2,3},{3,2},{4,5},{5,4},{6,7},{7,6},{8,9},{9,8},{10,11... | collective-permute-start | bytes 294920 | tf_op jit(solution)/shard_map/ppermute | solution.py:400
  33.3 12.0 %collective-permute-start.4 = (bf16[128,384]{1,0:T(8,128)(2,1)}, bf16[128,384]{1,0:T(8,128)(2,1)}, u32[]{:S(2)}, u32[]{:S(2)}) collective-permute-start(bf16[128,384]{1,0:T(8,128)(2,1)} %get-tuple-element.57), channel_id=1, source_target_pairs={{0,2},{1,3},{2,0},{3,1},{4,6},{5,7},{6,4},{7,5},{8,10},{9,11},{10,... | collective-permute-start | bytes 294920 | tf_op jit(solution)/shard_map/ppermute | solution.py:400
  35.0 13.5 %collective-permute-start.5 = (bf16[128,384]{1,0:T(8,128)(2,1)}, bf16[128,384]{1,0:T(8,128)(2,1)}, u32[]{:S(2)}, u32[]{:S(2)}) collective-permute-start(bf16[128,384]{1,0:T(8,128)(2,1)} %get-tuple-element.58), channel_id=1, source_target_pairs={{0,3},{1,2},{2,1},{3,0},{4,7},{5,6},{6,5},{7,4},{8,11},{9,10},{10,... | collective-permute-start | bytes 294920 | tf_op jit(solution)/shard_map/ppermute | solution.py:400
  35.1 13.4 %collective-permute-start.6 = (bf16[128,384]{1,0:T(8,128)(2,1)}, bf16[128,384]{1,0:T(8,128)(2,1)}, u32[]{:S(2)}, u32[]{:S(2)}) collective-permute-start(bf16[128,384]{1,0:T(8,128)(2,1)} %get-tuple-element.59), channel_id=1, source_target_pairs={{0,4},{1,5},{2,6},{3,7},{4,0},{5,1},{6,2},{7,3},{8,12},{9,13},{10,... | collective-permute-start | bytes 294920 | tf_op jit(solution)/shard_map/ppermute | solution.py:400
  36.7 11.8 %collective-permute-start.7 = (bf16[128,384]{1,0:T(8,128)(2,1)}, bf16[128,384]{1,0:T(8,128)(2,1)}, u32[]{:S(2)}, u32[]{:S(2)}) collective-permute-start(bf16[128,384]{1,0:T(8,128)(2,1)} %get-tuple-element.60), channel_id=1, source_target_pairs={{0,5},{1,4},{2,7},{3,6},{4,1},{5,0},{6,3},{7,2},{8,13},{9,12},{10,... | collective-permute-start | bytes 294920 | tf_op jit(solution)/shard_map/ppermute | solution.py:400
  36.8 16.9 %collective-permute-start.8 = (bf16[128,384]{1,0:T(8,128)(2,1)}, bf16[128,384]{1,0:T(8,128)(2,1)}, u32[]{:S(2)}, u32[]{:S(2)}) collective-permute-start(bf16[128,384]{1,0:T(8,128)(2,1)} %get-tuple-element.61), channel_id=1, source_target_pairs={{0,6},{1,7},{2,4},{3,5},{4,2},{5,3},{6,0},{7,1},{8,14},{9,15},{10,... | collective-permute-start | bytes 294920 | tf_op jit(solution)/shard_map/ppermute | solution.py:400
  45.3 9.6 %collective-permute-start.9 = (bf16[128,384]{1,0:T(8,128)(2,1)}, bf16[128,384]{1,0:T(8,128)(2,1)}, u32[]{:S(2)}, u32[]{:S(2)}) collective-permute-start(bf16[128,384]{1,0:T(8,128)(2,1)} %get-tuple-element.62), channel_id=1, source_target_pairs={{0,7},{1,6},{2,5},{3,4},{4,3},{5,2},{6,1},{7,0},{8,15},{9,14},{10,... | collective-permute-start | bytes 294920 | tf_op jit(solution)/shard_map/ppermute | solution.py:400
  60.7 13.7 %collective-permute-start.10 = (bf16[256,384]{1,0:T(8,128)(2,1)}, bf16[256,384]{1,0:T(8,128)(2,1)}, u32[]{:S(2)}, u32[]{:S(2)}) collective-permute-start(bf16[256,384]{1,0:T(8,128)(2,1)} %get-tuple-element.66), channel_id=1, source_target_pairs={{0,24},{1,25},{2,26},{3,27},{4,28},{5,29},{6,30},{7,31},{8,16},{9,... | collective-permute-start | bytes 589832 | tf_op jit(solution)/shard_map/ppermute | solution.py:400
  65.6 17.0 %collective-permute-start.11 = (bf16[256,384]{1,0:T(8,128)(2,1)}, bf16[256,384]{1,0:T(8,128)(2,1)}, u32[]{:S(2)}, u32[]{:S(2)}) collective-permute-start(bf16[256,384]{1,0:T(8,128)(2,1)} %get-tuple-element.67), channel_id=1, source_target_pairs={{0,16},{1,17},{2,18},{3,19},{4,20},{5,21},{6,22},{7,23},{8,24},{9,... | collective-permute-start | bytes 589832 | tf_op jit(solution)/shard_map/ppermute | solution.py:400
  65.6 17.0 %collective-permute-start.12 = (bf16[256,384]{1,0:T(8,128)(2,1)}, bf16[256,384]{1,0:T(8,128)(2,1)}, u32[]{:S(2)}, u32[]{:S(2)}) collective-permute-start(bf16[256,384]{1,0:T(8,128)(2,1)} %get-tuple-element.68), channel_id=1, source_target_pairs={{0,8},{1,9},{2,10},{3,11},{4,12},{5,13},{6,14},{7,15},{8,0},{9,1},... | collective-permute-start | bytes 589832 | tf_op jit(solution)/shard_map/ppermute | solution.py:400
  82.6 35.3 %all-to-all-start.1 = ((bf16[32,32,640]{2,1,0:T(8,128)(2,1)}), bf16[32,32,640]{2,1,0:T(8,128)(2,1)}, u32[]{:S(2)}, u32[]{:S(2)}) async-start(bf16[32,32,640]{2,1,0:T(8,128)(2,1)} %bitcast.10), calls=%async_computation.1 | async-start | bytes 2621440 | tf_op jit(solution)/shard_map/all_to_all | solution.py:409
  88.2 3.6 %collective-permute-start.13 = (bf16[128,384]{1,0:T(8,128)(2,1)}, bf16[128,384]{1,0:T(8,128)(2,1)}, u32[]{:S(2)}, u32[]{:S(2)}) collective-permute-start(bf16[128,384]{1,0:T(8,128)(2,1)} %get-tuple-element.75), channel_id=1, source_target_pairs={{0,1},{1,0},{2,3},{3,2},{4,5},{5,4},{6,7},{7,6},{8,9},{9,8},{10,11... | collective-permute-start | bytes 294920 | tf_op jit(solution)/shard_map/ppermute | solution.py:400
  88.2 11.9 %collective-permute-start.14 = (bf16[128,384]{1,0:T(8,128)(2,1)}, bf16[128,384]{1,0:T(8,128)(2,1)}, u32[]{:S(2)}, u32[]{:S(2)}) collective-permute-start(bf16[128,384]{1,0:T(8,128)(2,1)} %get-tuple-element.76), channel_id=1, source_target_pairs={{0,2},{1,3},{2,0},{3,1},{4,6},{5,7},{6,4},{7,5},{8,10},{9,11},{10,... | collective-permute-start | bytes 294920 | tf_op jit(solution)/shard_map/ppermute | solution.py:400
  89.9 13.5 %collective-permute-start.15 = (bf16[128,384]{1,0:T(8,128)(2,1)}, bf16[128,384]{1,0:T(8,128)(2,1)}, u32[]{:S(2)}, u32[]{:S(2)}) collective-permute-start(bf16[128,384]{1,0:T(8,128)(2,1)} %get-tuple-element.77), channel_id=1, source_target_pairs={{0,3},{1,2},{2,1},{3,0},{4,7},{5,6},{6,5},{7,4},{8,11},{9,10},{10,... | collective-permute-start | bytes 294920 | tf_op jit(solution)/shard_map/ppermute | solution.py:400
  90.0 13.3 %collective-permute-start.16 = (bf16[128,384]{1,0:T(8,128)(2,1)}, bf16[128,384]{1,0:T(8,128)(2,1)}, u32[]{:S(2)}, u32[]{:S(2)}) collective-permute-start(bf16[128,384]{1,0:T(8,128)(2,1)} %get-tuple-element.78), channel_id=1, source_target_pairs={{0,4},{1,5},{2,6},{3,7},{4,0},{5,1},{6,2},{7,3},{8,12},{9,13},{10,... | collective-permute-start | bytes 294920 | tf_op jit(solution)/shard_map/ppermute | solution.py:400
  91.6 11.7 %collective-permute-start.17 = (bf16[128,384]{1,0:T(8,128)(2,1)}, bf16[128,384]{1,0:T(8,128)(2,1)}, u32[]{:S(2)}, u32[]{:S(2)}) collective-permute-start(bf16[128,384]{1,0:T(8,128)(2,1)} %get-tuple-element.79), channel_id=1, source_target_pairs={{0,5},{1,4},{2,7},{3,6},{4,1},{5,0},{6,3},{7,2},{8,13},{9,12},{10,... | collective-permute-start | bytes 294920 | tf_op jit(solution)/shard_map/ppermute | solution.py:400
  91.7 16.9 %collective-permute-start.18 = (bf16[128,384]{1,0:T(8,128)(2,1)}, bf16[128,384]{1,0:T(8,128)(2,1)}, u32[]{:S(2)}, u32[]{:S(2)}) collective-permute-start(bf16[128,384]{1,0:T(8,128)(2,1)} %get-tuple-element.80), channel_id=1, source_target_pairs={{0,6},{1,7},{2,4},{3,5},{4,2},{5,3},{6,0},{7,1},{8,14},{9,15},{10,... | collective-permute-start | bytes 294920 | tf_op jit(solution)/shard_map/ppermute | solution.py:400
  100.1 9.8 %collective-permute-start.19 = (bf16[128,384]{1,0:T(8,128)(2,1)}, bf16[128,384]{1,0:T(8,128)(2,1)}, u32[]{:S(2)}, u32[]{:S(2)}) collective-permute-start(bf16[128,384]{1,0:T(8,128)(2,1)} %get-tuple-element.81), channel_id=1, source_target_pairs={{0,7},{1,6},{2,5},{3,4},{4,3},{5,2},{6,1},{7,0},{8,15},{9,14},{10,... | collective-permute-start | bytes 294920 | tf_op jit(solution)/shard_map/ppermute | solution.py:400

commit v5 on v4

--- a/solution.py
+++ b/solution.py
@@ -176,21 +176,38 @@
     )(items, slots, w_in)
 
 
-def regroup_kernel(count, *refs):
-    arrays, outs = refs[:count], refs[count:]
-    size = arrays[0].shape[0] // len(outs)
-    for first, array in enumerate(arrays):
-        for second, out in enumerate(outs):
-            out[first * size : (first + 1) * size, :] = array[second * size : (second + 1) * size, :]
+def regroup_kernel(count, parts, *refs):
+    arrays, outs, (held, staged, arrivals, departures) = refs[:count], refs[count : count + parts], refs[count + parts :]
+    size = held.shape[1] // parts
+    copies = started([(array, held.at[index]) for index, array in enumerate(arrays)], arrivals)
+    for copy in copies:
+        copy.wait()
+    leaving = []
+    for second in range(parts):
+        for first in range(count):
+            staged[second, first * size : (first + 1) * size, :] = held[first, second * size : (second + 1) * size, :]
+        leaving.append(pltpu.make_async_copy(staged.at[second], outs[second], departures.at[second]))
+        leaving[-1].start()
+    for copy in leaving:
+        copy.wait()
 
 
 def regroup(arrays, parts):
     count = len(arrays)
     rows, width = arrays[0].shape
     size = count * rows // parts
-    return pl.pallas_call(
-        functools.partial(regroup_kernel, count),
+    anywhere = pl.BlockSpec(memory_space=pl.ANY)
+    return pl.pallas_call(
+        functools.partial(regroup_kernel, count, parts),
+        in_specs=[anywhere] * count,
+        out_specs=[anywhere] * parts,
         out_shape=[jax.ShapeDtypeStruct((size, width), BF16)] * parts,
+        scratch_shapes=[
+            pltpu.VMEM((count, rows, width), BF16),
+            pltpu.VMEM((parts, size, width), BF16),
+            pltpu.SemaphoreType.DMA((count,)),
+            pltpu.SemaphoreType.DMA((parts,)),
+        ],
         compiler_params=params(),
         cost_estimate=cost(0, 4 * count * rows * width),
         name="regroup",

time: 124 us -> 124 us (level)
    all_to_all x2, starting transfers between devices: 8.42 us -> 9.66 us  [exchange(): lax.all_to_all(blocks, 'dev', split_axis=0, concat_axis=0, tiled=True)]
where the time goes in v5:
time: 124 us; the launch traced here: 123 us
  waiting for transfers between devices  48.6 us (39%)
  Pallas kernels  41.1 us (33%)
  starting transfers between devices  32.4 us (26%)
    ppermute x20, waiting for transfers between devices, swap(): lax.ppermute(array, 'dev', [(d, d ^ offset) for d in range(devices)])  43.3 us
    ppermute x20, starting transfers between devices, swap(): lax.ppermute(array, 'dev', [(d, d ^ offset) for d in range(devices)])  22.7 us
    all_to_all x2, starting transfers between devices, exchange(): lax.all_to_all(blocks, 'dev', split_axis=0, concat_axis=0, tiled=True)  9.66 us
    pallas_call x1, Pallas kernels, attend(): pl.pallas_call(attend_kernel, grid_spec=pltpu.PrefetchScalarGridSpec(num_...  8.15 us
    pallas_call x1, Pallas kernels, attend_apart(): pl.pallas_call(functools.partial(attend_apart_kernel, members), grid_spec...  5.8 us
    pallas_call x1, Pallas kernels, rest(): pl.pallas_call(rest_kernel, in_specs=[inside, inside, pl.BlockSpec(memory...  5.58 us
    all_to_all x2, waiting for transfers between devices, exchange(): lax.all_to_all(blocks, 'dev', split_axis=0, concat_axis=0, tiled=True)  5.26 us
    pallas_call x1, Pallas kernels, gates(): pl.pallas_call(gate_kernel, in_specs=[inside, pl.BlockSpec(memory_space=p...  5.13 us
  transfers between devices with their start and end apart: 22, of which 11 were waited for; matrix products, arithmetic and copies ran while one was open for 0% of the time, Pallas kernels for 26%

profile of v5, /device:TPU:0, one launch (start us, length us, event | category | flops | bytes accessed | tf_op | source)
XLA Modules:
  0.0 123.0 jit_solution(7403399069253091843)
XLA Ops:
  0.0 4.0 %prepare.1 = (bf16[256,384]{1,0:T(8,128)(2,1)}, bf16[256,384]{1,0:T(8,128)(2,1)}, bf16[256,384]{1,0:T(8,128)(2,1)}, bf16[256,384]{1,0:T(8,128)(2,1)}, s32[2,512]{1,0:T(2,128)}) custom-call(s32[1]{0:T(128)} %bitcast.place, bf16[512,1024]{1,0:T(8,128)(2,1)} %refs_4_.1, s32[1,512]{1,0:T(1,128)} %bitcast.11, s32[1,32]{1,0:T(1,128)} %bitcast.12, ...), custom_call_target="tpu_custom_call" | custom-call | flops 805306368 | bytes 4194304 | tf_op jit(solution)/shard_map/prepare/pallas_call | solution.py:126
  4.0 5.1 %collective-permute-start = (bf16[256,384]{1,0:T(8,128)(2,1)}, bf16[256,384]{1,0:T(8,128)(2,1)}, u32[]{:S(2)}, u32[]{:S(2)}) collective-permute-start(bf16[256,384]{1,0:T(8,128)(2,1)} %get-tuple-element.46), channel_id=1, source_target_pairs={{0,24},{1,25},{2,26},{3,27},{4,28},{5,29},{6,30},{7,31},{8,16},{9,... | collective-permute-start | bytes 589832 | tf_op jit(solution)/shard_map/ppermute | solution.py:417
  9.1 0.0 collective-permute-start.1
  9.1 0.6 collective-permute-start.2
  9.7 5.1 %gates.1.refs_3_ = bf16[512,1024]{1,0:T(8,128)(2,1)} custom-call(bf16[512,1024]{1,0:T(8,128)(2,1)} %refs_4_.1, bf16[1024,2048]{1,0:T(8,128)(2,1)} %w_in.5), custom_call_target="tpu_custom_call" | custom-call | flops 1073741824 | bytes 4194304 | tf_op jit(solution)/shard_map/gates/pallas_call | solution.py:394
  14.9 5.6 %rest.1 = bf16[1024,640]{1,0:T(8,128)(2,1)} custom-call(bf16[512,1024]{1,0:T(8,128)(2,1)} %refs_4_.1, s32[2,512]{1,0:T(2,128)} %get-tuple-element.44.slots.refs_0_, bf16[1024,2048]{1,0:T(8,128)(2,1)} %w_in.5), custom_call_target="tpu_custom_call" | custom-call | flops 1342177280 | bytes 7340032 | tf_op jit(solution)/shard_map/rest/pallas_call | solution.py:167
  20.5 5.6 %collective-permute-done.1.refs_2_ = bf16[256,384]{1,0:T(8,128)(2,1)} collective-permute-done((bf16[256,384]{1,0:T(8,128)(2,1)}, bf16[256,384]{1,0:T(8,128)(2,1)}, u32[]{:S(2)}, u32[]{:S(2)}) %collective-permute-start.1) | collective-permute-done | bytes 196640 | tf_op jit(solution)/shard_map/ppermute | solution.py:417
  26.1 0.0 collective-permute-done.2.refs_3_
  26.1 5.0 %all-to-all-start = ((bf16[32,32,640]{2,1,0:T(8,128)(2,1)}), bf16[32,32,640]{2,1,0:T(8,128)(2,1)}, u32[]{:S(2)}, u32[]{:S(2)}) async-start(bf16[32,32,640]{2,1,0:T(8,128)(2,1)} %bitcast.9), calls=%async_computation | async-start | bytes 2621440 | tf_op jit(solution)/shard_map/all_to_all | solution.py:426
  31.1 2.2 %regroup.2 = (bf16[128,384]{1,0:T(8,128)(2,1)}, bf16[128,384]{1,0:T(8,128)(2,1)}, bf16[128,384]{1,0:T(8,128)(2,1)}, bf16[128,384]{1,0:T(8,128)(2,1)}, bf16[128,3...) custom-call(bf16[256,384]{1,0:T(8,128)(2,1)} %get-tuple-element.51.refs_0_, ...), custom_call_target="tpu_custom_call" | custom-call | bytes 1572864 | tf_op jit(solution)/shard_map/regroup/pallas_call | solution.py:200
  33.4 0.1 collective-permute-start.3
  33.5 1.7 %collective-permute-start.4 = (bf16[128,384]{1,0:T(8,128)(2,1)}, bf16[128,384]{1,0:T(8,128)(2,1)}, u32[]{:S(2)}, u32[]{:S(2)}) collective-permute-start(bf16[128,384]{1,0:T(8,128)(2,1)} %get-tuple-element.57), channel_id=1, source_target_pairs={{0,2},{1,3},{2,0},{3,1},{4,6},{5,7},{6,4},{7,5},{8,10},{9,11},{10,... | collective-permute-start | bytes 294920 | tf_op jit(solution)/shard_map/ppermute | solution.py:417
  35.1 0.2 collective-permute-start.5
  35.3 1.5 %collective-permute-start.6 = (bf16[128,384]{1,0:T(8,128)(2,1)}, bf16[128,384]{1,0:T(8,128)(2,1)}, u32[]{:S(2)}, u32[]{:S(2)}) collective-permute-start(bf16[128,384]{1,0:T(8,128)(2,1)} %get-tuple-element.59), channel_id=1, source_target_pairs={{0,4},{1,5},{2,6},{3,7},{4,0},{5,1},{6,2},{7,3},{8,12},{9,13},{10,... | collective-permute-start | bytes 294920 | tf_op jit(solution)/shard_map/ppermute | solution.py:417
  36.8 0.2 collective-permute-start.7
  37.0 2.5 %collective-permute-start.8 = (bf16[128,384]{1,0:T(8,128)(2,1)}, bf16[128,384]{1,0:T(8,128)(2,1)}, u32[]{:S(2)}, u32[]{:S(2)}) collective-permute-start(bf16[128,384]{1,0:T(8,128)(2,1)} %get-tuple-element.61), channel_id=1, source_target_pairs={{0,6},{1,7},{2,4},{3,5},{4,2},{5,3},{6,0},{7,1},{8,14},{9,15},{10,... | collective-permute-start | bytes 294920 | tf_op jit(solution)/shard_map/ppermute | solution.py:417
  39.5 5.7 %collective-permute-done.4.refs_2_ = bf16[128,384]{1,0:T(8,128)(2,1)} collective-permute-done((bf16[128,384]{1,0:T(8,128)(2,1)}, bf16[128,384]{1,0:T(8,128)(2,1)}, u32[]{:S(2)}, u32[]{:S(2)}) %collective-permute-start.4) | collective-permute-done | bytes 98336 | tf_op jit(solution)/shard_map/ppermute | solution.py:417
  45.3 0.0 collective-permute-start.9
  45.9 2.6 %collective-permute-done.5.refs_3_ = bf16[128,384]{1,0:T(8,128)(2,1)} collective-permute-done((bf16[128,384]{1,0:T(8,128)(2,1)}, bf16[128,384]{1,0:T(8,128)(2,1)}, u32[]{:S(2)}, u32[]{:S(2)}) %collective-permute-start.5) | collective-permute-done | bytes 98336 | tf_op jit(solution)/shard_map/ppermute | solution.py:417
  48.5 5.2 %collective-permute-done.8.refs_6_ = bf16[128,384]{1,0:T(8,128)(2,1)} collective-permute-done((bf16[128,384]{1,0:T(8,128)(2,1)}, bf16[128,384]{1,0:T(8,128)(2,1)}, u32[]{:S(2)}, u32[]{:S(2)}) %collective-permute-start.8) | collective-permute-done | bytes 98336 | tf_op jit(solution)/shard_map/ppermute | solution.py:417
  53.7 1.2 collective-permute-done.9.refs_7_
  54.9 5.8 %attend_apart.1 = (bf16[256,384]{1,0:T(8,128)(2,1)}, bf16[256,384]{1,0:T(8,128)(2,1)}, bf16[256,384]{1,0:T(8,128)(2,1)}, bf16[256,384]{1,0:T(8,128)(2,1)}) custom-call(s32[1]{0:T(128)S(6)} %copy.9.blocks, bf16[128,384]{1,0:T(8,128)(2,1)} %get-tuple-element.55.refs_0_, bf16[128,384]{1,0:T(8,128)(2,1)} %collective-permute-done.3.refs_1_, ...), custom_call_target="tpu_custom_call" | custom-call | flops 3221225472 | bytes 3145728 | tf_op jit(solution)/shard_map/attend_apart/pallas_call | solution.py:292
  60.7 3.1 %collective-permute-start.10 = (bf16[256,384]{1,0:T(8,128)(2,1)}, bf16[256,384]{1,0:T(8,128)(2,1)}, u32[]{:S(2)}, u32[]{:S(2)}) collective-permute-start(bf16[256,384]{1,0:T(8,128)(2,1)} %get-tuple-element.66), channel_id=1, source_target_pairs={{0,24},{1,25},{2,26},{3,27},{4,28},{5,29},{6,30},{7,31},{8,16},{9,... | collective-permute-start | bytes 589832 | tf_op jit(solution)/shard_map/ppermute | solution.py:417
  63.8 0.0 collective-permute-start.11
  63.8 1.4 %collective-permute-start.12 = (bf16[256,384]{1,0:T(8,128)(2,1)}, bf16[256,384]{1,0:T(8,128)(2,1)}, u32[]{:S(2)}, u32[]{:S(2)}) collective-permute-start(bf16[256,384]{1,0:T(8,128)(2,1)} %get-tuple-element.68), channel_id=1, source_target_pairs={{0,8},{1,9},{2,10},{3,11},{4,12},{5,13},{6,14},{7,15},{8,0},{9,1},... | collective-permute-start | bytes 589832 | tf_op jit(solution)/shard_map/ppermute | solution.py:417
  65.2 8.1 %attend.1 = bf16[1024,640]{1,0:T(8,128)(2,1)} custom-call(s32[1]{0:T(128)S(6)} %copy.9.blocks, bf16[1024,640]{1,0:T(8,128)(2,1)} %bitcast.4.queries, bf16[1024,1024]{1,0:T(8,128)(2,1)} %bitcast.14, bf16[1024,1024]{1,0:T(8,128)(2,1)} %bitcast.16), custom_call_target="tpu_custom_call" | custom-call | flops 5368709120 | bytes 6291456 | tf_op jit(solution)/shard_map/attend/pallas_call | solution.py:245
  73.3 0.0 collective-permute-done.10.refs_1_
  73.3 7.6 %collective-permute-done.11.refs_2_ = bf16[256,384]{1,0:T(8,128)(2,1)} collective-permute-done((bf16[256,384]{1,0:T(8,128)(2,1)}, bf16[256,384]{1,0:T(8,128)(2,1)}, u32[]{:S(2)}, u32[]{:S(2)}) %collective-permute-start.11) | collective-permute-done | bytes 196640 | tf_op jit(solution)/shard_map/ppermute | solution.py:417
  80.9 0.0 collective-permute-done.12.refs_3_
  80.9 4.6 %all-to-all-start.1 = ((bf16[32,32,640]{2,1,0:T(8,128)(2,1)}), bf16[32,32,640]{2,1,0:T(8,128)(2,1)}, u32[]{:S(2)}, u32[]{:S(2)}) async-start(bf16[32,32,640]{2,1,0:T(8,128)(2,1)} %bitcast.10), calls=%async_computation.1 | async-start | bytes 2621440 | tf_op jit(solution)/shard_map/all_to_all | solution.py:426
  85.6 2.2 %regroup.3 = (bf16[128,384]{1,0:T(8,128)(2,1)}, bf16[128,384]{1,0:T(8,128)(2,1)}, bf16[128,384]{1,0:T(8,128)(2,1)}, bf16[128,384]{1,0:T(8,128)(2,1)}, bf16[128,3...) custom-call(bf16[256,384]{1,0:T(8,128)(2,1)} %get-tuple-element.70.refs_0_, ...), custom_call_target="tpu_custom_call" | custom-call | bytes 1572864 | tf_op jit(solution)/shard_map/regroup/pallas_call | solution.py:200
  87.8 0.3 collective-permute-start.13
  88.1 1.7 %collective-permute-start.14 = (bf16[128,384]{1,0:T(8,128)(2,1)}, bf16[128,384]{1,0:T(8,128)(2,1)}, u32[]{:S(2)}, u32[]{:S(2)}) collective-permute-start(bf16[128,384]{1,0:T(8,128)(2,1)} %get-tuple-element.76), channel_id=1, source_target_pairs={{0,2},{1,3},{2,0},{3,1},{4,6},{5,7},{6,4},{7,5},{8,10},{9,11},{10,... | collective-permute-start | bytes 294920 | tf_op jit(solution)/shard_map/ppermute | solution.py:417
  89.8 0.0 collective-permute-start.15
  89.8 1.7 %collective-permute-start.16 = (bf16[128,384]{1,0:T(8,128)(2,1)}, bf16[128,384]{1,0:T(8,128)(2,1)}, u32[]{:S(2)}, u32[]{:S(2)}) collective-permute-start(bf16[128,384]{1,0:T(8,128)(2,1)} %get-tuple-element.78), channel_id=1, source_target_pairs={{0,4},{1,5},{2,6},{3,7},{4,0},{5,1},{6,2},{7,3},{8,12},{9,13},{10,... | collective-permute-start | bytes 294920 | tf_op jit(solution)/shard_map/ppermute | solution.py:417
  91.5 0.1 collective-permute-start.17
  91.6 0.0 collective-permute-done.13.refs_1_
  91.6 2.6 %collective-permute-start.18 = (bf16[128,384]{1,0:T(8,128)(2,1)}, bf16[128,384]{1,0:T(8,128)(2,1)}, u32[]{:S(2)}, u32[]{:S(2)}) collective-permute-start(bf16[128,384]{1,0:T(8,128)(2,1)} %get-tuple-element.80), channel_id=1, source_target_pairs={{0,6},{1,7},{2,4},{3,5},{4,2},{5,3},{6,0},{7,1},{8,14},{9,15},{10,... | collective-permute-start | bytes 294920 | tf_op jit(solution)/shard_map/ppermute | solution.py:417
  94.2 5.8 %collective-permute-done.14.refs_2_ = bf16[128,384]{1,0:T(8,128)(2,1)} collective-permute-done((bf16[128,384]{1,0:T(8,128)(2,1)}, bf16[128,384]{1,0:T(8,128)(2,1)}, u32[]{:S(2)}, u32[]{:S(2)}) %collective-permute-start.14) | collective-permute-done | bytes 98336 | tf_op jit(solution)/shard_map/ppermute | solution.py:417
  99.9 0.0 collective-permute-start.19
  99.9 3.2 %collective-permute-done.15.refs_3_ = bf16[128,384]{1,0:T(8,128)(2,1)} collective-permute-done((bf16[128,384]{1,0:T(8,128)(2,1)}, bf16[128,384]{1,0:T(8,128)(2,1)}, u32[]{:S(2)}, u32[]{:S(2)}) %collective-permute-start.15) | collective-permute-done | bytes 98336 | tf_op jit(solution)/shard_map/ppermute | solution.py:417
  103.1 0.0 collective-permute-done.16.refs_4_
  103.1 0.0 collective-permute-done.17.refs_5_
  103.1 5.2 %collective-permute-done.18.refs_6_ = bf16[128,384]{1,0:T(8,128)(2,1)} collective-permute-done((bf16[128,384]{1,0:T(8,128)(2,1)}, bf16[128,384]{1,0:T(8,128)(2,1)}, u32[]{:S(2)}, u32[]{:S(2)}) %collective-permute-start.18) | collective-permute-done | bytes 98336 | tf_op jit(solution)/shard_map/ppermute | solution.py:417
  108.3 1.2 collective-permute-done.19.refs_7_
  109.5 3.0 %collect.1.refs_2_ = bf16[512,384]{1,0:T(8,128)(2,1)} custom-call(s32[2,512]{1,0:T(2,128)} %get-tuple-element.44.slots.refs_0_, bf16[128,384]{1,0:T(8,128)(2,1)} %get-tuple-element.74.refs_0_, bf16[128,384]{1,0:T(8,128)(2,1)} %collective-permute-done.13.refs_1_, bf16[128,384]{1,0:T(8,128)(2,1)} %collective-permute-done.14.refs_2_, ...), custom_call_target="tpu_custom_call" | custom-call | flops 402653184 | bytes 2097152 | tf_op jit(solution)/shard_map/collect/pallas_call | solution.py:325
  112.5 5.3 %all-to-all-done.1 = bf16[32,32,640]{2,1,0:T(8,128)(2,1)} async-done(((bf16[32,32,640]{2,1,0:T(8,128)(2,1)}), bf16[32,32,640]{2,1,0:T(8,128)(2,1)}, u32[]{:S(2)}, u32[]{:S(2)}) %all-to-all-start.1) | async-done | bytes 1310752 | tf_op jit(solution)/shard_map/all_to_all | solution.py:426
  117.8 5.0 %finish.1 = bf16[512,1024]{1,0:T(8,128)(2,1)} custom-call(s32[2,512]{1,0:T(2,128)} %get-tuple-element.44.slots.refs_0_, bf16[1024,640]{1,0:T(8,128)(2,1)} %bitcast.8.refs_1_, bf16[512,384]{1,0:T(8,128)(2,1)} %collect.1.refs_2_, bf16[512,1024]{1,0:T(8,128)(2,1)} %gates.1.refs_3_, bf16[512,1024]{1,0:T(8,128)(2,1)} %refs_4_.1, bf16[1024,1024]{1,0:T(8,128)(2,1)} %refs_5_.1), custom_call_target="tpu_custom_call" | custom-call | flops 2147483648 | bytes 7340032 | tf_op jit(solution)/shard_map/finish/pallas_call | solution.py:365
  (5 shorter events, 0.0 us)
Async XLA Ops:
  4.0 16.5 %collective-permute-start = (bf16[256,384]{1,0:T(8,128)(2,1)}, bf16[256,384]{1,0:T(8,128)(2,1)}, u32[]{:S(2)}, u32[]{:S(2)}) collective-permute-start(bf16[256,384]{1,0:T(8,128)(2,1)} %get-tuple-element.46), channel_id=1, source_target_pairs={{0,24},{1,25},{2,26},{3,27},{4,28},{5,29},{6,30},{7,31},{8,16},{9,... | collective-permute-start | bytes 589832 | tf_op jit(solution)/shard_map/ppermute | solution.py:417
  9.1 17.0 %collective-permute-start.1 = (bf16[256,384]{1,0:T(8,128)(2,1)}, bf16[256,384]{1,0:T(8,128)(2,1)}, u32[]{:S(2)}, u32[]{:S(2)}) collective-permute-start(bf16[256,384]{1,0:T(8,128)(2,1)} %get-tuple-element.47), channel_id=1, source_target_pairs={{0,16},{1,17},{2,18},{3,19},{4,20},{5,21},{6,22},{7,23},{8,24},{9,... | collective-permute-start | bytes 589832 | tf_op jit(solution)/shard_map/ppermute | solution.py:417
  9.1 17.0 %collective-permute-start.2 = (bf16[256,384]{1,0:T(8,128)(2,1)}, bf16[256,384]{1,0:T(8,128)(2,1)}, u32[]{:S(2)}, u32[]{:S(2)}) collective-permute-start(bf16[256,384]{1,0:T(8,128)(2,1)} %get-tuple-element.48), channel_id=1, source_target_pairs={{0,8},{1,9},{2,10},{3,11},{4,12},{5,13},{6,14},{7,15},{8,0},{9,1},... | collective-permute-start | bytes 589832 | tf_op jit(solution)/shard_map/ppermute | solution.py:417
  26.1 39.1 %all-to-all-start = ((bf16[32,32,640]{2,1,0:T(8,128)(2,1)}), bf16[32,32,640]{2,1,0:T(8,128)(2,1)}, u32[]{:S(2)}, u32[]{:S(2)}) async-start(bf16[32,32,640]{2,1,0:T(8,128)(2,1)} %bitcast.9), calls=%async_computation | async-start | bytes 2621440 | tf_op jit(solution)/shard_map/all_to_all | solution.py:426
  33.4 3.6 %collective-permute-start.3 = (bf16[128,384]{1,0:T(8,128)(2,1)}, bf16[128,384]{1,0:T(8,128)(2,1)}, u32[]{:S(2)}, u32[]{:S(2)}) collective-permute-start(bf16[128,384]{1,0:T(8,128)(2,1)} %get-tuple-element.56), channel_id=1, source_target_pairs={{0,1},{1,0},{2,3},{3,2},{4,5},{5,4},{6,7},{7,6},{8,9},{9,8},{10,11... | collective-permute-start | bytes 294920 | tf_op jit(solution)/shard_map/ppermute | solution.py:417
  33.5 11.8 %collective-permute-start.4 = (bf16[128,384]{1,0:T(8,128)(2,1)}, bf16[128,384]{1,0:T(8,128)(2,1)}, u32[]{:S(2)}, u32[]{:S(2)}) collective-permute-start(bf16[128,384]{1,0:T(8,128)(2,1)} %get-tuple-element.57), channel_id=1, source_target_pairs={{0,2},{1,3},{2,0},{3,1},{4,6},{5,7},{6,4},{7,5},{8,10},{9,11},{10,... | collective-permute-start | bytes 294920 | tf_op jit(solution)/shard_map/ppermute | solution.py:417
  35.1 13.4 %collective-permute-start.5 = (bf16[128,384]{1,0:T(8,128)(2,1)}, bf16[128,384]{1,0:T(8,128)(2,1)}, u32[]{:S(2)}, u32[]{:S(2)}) collective-permute-start(bf16[128,384]{1,0:T(8,128)(2,1)} %get-tuple-element.58), channel_id=1, source_target_pairs={{0,3},{1,2},{2,1},{3,0},{4,7},{5,6},{6,5},{7,4},{8,11},{9,10},{10,... | collective-permute-start | bytes 294920 | tf_op jit(solution)/shard_map/ppermute | solution.py:417
  35.3 13.2 %collective-permute-start.6 = (bf16[128,384]{1,0:T(8,128)(2,1)}, bf16[128,384]{1,0:T(8,128)(2,1)}, u32[]{:S(2)}, u32[]{:S(2)}) collective-permute-start(bf16[128,384]{1,0:T(8,128)(2,1)} %get-tuple-element.59), channel_id=1, source_target_pairs={{0,4},{1,5},{2,6},{3,7},{4,0},{5,1},{6,2},{7,3},{8,12},{9,13},{10,... | collective-permute-start | bytes 294920 | tf_op jit(solution)/shard_map/ppermute | solution.py:417
  36.8 11.7 %collective-permute-start.7 = (bf16[128,384]{1,0:T(8,128)(2,1)}, bf16[128,384]{1,0:T(8,128)(2,1)}, u32[]{:S(2)}, u32[]{:S(2)}) collective-permute-start(bf16[128,384]{1,0:T(8,128)(2,1)} %get-tuple-element.60), channel_id=1, source_target_pairs={{0,5},{1,4},{2,7},{3,6},{4,1},{5,0},{6,3},{7,2},{8,13},{9,12},{10,... | collective-permute-start | bytes 294920 | tf_op jit(solution)/shard_map/ppermute | solution.py:417
  37.0 16.7 %collective-permute-start.8 = (bf16[128,384]{1,0:T(8,128)(2,1)}, bf16[128,384]{1,0:T(8,128)(2,1)}, u32[]{:S(2)}, u32[]{:S(2)}) collective-permute-start(bf16[128,384]{1,0:T(8,128)(2,1)} %get-tuple-element.61), channel_id=1, source_target_pairs={{0,6},{1,7},{2,4},{3,5},{4,2},{5,3},{6,0},{7,1},{8,14},{9,15},{10,... | collective-permute-start | bytes 294920 | tf_op jit(solution)/shard_map/ppermute | solution.py:417
  45.3 9.6 %collective-permute-start.9 = (bf16[128,384]{1,0:T(8,128)(2,1)}, bf16[128,384]{1,0:T(8,128)(2,1)}, u32[]{:S(2)}, u32[]{:S(2)}) collective-permute-start(bf16[128,384]{1,0:T(8,128)(2,1)} %get-tuple-element.62), channel_id=1, source_target_pairs={{0,7},{1,6},{2,5},{3,4},{4,3},{5,2},{6,1},{7,0},{8,15},{9,14},{10,... | collective-permute-start | bytes 294920 | tf_op jit(solution)/shard_map/ppermute | solution.py:417
  60.7 12.6 %collective-permute-start.10 = (bf16[256,384]{1,0:T(8,128)(2,1)}, bf16[256,384]{1,0:T(8,128)(2,1)}, u32[]{:S(2)}, u32[]{:S(2)}) collective-permute-start(bf16[256,384]{1,0:T(8,128)(2,1)} %get-tuple-element.66), channel_id=1, source_target_pairs={{0,24},{1,25},{2,26},{3,27},{4,28},{5,29},{6,30},{7,31},{8,16},{9,... | collective-permute-start | bytes 589832 | tf_op jit(solution)/shard_map/ppermute | solution.py:417
  63.8 17.2 %collective-permute-start.11 = (bf16[256,384]{1,0:T(8,128)(2,1)}, bf16[256,384]{1,0:T(8,128)(2,1)}, u32[]{:S(2)}, u32[]{:S(2)}) collective-permute-start(bf16[256,384]{1,0:T(8,128)(2,1)} %get-tuple-element.67), channel_id=1, source_target_pairs={{0,16},{1,17},{2,18},{3,19},{4,20},{5,21},{6,22},{7,23},{8,24},{9,... | collective-permute-start | bytes 589832 | tf_op jit(solution)/shard_map/ppermute | solution.py:417
  63.8 17.2 %collective-permute-start.12 = (bf16[256,384]{1,0:T(8,128)(2,1)}, bf16[256,384]{1,0:T(8,128)(2,1)}, u32[]{:S(2)}, u32[]{:S(2)}) collective-permute-start(bf16[256,384]{1,0:T(8,128)(2,1)} %get-tuple-element.68), channel_id=1, source_target_pairs={{0,8},{1,9},{2,10},{3,11},{4,12},{5,13},{6,14},{7,15},{8,0},{9,1},... | collective-permute-start | bytes 589832 | tf_op jit(solution)/shard_map/ppermute | solution.py:417
  80.9 36.9 %all-to-all-start.1 = ((bf16[32,32,640]{2,1,0:T(8,128)(2,1)}), bf16[32,32,640]{2,1,0:T(8,128)(2,1)}, u32[]{:S(2)}, u32[]{:S(2)}) async-start(bf16[32,32,640]{2,1,0:T(8,128)(2,1)} %bitcast.10), calls=%async_computation.1 | async-start | bytes 2621440 | tf_op jit(solution)/shard_map/all_to_all | solution.py:426
  87.8 3.7 %collective-permute-start.13 = (bf16[128,384]{1,0:T(8,128)(2,1)}, bf16[128,384]{1,0:T(8,128)(2,1)}, u32[]{:S(2)}, u32[]{:S(2)}) collective-permute-start(bf16[128,384]{1,0:T(8,128)(2,1)} %get-tuple-element.75), channel_id=1, source_target_pairs={{0,1},{1,0},{2,3},{3,2},{4,5},{5,4},{6,7},{7,6},{8,9},{9,8},{10,11... | collective-permute-start | bytes 294920 | tf_op jit(solution)/shard_map/ppermute | solution.py:417
  88.1 11.8 %collective-permute-start.14 = (bf16[128,384]{1,0:T(8,128)(2,1)}, bf16[128,384]{1,0:T(8,128)(2,1)}, u32[]{:S(2)}, u32[]{:S(2)}) collective-permute-start(bf16[128,384]{1,0:T(8,128)(2,1)} %get-tuple-element.76), channel_id=1, source_target_pairs={{0,2},{1,3},{2,0},{3,1},{4,6},{5,7},{6,4},{7,5},{8,10},{9,11},{10,... | collective-permute-start | bytes 294920 | tf_op jit(solution)/shard_map/ppermute | solution.py:417
  89.8 13.4 %collective-permute-start.15 = (bf16[128,384]{1,0:T(8,128)(2,1)}, bf16[128,384]{1,0:T(8,128)(2,1)}, u32[]{:S(2)}, u32[]{:S(2)}) collective-permute-start(bf16[128,384]{1,0:T(8,128)(2,1)} %get-tuple-element.77), channel_id=1, source_target_pairs={{0,3},{1,2},{2,1},{3,0},{4,7},{5,6},{6,5},{7,4},{8,11},{9,10},{10,... | collective-permute-start | bytes 294920 | tf_op jit(solution)/shard_map/ppermute | solution.py:417
  89.8 13.4 %collective-permute-start.16 = (bf16[128,384]{1,0:T(8,128)(2,1)}, bf16[128,384]{1,0:T(8,128)(2,1)}, u32[]{:S(2)}, u32[]{:S(2)}) collective-permute-start(bf16[128,384]{1,0:T(8,128)(2,1)} %get-tuple-element.78), channel_id=1, source_target_pairs={{0,4},{1,5},{2,6},{3,7},{4,0},{5,1},{6,2},{7,3},{8,12},{9,13},{10,... | collective-permute-start | bytes 294920 | tf_op jit(solution)/shard_map/ppermute | solution.py:417
  91.5 11.7 %collective-permute-start.17 = (bf16[128,384]{1,0:T(8,128)(2,1)}, bf16[128,384]{1,0:T(8,128)(2,1)}, u32[]{:S(2)}, u32[]{:S(2)}) collective-permute-start(bf16[128,384]{1,0:T(8,128)(2,1)} %get-tuple-element.79), channel_id=1, source_target_pairs={{0,5},{1,4},{2,7},{3,6},{4,1},{5,0},{6,3},{7,2},{8,13},{9,12},{10,... | collective-permute-start | bytes 294920 | tf_op jit(solution)/shard_map/ppermute | solution.py:417
  91.6 16.8 %collective-permute-start.18 = (bf16[128,384]{1,0:T(8,128)(2,1)}, bf16[128,384]{1,0:T(8,128)(2,1)}, u32[]{:S(2)}, u32[]{:S(2)}) collective-permute-start(bf16[128,384]{1,0:T(8,128)(2,1)} %get-tuple-element.80), channel_id=1, source_target_pairs={{0,6},{1,7},{2,4},{3,5},{4,2},{5,3},{6,0},{7,1},{8,14},{9,15},{10,... | collective-permute-start | bytes 294920 | tf_op jit(solution)/shard_map/ppermute | solution.py:417
  99.9 9.6 %collective-permute-start.19 = (bf16[128,384]{1,0:T(8,128)(2,1)}, bf16[128,384]{1,0:T(8,128)(2,1)}, u32[]{:S(2)}, u32[]{:S(2)}) collective-permute-start(bf16[128,384]{1,0:T(8,128)(2,1)} %get-tuple-element.81), channel_id=1, source_target_pairs={{0,7},{1,6},{2,5},{3,4},{4,3},{5,2},{6,1},{7,0},{8,15},{9,14},{10,... | collective-permute-start | bytes 294920 | tf_op jit(solution)/shard_map/ppermute | solution.py:417
